TPU v7x, 256 devices: a whole 4x4x8 slice. The times are simulated.
256 devices in a mesh: seq: 128 (over x_lo, y, z, core), ch: 2 (over x_hi).
Axes of the slice: x: 4 (x_hi: 2, x_lo: 2; x = x_hi * 2 + x_lo), y: 4, z: 8, core: 2. Of those that a mesh axis runs over, the one named last changes fastest.
Arguments:
- tokens: bfloat16 [131072, 1536], P('seq', 'ch'), may hold values from -16 to 16
- spectrum: bfloat16 [2, 512, 256, 768], P(None, 'seq', None, 'ch'), may hold values from -4 to 4
- skip: float32 [1536], P('ch'), may hold values from -1 to 1
- gain: float32 [1536], P('ch'), may hold values from 0.1 to 1.9
- mix_in: bfloat16 [4, 384, 384], P('ch'), may hold values from -0.3125 to 0.3125
- w_up: bfloat16 [4, 384, 1536], P('ch'), may hold values from -0.3125 to 0.3125
- w_down: bfloat16 [4, 1536, 384], P('ch'), may hold values from -0.15625 to 0.15625
- mix_out: bfloat16 [4, 384, 384], P('ch'), may hold values from -0.3125 to 0.3125
Outputs:
- layer_out: bfloat16 [131072, 1536], P('seq', 'ch')
All inputs are finite; a program needn't handle non-finite values.
Results may differ from a plain program's by a relative error of at most 0.012.
Values may be sent and summed in bfloat16 or wider, within the bound.
No kernel may reach another device: no remote copies, remote signals or barrier semaphores. Data moves between devices by JAX's collectives and lax.ppermute only.
A program may use at most 128 MiB of HBM per device.

v0:
```python
import functools
import math

import jax
import jax.numpy as jnp
import ml_dtypes
import numpy as np
from jax import lax
from jax.experimental import pallas as pl
from jax.experimental.pallas import tpu as pltpu
from jax.sharding import PartitionSpec as P

D = 1536
NB = 4
PBLK = 256
QBLK = 512
LANES = 128
F32 = jnp.float32
BF16 = jnp.bfloat16
VMEM_LIMIT = 56 * 1024 * 1024


def dft_numpy(length):
    index = np.arange(length, dtype=np.int64)
    angle = (index[:, None] * index[None, :] % length).astype(np.float32)
    angle = angle * np.float32(2.0 * math.pi / length)
    return (
        np.cos(angle).astype(ml_dtypes.bfloat16).astype(np.float32),
        np.sin(angle).astype(ml_dtypes.bfloat16).astype(np.float32),
    )


def make_tables(groups):
    low = QBLK // groups
    order = (np.arange(groups)[None, :] * low + np.arange(low)[:, None]).reshape(-1)
    cos_long, sin_long = dft_numpy(QBLK)
    cos_long, sin_long = cos_long[order][:, order], sin_long[order][:, order]
    cos_short, sin_short = dft_numpy(PBLK)
    forward = np.concatenate([cos_long, -sin_long], axis=0)
    backward = np.concatenate([cos_long, -sin_long], axis=1) * np.float32(1.0 / (PBLK * QBLK))
    second = np.block([[cos_short, -sin_short], [sin_short, cos_short]])
    third = np.block([[cos_short, sin_short], [-sin_short, cos_short]])
    seq_len = PBLK * QBLK
    angle = (order[:, None].astype(np.int64) * np.arange(PBLK)[None, :] % seq_len).astype(np.float32)
    angle = angle * np.float32(2.0 * math.pi / seq_len)
    half = [t.astype(ml_dtypes.bfloat16) for t in (forward, second, third, backward)]
    return half + [np.cos(angle).astype(np.float32), np.sin(angle).astype(np.float32)]


def pair_split():
    table = np.zeros((2 * LANES, 2 * LANES), np.float32)
    for e in range(2):
        for d in range(LANES):
            table[e * LANES + d, 2 * d + e] = 1.0
    return table.astype(ml_dtypes.bfloat16)


def nt_dot(left, right):
    return lax.dot_general(left, right, (((1,), (1,)), ((), ())), preferred_element_type=F32)


def pack_kernel(tokens_ref, spectrum_ref, split_ref, out_ref, wide):
    split = split_ref[...]
    for block in range(8):
        low, half = block // 2, block % 2
        turned = nt_dot(split, tokens_ref[block * LANES : (block + 1) * LANES, :])
        for e in range(2):
            row = e * 8 + half * 4 + low
            wide[pl.ds(row, LANES, stride=32), :] = turned[e * LANES : (e + 1) * LANES]
    lane = lax.broadcasted_iota(jnp.int32, (LANES, LANES), 0)
    eye = (lane == lax.broadcasted_iota(jnp.int32, (LANES, LANES), 1)).astype(F32).astype(BF16)
    for part in range(2):
        for low in range(4):
            turned = nt_dot(eye, spectrum_ref[part, low])
            for half in range(2):
                row = 16 + part * 8 + half * 4 + low
                wide[pl.ds(row, LANES, stride=32), :] = turned[:, half * LANES : (half + 1) * LANES]
    out_ref[...] = wide[...].reshape(LANES, 32, LANES).astype(BF16)


def pack(tokens, spectrum):
    return pl.pallas_call(
        pack_kernel,
        grid=(3,),
        in_specs=[
            pl.BlockSpec((1024, 256), lambda i: (0, i)),
            pl.BlockSpec((2, 4, 256, LANES), lambda i: (0, 0, 0, i)),
            pl.BlockSpec((256, 256), lambda i: (0, 0)),
        ],
        out_specs=pl.BlockSpec((LANES, 32, LANES), lambda i: (0, i, 0)),
        out_shape=jax.ShapeDtypeStruct((LANES, 96, LANES), BF16),
        scratch_shapes=[pltpu.VMEM((LANES * 32, LANES), F32)],
        compiler_params=pltpu.CompilerParams(vmem_limit_bytes=VMEM_LIMIT),
        cost_estimate=pl.CostEstimate(flops=2 * 10**9, bytes_accessed=6 * 2**20, transcendentals=0),
        name="pack",
    )(tokens, spectrum, pair_split())


def conv_kernel(chunks, data_ref, forward_ref, second_ref, third_ref, backward_ref, cos_ref, sin_ref, *rest):
    out_refs, (wide, back), outs = rest[:chunks], rest[chunks : chunks + 2], rest[chunks + 2 :]
    slot = pl.program_id(0)
    rows_each = 48 // chunks
    low_each = 4 // chunks
    wide[...] = data_ref[...].reshape(LANES * 32, LANES).astype(F32)

    def piece(row):
        return wide[pl.ds(row, LANES, stride=32), :]

    def filters(part):
        return jnp.concatenate(
            [
                jnp.concatenate([piece(16 + part * 8 + half * 4 + low) for half in range(2)], axis=1)
                for low in range(4)
            ],
            axis=0,
        )

    filter_real, filter_imag = filters(0), filters(1)
    for e in range(2):
        block = jnp.concatenate(
            [
                jnp.concatenate([piece(e * 8 + half * 4 + low) for half in range(2)], axis=1).astype(BF16)
                for low in range(4)
            ],
            axis=0,
        )
        first = jnp.dot(forward_ref[...], block, preferred_element_type=F32)
        first_real, first_imag = first[:QBLK], first[QBLK:]
        turn_cos, turn_sin = cos_ref[...], sin_ref[...]
        turned = jnp.concatenate(
            [
                (first_real * turn_cos + first_imag * turn_sin).astype(BF16),
                (first_imag * turn_cos - first_real * turn_sin).astype(BF16),
            ],
            axis=1,
        )
        spectral = jnp.dot(turned, second_ref[...], preferred_element_type=F32)
        spectral_real, spectral_imag = spectral[:, :PBLK], spectral[:, PBLK:]
        filtered = jnp.concatenate(
            [
                (spectral_real * filter_real - spectral_imag * filter_imag).astype(BF16),
                (spectral_real * filter_imag + spectral_imag * filter_real).astype(BF16),
            ],
            axis=1,
        )
        third = jnp.dot(filtered, third_ref[...], preferred_element_type=F32)
        back_real, back_imag = third[:, :PBLK], third[:, PBLK:]
        back[:QBLK, :] = (back_real * turn_cos - back_imag * turn_sin).astype(BF16)
        back[QBLK:, :] = (back_real * turn_sin + back_imag * turn_cos).astype(BF16)
        conv = jnp.dot(backward_ref[...], back[...], preferred_element_type=F32)
        for low in range(4):
            for half in range(2):
                row = ((slot * 2 + e) * 2 + half) * low_each + low % low_each
                outs[low // low_each][pl.ds(row, LANES, stride=rows_each), :] = conv[
                    low * LANES : (low + 1) * LANES, half * LANES : (half + 1) * LANES
                ]

    @pl.when(slot == 2)
    def _():
        for q in range(chunks):
            out_refs[q][...] = outs[q][...].astype(BF16)


def convolve(data, tables, chunks):
    rows = LANES * 48 // chunks
    whole = lambda shape: pl.BlockSpec(shape, lambda i: (0,) * len(shape))
    return pl.pallas_call(
        functools.partial(conv_kernel, chunks),
        grid=(3,),
        in_specs=[pl.BlockSpec((LANES, 32, LANES), lambda i: (0, i, 0))] + [whole(t.shape) for t in tables],
        out_specs=[whole((rows, LANES))] * chunks,
        out_shape=[jax.ShapeDtypeStruct((rows, LANES), BF16)] * chunks,
        scratch_shapes=[
            pltpu.VMEM((LANES * 32, LANES), F32),
            pltpu.VMEM((2 * QBLK, PBLK), BF16),
        ]
        + [pltpu.VMEM((rows, LANES), F32)] * chunks,
        compiler_params=pltpu.CompilerParams(vmem_limit_bytes=VMEM_LIMIT),
        cost_estimate=pl.CostEstimate(flops=64 * 10**8, bytes_accessed=8 * 2**20, transcendentals=0),
        name="convolve",
    )(data, *tables)


def hidden_kernel(lows, conv_ref, tokens_ref, skip_ref, split_ref, hidden_ref, stats_ref, wide):
    per_slot = 4 * lows
    wide[...] = conv_ref[...].astype(F32)
    split = split_ref[...]
    lane = lax.broadcasted_iota(jnp.int32, (LANES, LANES), 1)
    for block in range(2 * lows):
        low, half = block // 2, block % 2
        rows = slice(block * LANES, (block + 1) * LANES)
        pieces = []
        for slot in range(3):
            turned = jnp.concatenate(
                [
                    wide[pl.ds(((slot * 2 + e) * 2 + half) * lows + low, LANES, stride=3 * per_slot), :].T
                    for e in range(2)
                ],
                axis=1,
            ).astype(BF16)
            conv = jnp.dot(turned, split, preferred_element_type=F32)
            cols = slice(slot * 256, (slot + 1) * 256)
            values = tokens_ref[rows, cols].astype(F32)
            mixed = conv + skip_ref[:, cols] * values
            pieces.append(values + mixed * jax.nn.sigmoid(values))
        hidden = jnp.concatenate(pieces, axis=1)
        hidden_ref[rows, :] = hidden
        mean = jnp.mean(hidden, axis=1, keepdims=True)
        centered = hidden - mean
        square = jnp.sum(centered * centered, axis=1, keepdims=True)
        both = jnp.where(lane == 0, mean, jnp.where(lane == 1, square, 0.0))
        stats_ref[block] = both.T[:8]


def make_hidden(conv, tokens, skip, chunk, chunks):
    rows = tokens.shape[0] // chunks
    return pl.pallas_call(
        functools.partial(hidden_kernel, 4 // chunks),
        grid=(1,),
        in_specs=[
            pl.BlockSpec(conv.shape, lambda i: (0, 0)),
            pl.BlockSpec((rows, 768), lambda i: (chunk, 0)),
            pl.BlockSpec((1, 768), lambda i: (0, 0)),
            pl.BlockSpec((256, 256), lambda i: (0, 0)),
        ],
        out_specs=[
            pl.BlockSpec((rows, 768), lambda i: (0, 0)),
            pl.BlockSpec((rows // LANES, 8, LANES), lambda i: (0, 0, 0)),
        ],
        out_shape=[
            jax.ShapeDtypeStruct((rows, 768), F32),
            jax.ShapeDtypeStruct((rows // LANES, 8, LANES), F32),
        ],
        scratch_shapes=[pltpu.VMEM(conv.shape, F32)],
        compiler_params=pltpu.CompilerParams(vmem_limit_bytes=VMEM_LIMIT),
        cost_estimate=pl.CostEstimate(flops=4 * 10**8, bytes_accessed=6 * 2**20 // chunks, transcendentals=10**6),
        name="hidden",
    )(conv, tokens, skip, pair_split())


def mix_kernel(hidden_ref, mine_ref, other_ref, gain_ref, weight_ref, own_ref, send_ref):
    width = hidden_ref.shape[1]
    for block in range(hidden_ref.shape[0] // LANES):
        rows = slice(block * LANES, (block + 1) * LANES)
        mine = jnp.concatenate([mine_ref[block]] * 16, axis=0).T
        other = jnp.concatenate([other_ref[block]] * 16, axis=0).T
        mean = 0.5 * (mine[:, 0:1] + other[:, 0:1])
        gap = mine[:, 0:1] - other[:, 0:1]
        square = mine[:, 1:2] + other[:, 1:2] + gap * gap * (0.5 * width)
        scale = lax.rsqrt(square / (2 * width) + 1e-05)
        normed = ((hidden_ref[rows, :] - mean) * scale * gain_ref[...]).astype(BF16)
        mixed = jnp.dot(normed, weight_ref[...], preferred_element_type=F32).astype(BF16)
        own_ref[rows, :] = mixed[:, : width // 2]
        send_ref[rows, :] = mixed[:, width // 2 :]


def first_mix(hidden, mine, other, gain, weight):
    rows, width = hidden.shape
    return pl.pallas_call(
        mix_kernel,
        out_shape=[jax.ShapeDtypeStruct((rows, width // 2), BF16)] * 2,
        compiler_params=pltpu.CompilerParams(vmem_limit_bytes=VMEM_LIMIT),
        cost_estimate=pl.CostEstimate(flops=2 * rows * 768 * 768, bytes_accessed=rows * 768 * 6, transcendentals=0),
        name="first_mix",
    )(hidden, mine, other, gain, weight)


def mlp_kernel(own_ref, rem_ref, up_own_ref, up_rem_ref, down_own_ref, down_send_ref, keep_ref, send_ref):
    rows = min(256, own_ref.shape[0])
    for block in range(own_ref.shape[0] // rows):
        at = slice(block * rows, (block + 1) * rows)
        keep, send = [], []
        for c in range(2):
            window = slice(c * LANES, c * LANES + 256)
            up = jnp.dot(own_ref[at, window], up_own_ref[c], preferred_element_type=F32)
            up = up + jnp.dot(rem_ref[at, window], up_rem_ref[c], preferred_element_type=F32)
            active = jax.nn.gelu(up, approximate=True).astype(BF16)
            keep.append(jnp.dot(active, down_own_ref[c], preferred_element_type=F32))
            send.append(jnp.dot(active, down_send_ref[c], preferred_element_type=F32))
        for parts, ref in ((keep, keep_ref), (send, send_ref)):
            ref[at, 0:128] = parts[0][:, 0:128].astype(BF16)
            ref[at, 128:256] = (parts[0][:, 128:256] + parts[1][:, 0:128]).astype(BF16)
            ref[at, 256:384] = parts[1][:, 128:256].astype(BF16)


def mlp(own, rem, up_own, up_rem, down_own, down_send):
    rows, width = own.shape
    return pl.pallas_call(
        mlp_kernel,
        out_shape=[jax.ShapeDtypeStruct((rows, width), BF16)] * 2,
        compiler_params=pltpu.CompilerParams(vmem_limit_bytes=VMEM_LIMIT),
        cost_estimate=pl.CostEstimate(
            flops=rows * 48 * 10**5, bytes_accessed=6 * 2**20 + rows * 3072, transcendentals=rows * 3072
        ),
        name="mlp",
    )(own, rem, up_own, up_rem, down_own, down_send)


def last_kernel(hidden_ref, keep_ref, rem_ref, weight_ref, out_ref):
    half = keep_ref.shape[1]
    rows = min(256, keep_ref.shape[0])
    for block in range(keep_ref.shape[0] // rows):
        at = slice(block * rows, (block + 1) * rows)
        outcome = jnp.dot(keep_ref[at, :], weight_ref[:half, :], preferred_element_type=F32)
        outcome = outcome + jnp.dot(rem_ref[at, :], weight_ref[half:, :], preferred_element_type=F32)
        out_ref[at, :] = (hidden_ref[at, :] + outcome).astype(BF16)


def last_mix(hidden, keep, rem, weight):
    rows, width = hidden.shape
    return pl.pallas_call(
        last_kernel,
        out_shape=jax.ShapeDtypeStruct((rows, width), BF16),
        compiler_params=pltpu.CompilerParams(vmem_limit_bytes=VMEM_LIMIT),
        cost_estimate=pl.CostEstimate(flops=2 * rows * 768 * 768, bytes_accessed=rows * 768 * 8, transcendentals=0),
        name="last_mix",
    )(hidden, keep, rem, weight)


def prepare_weights(mix_in, w_up, w_down, mix_out, side):
    blocks, inner = mix_in.shape[0], mix_in.shape[1]
    piece = inner // NB
    half = inner // 2
    eye = jnp.eye(blocks, dtype=mix_in.dtype)
    other = 1 - side

    grid = mix_in.reshape(blocks, inner, 2, 2, piece)
    grid = lax.dynamic_slice_in_dim(jnp.concatenate([grid, grid[:, :, :1]], axis=2), side, 2, axis=2)
    weight_in = jnp.einsum("bisce,bx->biscxe", grid, eye).reshape(blocks * inner, 2 * inner)

    grid = mix_out.reshape(blocks, 2, 2, piece, inner)
    grid = lax.dynamic_slice_in_dim(jnp.concatenate([grid, grid[:, :1]], axis=1), side, 2, axis=1)
    weight_out = jnp.einsum("bscej,bx->scbexj", grid, eye).reshape(2 * inner, blocks * inner)

    def rows(which):
        part = lax.dynamic_slice_in_dim(w_up, which * half, half, axis=1)
        first = jnp.pad(part[0], ((0, 256 - half), (0, 0)))
        second = jnp.pad(part[1], ((256 - half, 0), (0, 0)))
        return jnp.stack([first, second])

    def columns(which):
        part = lax.dynamic_slice_in_dim(w_down, which * half, half, axis=2)
        first = jnp.pad(part[0], ((0, 0), (0, 256 - half)))
        second = jnp.pad(part[1], ((0, 0), (256 - half, 0)))
        return jnp.stack([first, second])

    return weight_in, weight_out, rows(side), rows(other), columns(side), columns(other)


def make_per_device(chunks):
    def per_device(tokens, spectrum, skip, gain, mix_in, w_up, w_down, mix_out):
        groups = lax.axis_size("seq")
        side = lax.axis_index("ch")
        swap = [(0, 1), (1, 0)]
        weight_in, weight_out, up_own, up_rem, down_own, down_send = prepare_weights(
            mix_in, w_up, w_down, mix_out, side
        )
        gain = gain[None, :]
        skip = skip[None, :]
        packed = pack(tokens, spectrum)
        data = lax.all_to_all(packed, "seq", split_axis=0, concat_axis=0, tiled=True)
        convs = convolve(data, make_tables(groups), chunks)
        outs = []
        for q in range(chunks):
            conv = lax.all_to_all(convs[q], "seq", split_axis=0, concat_axis=0, tiled=True)
            hidden, mine = make_hidden(conv, tokens, skip, q, chunks)
            other = lax.ppermute(mine, "ch", swap)
            own, send = first_mix(hidden, mine, other, gain, weight_in)
            rem = lax.ppermute(send, "ch", swap)
            keep, send = mlp(own, rem, up_own, up_rem, down_own, down_send)
            rem = lax.ppermute(send, "ch", swap)
            outs.append(last_mix(hidden, keep, rem, weight_out))
        return outs[0] if chunks == 1 else jnp.concatenate(outs, axis=0)

    return per_device


def solution(mesh):
    return jax.shard_map(
        make_per_device(1),
        mesh=mesh,
        in_specs=(
            P("seq", "ch"),
            P(None, "seq", None, "ch"),
            P("ch"),
            P("ch"),
            P("ch", None, None),
            P("ch", None, None),
            P("ch", None, None),
            P("ch", None, None),
        ),
        out_specs=P("seq", "ch"),
        check_vma=False,
    )
```

profile of v0, /device:TPU:8, one launch (start us, length us, event | category | flops | bytes accessed | tf_op | source)
XLA Modules:
  0.0 239.6 jit_solution(17275342735111714188)
XLA Ops:
  0.0 7.6 %pack.1 = bf16[128,96,128]{2,1,0:T(8,128)(2,1)} custom-call(bf16[1024,768]{1,0:T(8,128)(2,1)} %tokens_ref.3, bf16[2,4,256,384]{3,2,1,0:T(8,128)(2,1)} %spectrum_ref.1, bf16[256,256]{1,0:T(8,128)(2,1)} %constant.30.clone.split_ref), custom_call_target="tpu_custom_call" | custom-call | flops 2000000000 | bytes 6291456 | tf_op jit(solution)/shard_map/pack/pallas_call | solution.py:82
  7.6 84.9 %all_to_all.16.data_ref = bf16[128,96,128]{2,1,0:T(8,128)(2,1)} all-to-all(bf16[128,96,128]{2,1,0:T(8,128)(2,1)} %pack.1), channel_id=1, replica_groups=mesh['seq'=128,'ch'=2] {'seq'}, dimensions={0} | all-to-all | bytes 6291456 | tf_op jit(solution)/shard_map/all_to_all | solution.py:361
  92.5 16.2 %convolve.1 = bf16[6144,128]{1,0:T(8,128)(2,1)} custom-call(bf16[128,96,128]{2,1,0:T(8,128)(2,1)} %all_to_all.16.data_ref, bf16[1024,512]{1,0:T(8,128)(2,1)} %constant.31.clone.forward_ref, bf16[512,512]{1,0:T(8,128)(2,1)} %constant.32.clone.second_ref, bf16[512,512]{1,0:T(8,128)(2,1)} %constant.33.clone.third_ref, ...), custom_call_target="tpu_custom_call" | custom-call | flops 6400000000 | bytes 8388608 | tf_op jit(solution)/shard_map/convolve/pallas_call | solution.py:167
  108.7 10.6 %all-to-all-start.1 = ((bf16[128,48,128]{2,1,0:T(8,128)(2,1)}), bf16[128,48,128]{2,1,0:T(8,128)(2,1)S(1)}, u32[]{:S(2)}, u32[]{:S(2)}) async-start(bf16[128,48,128]{2,1,0:T(8,128)(2,1)} %bitcast.53), calls=%async_computation.1 | async-start | bytes 3145728 | tf_op jit(solution)/shard_map/all_to_all | solution.py:365
  119.4 0.6 broadcast_in_dim.6.skip_ref
  120.5 1.5 copy.19
  122.0 1.8 dynamic-slice_bitcast_fusion.5
  123.9 1.3 pad_maximum_fusion.up_own_ref
  125.3 1.3 pad_maximum_fusion.1.up_rem_ref
  126.7 0.9 copy-done.1
  127.6 2.7 %dynamic-slice_bitcast_fusion.1 = (bf16[1536,192]{1,0:T(8,128)(2,1)}, bf16[1536,192]{1,0:T(8,128)(2,1)S(1)}, bf16[1536,192]{1,0:T(8,128)(2,1)}, bf16[1536,192]{1,0:T(8,128)(2,1)S(1)}) fusion(bf16[2,1536,384]{2,1,0:T(8,128)(2,1)S(1)} %copy-done.1, s32[]{:T(128)S(6)} %select_n.14, s32[]{:T(128)S(6)} %select_n.13, s32[]{:T(128)S(6)} %add.31), kind=kLoop, calls=%fused_computation.9 | loop fusion | bytes 4718604 | tf_op jit(solution)/shard_map/squeeze | solution.py:343
  130.7 26.2 %all-to-all-done.1 = bf16[128,48,128]{2,1,0:T(8,128)(2,1)S(1)} async-done(((bf16[128,48,128]{2,1,0:T(8,128)(2,1)}), bf16[128,48,128]{2,1,0:T(8,128)(2,1)S(1)}, u32[]{:S(2)}, u32[]{:S(2)}) %all-to-all-start.1) | async-done | bytes 1572896 | tf_op jit(solution)/shard_map/all_to_all | solution.py:365
  156.9 1.1 copy-done
  158.0 6.3 %hidden.1 = (f32[1024,768]{1,0:T(8,128)}, f32[8,8,128]{2,1,0:T(8,128)}) custom-call(bf16[6144,128]{1,0:T(8,128)(2,1)} %bitcast.46, bf16[1024,768]{1,0:T(8,128)(2,1)} %tokens_ref.3, f32[1,768]{1,0:T(1,128)} %broadcast_in_dim.6.skip_ref, bf16[256,256]{1,0:T(8,128)(2,1)} %constant.30.clone.split_ref), custom_call_target="tpu_custom_call" | custom-call | flops 400000000 | bytes 6291456 | tf_op jit(solution)/shard_map/hidden/pallas_call | solution.py:217
  164.3 2.7 %collective-permute-start = (f32[8,8,128]{2,1,0:T(8,128)}, f32[8,8,128]{2,1,0:T(8,128)S(1)}, u32[]{:S(2)}, u32[]{:S(2)}) collective-permute-start(f32[8,8,128]{2,1,0:T(8,128)} %get-tuple-element.12.mine_ref), channel_id=1, source_target_pairs={{0,1},{1,0},{2,3},{3,2},{4,5},{5,4},{6,7},{7,6},{8,9},{9,8},{10,11... | collective-permute-start | bytes 98312 | tf_op jit(solution)/shard_map/ppermute | solution.py:367
  167.1 1.0 broadcast_multiply_fusion.1
  168.9 1.5 copy.20.weight_ref
  170.3 0.6 copy-done.11
  170.9 5.5 %first_mix.1 = (bf16[1024,384]{1,0:T(8,128)(2,1)}, bf16[1024,384]{1,0:T(8,128)(2,1)}) custom-call(f32[1024,768]{1,0:T(8,128)} %get-tuple-element.11.hidden_ref, f32[8,8,128]{2,1,0:T(8,128)} %get-tuple-element.12.mine_ref, f32[8,8,128]{2,1,0:T(8,128)} %copy-done.11, f32[1,768]{1,0:T(1,128)} %broadcast_in_dim.7.gain_ref, bf16[768,768]{1,0:T(8,128)(2,1)} %copy.20.weight_ref), custom_call_target="tpu_custom_call" | custom-call | flops 1207959552 | bytes 4718592 | tf_op jit(solution)/shard_map/first_mix/pallas_call | solution.py:259
  176.5 2.4 collective-permute-start.1
  178.8 1.3 pad_maximum_fusion.2.down_own_ref
  180.2 0.6 copy-done.3
  181.2 1.3 pad_maximum_fusion.3.down_send_ref
  182.5 15.6 %collective-permute-done.1.rem_ref = bf16[1024,384]{1,0:T(8,128)(2,1)S(1)} collective-permute-done((bf16[1024,384]{1,0:T(8,128)(2,1)}, bf16[1024,384]{1,0:T(8,128)(2,1)S(1)}, u32[]{:S(2)}, u32[]{:S(2)}) %collective-permute-start.1) | collective-permute-done | bytes 786464 | tf_op jit(solution)/shard_map/ppermute | solution.py:369
  198.1 0.9 copy-done.10
  199.0 12.6 %mlp.1 = (bf16[1024,384]{1,0:T(8,128)(2,1)}, bf16[1024,384]{1,0:T(8,128)(2,1)}) custom-call(bf16[1024,384]{1,0:T(8,128)(2,1)} %get-tuple-element.13.own_ref, bf16[1024,384]{1,0:T(8,128)(2,1)} %copy-done.10, bf16[2,256,1536]{2,1,0:T(8,128)(2,1)} %pad_maximum_fusion.up_own_ref, bf16[2,256,1536]{2,1,0:T(8,128)(2,1)} %pad_maximum_fusion.1.up_rem_ref, ...), custom_call_target="tpu_custom_call" | custom-call | flops 4915200000 | bytes 9437184 | tf_op jit(solution)/shard_map/mlp/pallas_call | solution.py:288
  211.6 2.5 %collective-permute-start.2 = (bf16[1024,384]{1,0:T(8,128)(2,1)}, bf16[1024,384]{1,0:T(8,128)(2,1)S(1)}, u32[]{:S(2)}, u32[]{:S(2)}) collective-permute-start(bf16[1024,384]{1,0:T(8,128)(2,1)} %get-tuple-element.16), channel_id=1, source_target_pairs={{0,1},{1,0},{2,3},{3,2},{4,5},{5,4},{6,7},{7,6},{8,9},{9,8},{10,11... | collective-permute-start | bytes 2359304 | tf_op jit(solution)/shard_map/ppermute | solution.py:371
  214.2 1.2 broadcast_multiply_fusion
  215.4 1.2 copy.24
  216.6 16.4 %collective-permute-done.2.rem_ref = bf16[1024,384]{1,0:T(8,128)(2,1)S(1)} collective-permute-done((bf16[1024,384]{1,0:T(8,128)(2,1)}, bf16[1024,384]{1,0:T(8,128)(2,1)S(1)}, u32[]{:S(2)}, u32[]{:S(2)}) %collective-permute-start.2) | collective-permute-done | bytes 786464 | tf_op jit(solution)/shard_map/ppermute | solution.py:371
  233.0 0.9 copy-done.6
  233.9 5.6 %last_mix.1 = bf16[1024,768]{1,0:T(8,128)(2,1)} custom-call(f32[1024,768]{1,0:T(8,128)} %get-tuple-element.11.hidden_ref, bf16[1024,384]{1,0:T(8,128)(2,1)} %get-tuple-element.15.keep_ref, bf16[1024,384]{1,0:T(8,128)(2,1)} %copy-done.6, bf16[768,768]{1,0:T(8,128)(2,1)} %bitcast.47), custom_call_target="tpu_custom_call" | custom-call | flops 1207959552 | bytes 6291456 | tf_op jit(solution)/shard_map/last_mix/pallas_call | solution.py:311
  (31 shorter events, 2.7 us)
Async XLA Ops:
  108.7 10.6 %copy-start.8 = (f32[768]{0:T(1024)S(1)}, f32[768]{0:T(1024)}, u32[]{:S(2)}) copy-start(f32[768]{0:T(1024)} %param.18) | copy-start | bytes 9220
  108.7 11.3 %copy-start.7 = (bf16[2,384,384]{2,1,0:T(8,128)(2,1)S(1)}, bf16[2,384,384]{2,1,0:T(8,128)(2,1)}, u32[]{:S(2)}) copy-start(bf16[2,384,384]{2,1,0:T(8,128)(2,1)} %param.20) | copy-start | bytes 1769476
  108.7 48.2 %all-to-all-start.1 = ((bf16[128,48,128]{2,1,0:T(8,128)(2,1)}), bf16[128,48,128]{2,1,0:T(8,128)(2,1)S(1)}, u32[]{:S(2)}, u32[]{:S(2)}) async-start(bf16[128,48,128]{2,1,0:T(8,128)(2,1)} %bitcast.53), calls=%async_computation.1 | async-start | bytes 3145728 | tf_op jit(solution)/shard_map/all_to_all | solution.py:365
  125.3 2.2 copy-start.1
  156.9 1.1 copy-start
  158.0 9.1 %copy-start.4 = (bf16[2,384,2,2,96]{1,0,4,3,2:T(2,128)(2,1)S(1)}, bf16[2,384,2,2,96]{1,0,4,3,2:T(2,128)(2,1)}, u32[]{:S(2)}) copy-start(bf16[2,384,2,2,96]{1,0,4,3,2:T(2,128)(2,1)} %copy.19) | copy-start | bytes 1769476
  164.3 3.7 %copy-start.9 = (f32[768]{0:T(1024)S(1)}, f32[768]{0:T(1024)}, u32[]{:S(2)}) copy-start(f32[768]{0:T(1024)} %param.19) | copy-start | bytes 9220
  164.3 6.0 %collective-permute-start = (f32[8,8,128]{2,1,0:T(8,128)}, f32[8,8,128]{2,1,0:T(8,128)S(1)}, u32[]{:S(2)}, u32[]{:S(2)}) collective-permute-start(f32[8,8,128]{2,1,0:T(8,128)} %get-tuple-element.12.mine_ref), channel_id=1, source_target_pairs={{0,1},{1,0},{2,3},{3,2},{4,5},{5,4},{6,7},{7,6},{8,9},{9,8},{10,11... | collective-permute-start | bytes 98312 | tf_op jit(solution)/shard_map/ppermute | solution.py:367
  170.3 0.6 copy-start.11
  176.5 21.6 %collective-permute-start.1 = (bf16[1024,384]{1,0:T(8,128)(2,1)}, bf16[1024,384]{1,0:T(8,128)(2,1)S(1)}, u32[]{:S(2)}, u32[]{:S(2)}) collective-permute-start(bf16[1024,384]{1,0:T(8,128)(2,1)} %get-tuple-element.14), channel_id=1, source_target_pairs={{0,1},{1,0},{2,3},{3,2},{4,5},{5,4},{6,7},{7,6},{8,9},{9,8},{10,11... | collective-permute-start | bytes 2359304 | tf_op jit(solution)/shard_map/ppermute | solution.py:369
  178.8 1.3 copy-start.2
  178.8 1.9 copy-start.3
  198.1 0.9 copy-start.10
  199.0 15.2 %copy-start.5 = (bf16[2,384,384]{2,1,0:T(8,128)(2,1)S(1)}, bf16[2,384,384]{2,1,0:T(8,128)(2,1)}, u32[]{:S(2)}) copy-start(bf16[2,384,384]{2,1,0:T(8,128)(2,1)} %param.23) | copy-start | bytes 1769476
  211.6 21.5 %collective-permute-start.2 = (bf16[1024,384]{1,0:T(8,128)(2,1)}, bf16[1024,384]{1,0:T(8,128)(2,1)S(1)}, u32[]{:S(2)}, u32[]{:S(2)}) collective-permute-start(bf16[1024,384]{1,0:T(8,128)(2,1)} %get-tuple-element.16), channel_id=1, source_target_pairs={{0,1},{1,0},{2,3},{3,2},{4,5},{5,4},{6,7},{7,6},{8,9},{9,8},{10,11... | collective-permute-start | bytes 2359304 | tf_op jit(solution)/shard_map/ppermute | solution.py:371
  233.0 0.9 copy-start.6
where the time goes:
time: 241 us; the launch traced here: 240 us
  blocking collectives  84.9 us (35%)
  waiting for transfers between devices  58.2 us (24%)
  Pallas kernels  53.8 us (22%)
  starting transfers between devices  18.3 us (8%)
  local copies, waits for them, and re-layouts  16.7 us (7%)
  other arithmetic  7.54 us (3%)
    all_to_all x1, blocking collectives, per_device(): lax.all_to_all(packed, 'seq', split_axis=0, concat_axis=0, tiled=True)  84.9 us
    ppermute x2, waiting for transfers between devices, per_device(): rem = lax.ppermute(send, 'ch', swap)  32 us
    all_to_all x1, waiting for transfers between devices, per_device(): lax.all_to_all(convs[q], 'seq', split_axis=0, concat_axis=0, tiled=True)  26.2 us
    pallas_call x1, Pallas kernels, convolve(): pl.pallas_call(functools.partial(conv_kernel, chunks), grid=(3,), in_spec...  16.2 us
    pallas_call x1, Pallas kernels, mlp(): pl.pallas_call(mlp_kernel, out_shape=[jax.ShapeDtypeStruct((rows, width),...  12.6 us
    all_to_all x1, starting transfers between devices, per_device(): lax.all_to_all(convs[q], 'seq', split_axis=0, concat_axis=0, tiled=True)  10.6 us
    pallas_call x1, Pallas kernels, pack(): pl.pallas_call(pack_kernel, grid=(3,), in_specs=[pl.BlockSpec((1024, 256)...  7.55 us
    unnamed x27, local copies, waits for them, and re-layouts  6.88 us
  transfers between devices with their start and end apart: 4, of which 3 were waited for; matrix products, arithmetic and copies ran while one was open for 8% of the time, Pallas kernels for 0%

commit v1 on v0

v1 whole, which is shorter than its diff:
```python
import functools
import math

import jax
import jax.numpy as jnp
import ml_dtypes
import numpy as np
from jax import lax
from jax.experimental import pallas as pl
from jax.experimental.pallas import tpu as pltpu
from jax.sharding import PartitionSpec as P

D = 1536
NB = 4
PBLK = 256
QBLK = 512
LANES = 128
F32 = jnp.float32
BF16 = jnp.bfloat16
VMEM_LIMIT = 56 * 1024 * 1024
SMALL_LIMIT = 32 * 1024 * 1024


def dft_numpy(length):
    index = np.arange(length, dtype=np.int64)
    angle = (index[:, None] * index[None, :] % length).astype(np.float32)
    angle = angle * np.float32(2.0 * math.pi / length)
    return (
        np.cos(angle).astype(ml_dtypes.bfloat16).astype(np.float32),
        np.sin(angle).astype(ml_dtypes.bfloat16).astype(np.float32),
    )


def make_tables(groups):
    low = QBLK // groups
    order = (np.arange(groups)[None, :] * low + np.arange(low)[:, None]).reshape(-1)
    cos_long, sin_long = dft_numpy(QBLK)
    cos_long, sin_long = cos_long[order][:, order], sin_long[order][:, order]
    cos_short, sin_short = dft_numpy(PBLK)
    forward = np.concatenate([cos_long, -sin_long], axis=0)
    backward = np.concatenate([cos_long, -sin_long], axis=1) * np.float32(1.0 / (PBLK * QBLK))
    second = np.block([[cos_short, -sin_short], [sin_short, cos_short]])
    third = np.block([[cos_short, sin_short], [-sin_short, cos_short]])
    seq_len = PBLK * QBLK
    angle = (order[:, None].astype(np.int64) * np.arange(PBLK)[None, :] % seq_len).astype(np.float32)
    angle = angle * np.float32(2.0 * math.pi / seq_len)
    half = [t.astype(ml_dtypes.bfloat16) for t in (forward, second, third, backward)]
    return half + [np.cos(angle).astype(np.float32), np.sin(angle).astype(np.float32)]


def pair_split():
    table = np.zeros((2 * LANES, 2 * LANES), np.float32)
    for e in range(2):
        for d in range(LANES):
            table[e * LANES + d, 2 * d + e] = 1.0
    return table.astype(ml_dtypes.bfloat16)


def nt_dot(left, right):
    return lax.dot_general(left, right, (((1,), (1,)), ((), ())), preferred_element_type=F32)


def pack_kernel(tokens_ref, spectrum_ref, split_ref, out_ref, wide):
    split = split_ref[...]
    for block in range(8):
        low, half = block // 2, block % 2
        turned = nt_dot(split, tokens_ref[block * LANES : (block + 1) * LANES, :])
        for e in range(2):
            row = e * 8 + half * 4 + low
            wide[pl.ds(row, LANES, stride=32), :] = turned[e * LANES : (e + 1) * LANES]
    lane = lax.broadcasted_iota(jnp.int32, (LANES, LANES), 0)
    eye = (lane == lax.broadcasted_iota(jnp.int32, (LANES, LANES), 1)).astype(F32).astype(BF16)
    for part in range(2):
        for low in range(4):
            turned = nt_dot(eye, spectrum_ref[part, low])
            for half in range(2):
                row = 16 + part * 8 + half * 4 + low
                wide[pl.ds(row, LANES, stride=32), :] = turned[:, half * LANES : (half + 1) * LANES]
    out_ref[...] = wide[...].reshape(LANES, 32, LANES).astype(BF16)


def pack(tokens, spectrum):
    return pl.pallas_call(
        pack_kernel,
        grid=(3,),
        in_specs=[
            pl.BlockSpec((1024, 256), lambda i: (0, i)),
            pl.BlockSpec((2, 4, 256, LANES), lambda i: (0, 0, 0, i)),
            pl.BlockSpec((256, 256), lambda i: (0, 0)),
        ],
        out_specs=pl.BlockSpec((LANES, 32, LANES), lambda i: (0, i, 0)),
        out_shape=jax.ShapeDtypeStruct((LANES, 96, LANES), BF16),
        scratch_shapes=[pltpu.VMEM((LANES * 32, LANES), F32)],
        compiler_params=pltpu.CompilerParams(vmem_limit_bytes=VMEM_LIMIT),
        cost_estimate=pl.CostEstimate(flops=2 * 10**9, bytes_accessed=6 * 2**20, transcendentals=0),
        name="pack",
    )(tokens, spectrum, pair_split())


def conv_kernel(data_ref, forward_ref, second_ref, third_ref, backward_ref, cos_ref, sin_ref, out_ref, wide, back, outs):
    slot = pl.program_id(0)
    wide[...] = data_ref[...].reshape(LANES * 32, LANES).astype(F32)

    def piece(row):
        return wide[pl.ds(row, LANES, stride=32), :]

    def filters(part):
        return jnp.concatenate(
            [
                jnp.concatenate([piece(16 + part * 8 + half * 4 + low) for half in range(2)], axis=1)
                for low in range(4)
            ],
            axis=0,
        )

    filter_real, filter_imag = filters(0), filters(1)
    for e in range(2):
        block = jnp.concatenate(
            [
                jnp.concatenate([piece(e * 8 + half * 4 + low) for half in range(2)], axis=1).astype(BF16)
                for low in range(4)
            ],
            axis=0,
        )
        first = jnp.dot(forward_ref[...], block, preferred_element_type=F32)
        first_real, first_imag = first[:QBLK], first[QBLK:]
        turn_cos, turn_sin = cos_ref[...], sin_ref[...]
        turned = jnp.concatenate(
            [
                (first_real * turn_cos + first_imag * turn_sin).astype(BF16),
                (first_imag * turn_cos - first_real * turn_sin).astype(BF16),
            ],
            axis=1,
        )
        spectral = jnp.dot(turned, second_ref[...], preferred_element_type=F32)
        spectral_real, spectral_imag = spectral[:, :PBLK], spectral[:, PBLK:]
        filtered = jnp.concatenate(
            [
                (spectral_real * filter_real - spectral_imag * filter_imag).astype(BF16),
                (spectral_real * filter_imag + spectral_imag * filter_real).astype(BF16),
            ],
            axis=1,
        )
        third = jnp.dot(filtered, third_ref[...], preferred_element_type=F32)
        back_real, back_imag = third[:, :PBLK], third[:, PBLK:]
        back[:QBLK, :] = (back_real * turn_cos - back_imag * turn_sin).astype(BF16)
        back[QBLK:, :] = (back_real * turn_sin + back_imag * turn_cos).astype(BF16)
        conv = jnp.dot(backward_ref[...], back[...], preferred_element_type=F32)
        for low in range(4):
            for half in range(2):
                row = (low // 2) * 24 + ((slot * 2 + e) * 2 + half) * 2 + low % 2
                outs[pl.ds(row, LANES, stride=48), :] = conv[
                    low * LANES : (low + 1) * LANES, half * LANES : (half + 1) * LANES
                ]

    @pl.when(slot == 2)
    def _():
        out_ref[...] = outs[...].astype(BF16)


def convolve(data, tables):
    rows = LANES * 48
    whole = lambda shape: pl.BlockSpec(shape, lambda i: (0,) * len(shape))
    return pl.pallas_call(
        conv_kernel,
        grid=(3,),
        in_specs=[pl.BlockSpec((LANES, 32, LANES), lambda i: (0, i, 0))] + [whole(t.shape) for t in tables],
        out_specs=whole((rows, LANES)),
        out_shape=jax.ShapeDtypeStruct((rows, LANES), BF16),
        scratch_shapes=[
            pltpu.VMEM((LANES * 32, LANES), F32),
            pltpu.VMEM((2 * QBLK, PBLK), BF16),
            pltpu.VMEM((rows, LANES), F32),
        ],
        compiler_params=pltpu.CompilerParams(vmem_limit_bytes=VMEM_LIMIT),
        cost_estimate=pl.CostEstimate(flops=64 * 10**8, bytes_accessed=8 * 2**20, transcendentals=0),
        name="convolve",
    )(data, *tables)


def hidden_kernel(
    side_ref, scales_ref, split_ref, conv_hbm, mine_hbm, theirs_hbm, mix_mine, mix_theirs,
    hidden_ref, shuffled_ref, conv_ref, tokens_ref, mix_ref, wide, normed, sems,
):
    side = side_ref[0]
    width = hidden_ref.shape[2]
    count = hidden_ref.shape[1]
    start = pl.multiple_of(side * count, count)
    copies = [
        pltpu.make_async_copy(conv_hbm, conv_ref, sems.at[0]),
        pltpu.make_async_copy(mine_hbm.at[pl.ds(start, count)], tokens_ref.at[0], sems.at[1]),
        pltpu.make_async_copy(theirs_hbm, tokens_ref.at[1], sems.at[2]),
        pltpu.make_async_copy(mix_mine, mix_ref.at[0], sems.at[3]),
        pltpu.make_async_copy(mix_theirs, mix_ref.at[1], sems.at[4]),
    ]
    for copy in copies:
        copy.start()
    split = split_ref[...]
    copies[0].wait()
    wide[...] = conv_ref[...].astype(F32)
    copies[1].wait()
    copies[2].wait()
    for block in range(count // LANES):
        low, half = block // 2, block % 2
        rows = slice(block * LANES, (block + 1) * LANES)
        total = 0.0
        for s in range(2):
            home = side if s == 0 else 1 - side
            pieces = []
            for slot in range(3):
                turned = jnp.concatenate(
                    [
                        wide[pl.ds(home * 24 + ((slot * 2 + e) * 2 + half) * 2 + low, LANES, stride=48), :].T
                        for e in range(2)
                    ],
                    axis=1,
                ).astype(BF16)
                conv = jnp.dot(turned, split, preferred_element_type=F32)
                cols = slice(slot * 256, (slot + 1) * 256)
                values = tokens_ref[s, rows, cols].astype(F32)
                mixed = conv + scales_ref[s, 0:1, cols] * values
                hidden = values + mixed * jax.nn.sigmoid(values)
                hidden_ref[s, rows, cols] = hidden
                pieces.append(jnp.sum(hidden, axis=1, keepdims=True))
            total = total + (pieces[0] + pieces[1] + pieces[2])
        mean = total / (2 * width)
        first = hidden_ref[0, rows, :] - mean
        second = hidden_ref[1, rows, :] - mean
        square = jnp.sum(first * first, axis=1, keepdims=True) + jnp.sum(second * second, axis=1, keepdims=True)
        scale = lax.rsqrt(square / (2 * width) + 1e-05)
        normed[0, rows, :] = (first * scale * scales_ref[0, 1:2, :]).astype(BF16)
        normed[1, rows, :] = (second * scale * scales_ref[1, 1:2, :]).astype(BF16)
    for s in range(2):
        copies[3 + s].wait()
        shuffled_ref[s] = jnp.dot(normed[s], mix_ref[s], preferred_element_type=F32).astype(BF16)


def make_hidden(side, conv, mine, theirs, scales, mix):
    rows = theirs.shape[0]
    return pl.pallas_call(
        hidden_kernel,
        in_specs=[pl.BlockSpec(memory_space=pltpu.SMEM)]
        + [pl.BlockSpec(memory_space=pltpu.VMEM)] * 2
        + [pl.BlockSpec(memory_space=pltpu.HBM)] * 5,
        out_shape=[
            jax.ShapeDtypeStruct((2, rows, 768), F32),
            jax.ShapeDtypeStruct((2, rows, 1024), BF16),
        ],
        scratch_shapes=[
            pltpu.VMEM(conv.shape, BF16),
            pltpu.VMEM((2, rows, 768), BF16),
            pltpu.VMEM((2, 768, 1024), BF16),
            pltpu.VMEM(conv.shape, F32),
            pltpu.VMEM((2, rows, 768), BF16),
            pltpu.SemaphoreType.DMA((5,)),
        ],
        compiler_params=pltpu.CompilerParams(vmem_limit_bytes=SMALL_LIMIT),
        cost_estimate=pl.CostEstimate(flops=3 * 10**9, bytes_accessed=12 * 2**20, transcendentals=10**6),
        name="hidden",
    )(side, scales, pair_split(), conv, mine, theirs, *mix)


def mlp_kernel(
    side_ref, hidden_ref, shuffled_ref, up_mine, up_theirs, down_mine, down_theirs, mix_mine, mix_theirs,
    keep_ref, send_ref, down_buf, gathered,
):
    side = side_ref[0]
    for group, (up_ref, down_ref) in enumerate(((up_mine, down_mine), (up_theirs, down_theirs))):
        home = side if group == 0 else 1 - side
        for c in range(2):
            lanes = pl.multiple_of((2 * home + c) * 256, 256)
            total = 0.0
            for s in range(2):
                start = pl.multiple_of((side if s == 0 else 1 - side) * 192, 192)
                mixed = shuffled_ref[s, :, pl.ds(lanes, 256)][:, :192]
                total = total + jnp.dot(mixed, up_ref[c, pl.ds(start, 192), :], preferred_element_type=F32)
            active = jax.nn.gelu(total, approximate=True).astype(BF16)
            down_buf[...] = jnp.dot(active, down_ref[c], preferred_element_type=F32).astype(BF16)
            for s in range(2):
                start = pl.multiple_of((side if s == 0 else 1 - side) * LANES, LANES)
                gathered[s, :, pl.ds(lanes, 256)] = down_buf[:, pl.ds(start, 256)]
    for s, (ref, mix_ref) in enumerate(((keep_ref, mix_mine), (send_ref, mix_theirs))):
        outcome = jnp.dot(gathered[s], mix_ref[...], preferred_element_type=F32)
        ref[...] = (hidden_ref[s] + outcome).astype(BF16)


def mlp(side, hidden, shuffled, ups, downs, mix, chunk, chunks):
    rows = hidden.shape[1] // chunks
    whole = lambda shape: pl.BlockSpec(shape, lambda i: (0,) * len(shape), pipeline_mode=pl.Buffered(1))
    return pl.pallas_call(
        mlp_kernel,
        grid=(1,),
        in_specs=[
            pl.BlockSpec(memory_space=pltpu.SMEM),
            pl.BlockSpec((2, rows, 768), lambda i: (0, chunk, 0), pipeline_mode=pl.Buffered(1)),
            pl.BlockSpec((2, rows, 1024), lambda i: (0, chunk, 0), pipeline_mode=pl.Buffered(1)),
        ]
        + [whole(w.shape) for w in (*ups, *downs, *mix)],
        out_specs=[whole((rows, 768))] * 2,
        out_shape=[jax.ShapeDtypeStruct((rows, 768), BF16)] * 2,
        scratch_shapes=[pltpu.VMEM((rows, 384), BF16), pltpu.VMEM((2, rows, 1024), BF16)],
        compiler_params=pltpu.CompilerParams(vmem_limit_bytes=SMALL_LIMIT),
        cost_estimate=pl.CostEstimate(
            flops=rows * 14 * 10**6, bytes_accessed=14 * 2**20, transcendentals=rows * 6144
        ),
        name="mlp",
    )(side, hidden, shuffled, *ups, *downs, *mix)


def prepare_kernel(place_ref, in_got, in_passed, out_got, out_passed, first_ref, last_ref):
    home, core = place_ref[0], place_ref[1]
    blocks, inner = in_got.shape[0], in_got.shape[1]
    piece = inner // NB
    spare = 256 - blocks * piece

    def places(shape, axis, offset):
        row = lax.broadcasted_iota(jnp.int32, shape, axis)
        group = sum((row >= c * piece).astype(jnp.int32) for c in range(1, NB))
        target = lax.broadcasted_iota(jnp.int32, shape, 1 - axis)
        return (target == row + group * (256 - piece) + offset).astype(F32).astype(BF16)

    for b in range(blocks):
        weight = jnp.where(core == 0, in_got[b], in_passed[b])
        picked = jnp.dot(weight, places((inner, NB * 256), 0, b * piece), preferred_element_type=F32)
        first_ref[b * inner : (b + 1) * inner, :] = picked.astype(BF16)
        weight = jnp.where(core == 1, out_got[b], out_passed[b])
        offset = b * piece + jnp.where(home == 0, 0, spare)
        picked = jnp.dot(places((NB * 256, inner), 1, offset), weight, preferred_element_type=F32)
        last_ref[:, b * inner : (b + 1) * inner] = picked.astype(BF16)


def prepare(place, in_got, in_passed, out_got, out_passed):
    blocks, inner = in_got.shape[0], in_got.shape[1]
    return pl.pallas_call(
        prepare_kernel,
        in_specs=[pl.BlockSpec(memory_space=pltpu.SMEM)] + [pl.BlockSpec(memory_space=pltpu.VMEM)] * 4,
        out_shape=[
            jax.ShapeDtypeStruct((blocks * inner, NB * 256), BF16),
            jax.ShapeDtypeStruct((NB * 256, blocks * inner), BF16),
        ],
        compiler_params=pltpu.CompilerParams(vmem_limit_bytes=VMEM_LIMIT),
        cost_estimate=pl.CostEstimate(flops=2 * 10**9, bytes_accessed=6 * 2**20, transcendentals=0),
        name="prepare",
    )(place, in_got, in_passed, out_got, out_passed)


def make_per_device(chunks):
    def per_device(tokens, spectrum, skip, gain, mix_in, w_up, w_down, mix_out):
        groups = lax.axis_size("seq")
        both = ("seq", "ch")
        side = lax.axis_index("ch")
        core = lax.axis_index("seq") % 2
        swap = [(0, 1), (1, 0)]
        step = groups // 2

        def near(which):
            return [
                (s * 2 + h, (s ^ step) * 2 + 1 - h) for h in range(2) for s in range(groups) if s % 2 == which
            ]

        def across(which):
            return [(s, s ^ 1) for s in range(groups) if s % 2 == which]

        count = tokens.shape[0] // 2
        place = jnp.stack([side, core]).astype(jnp.int32)
        other_place = jnp.stack([1 - side, core]).astype(jnp.int32)
        packed = pack(tokens, spectrum)
        data = lax.all_to_all(packed, "seq", split_axis=0, concat_axis=0, tiled=True)

        weights, cores = (w_up, w_down, mix_in, mix_out), (0, 1, 0, 1)
        got = [lax.ppermute(w, both, near(which)) for w, which in zip(weights, cores)]
        theirs = lax.ppermute(lax.dynamic_slice_in_dim(tokens, (1 - side) * count, count, axis=0), "ch", swap)
        scales_mine = jnp.stack([skip, gain])
        scales = jnp.stack([scales_mine, lax.ppermute(scales_mine, "ch", swap)])
        first_mine, last_mine = prepare(place, mix_in, mix_in, mix_out, mix_out)
        data, first_mine, last_mine, theirs, scales = lax.optimization_barrier(
            (data, first_mine, last_mine, theirs, scales)
        )
        conv = convolve(data, make_tables(groups))

        conv, *got = lax.optimization_barrier((conv, *got))
        conv = lax.all_to_all(conv, both, split_axis=0, concat_axis=0, tiled=True)
        passed = [lax.ppermute(g, "seq", across(which)) for g, which in zip(got, cores)]
        up_theirs, down_theirs = (jnp.where(core == cores[i], got[i], passed[i]) for i in range(2))
        first_theirs, last_theirs = prepare(other_place, got[2], passed[2], got[3], passed[3])
        mix_first = (first_mine, first_theirs)
        mix_last = (last_mine, last_theirs)
        hidden, shuffled = make_hidden(place, conv, tokens, theirs, scales, mix_first)
        out = jnp.zeros(tokens.shape, tokens.dtype)
        rows = count // chunks
        for q in range(chunks):
            keep, send = mlp(place, hidden, shuffled, (w_up, up_theirs), (w_down, down_theirs), mix_last, q, chunks)
            sent = lax.ppermute(send, "ch", swap)
            out = lax.dynamic_update_slice_in_dim(out, keep, side * count + q * rows, axis=0)
            out = lax.dynamic_update_slice_in_dim(out, sent, (1 - side) * count + q * rows, axis=0)
        return out

    return per_device


def solution(mesh):
    return jax.shard_map(
        make_per_device(2),
        mesh=mesh,
        in_specs=(
            P("seq", "ch"),
            P(None, "seq", None, "ch"),
            P("ch"),
            P("ch"),
            P("ch", None, None),
            P("ch", None, None),
            P("ch", None, None),
            P("ch", None, None),
        ),
        out_specs=P("seq", "ch"),
        check_vma=False,
    )
```

time: 241 us -> 207 us (0.86)
  blocking collectives: 84.9 us -> 0 us
  starting transfers between devices: 18.3 us -> 54.7 us
  waiting for transfers between devices: 58.2 us -> 81.7 us
  local copies, waits for them, and re-layouts: 16.7 us -> 10.3 us
    all_to_all x1 -> x0, blocking collectives: 84.9 us -> none  [per_device(): lax.all_to_all(packed, 'seq', split_axis=0, concat_axis=0, tiled=True)]
    all_to_all x1 -> x2, waiting for transfers between devices: 26.2 us -> 46.1 us  [the longest x1 25.1 us: per_device(): lax.all_to_all(packed, 'seq', split_axis=0, concat_axis=0, tiled=True)]
    all_to_all x1 -> x2, starting transfers between devices: 10.6 us -> 29.3 us  [the longest x1 14.9 us: per_device(): conv = lax.all_to_all(conv, both, split_axis=0, concat_axis=0, tiled=True)]
    ppermute x3 -> x12, starting transfers between devices: 7.63 us -> 25.4 us  [the longest x4 10.6 us: per_device(): lax.ppermute(w, both, near(which))]
    select_n x0 -> x2, other arithmetic: none -> 5.33 us  [per_device(): jnp.where(core == cores[i], got[i], passed[i])]
    squeeze x2 -> x0, local copies, waits for them, and re-layouts: 4.46 us -> none  [the longest x1 2.71 us: columns(): first = jnp.pad(part[0], ((0, 0), (0, 256 - half)))]
    another operation x5 -> x4, other arithmetic: 5.2 us -> 1.33 us  [the longest x1 0.65 us: per_device(): other_place = jnp.stack([1 - side, core]).astype(jnp.int32)]
    ppermute x3 -> x12, waiting for transfers between devices: 32 us -> 35.6 us  [the longest x1 23.8 us: per_device(): scales = jnp.stack([scales_mine, lax.ppermute(scales_mine, 'ch', swap)])]
  transfers between devices with their start and end apart: 4 -> 14, of which waited for: 3 -> 7; matrix products, arithmetic and copies ran while one was open for 8% -> 5% of each run, Pallas kernels for 0% -> 15%
where the time goes in v1:
time: 207 us; the launch traced here: 206 us
  waiting for transfers between devices  81.7 us (39%)
  starting transfers between devices  54.7 us (26%)
  Pallas kernels  52.5 us (25%)
  local copies, waits for them, and re-layouts  10.3 us (5%)
  other arithmetic  6.66 us (3%)
    all_to_all x1, waiting for transfers between devices, per_device(): lax.all_to_all(packed, 'seq', split_axis=0, concat_axis=0, tiled=True)  25.1 us
    ppermute x1, waiting for transfers between devices, per_device(): scales = jnp.stack([scales_mine, lax.ppermute(scales_mine, 'ch', swap)])  23.8 us
    all_to_all x1, waiting for transfers between devices, per_device(): conv = lax.all_to_all(conv, both, split_axis=0, concat_axis=0, tiled=True)  21.1 us
    pallas_call x1, Pallas kernels, convolve(): pl.pallas_call(conv_kernel, grid=(3,), in_specs=[pl.BlockSpec((LANES, 32,...  16.2 us
    all_to_all x1, starting transfers between devices, per_device(): conv = lax.all_to_all(conv, both, split_axis=0, concat_axis=0, tiled=True)  14.9 us
    all_to_all x1, starting transfers between devices, per_device(): lax.all_to_all(packed, 'seq', split_axis=0, concat_axis=0, tiled=True)  14.4 us
    pallas_call x2, Pallas kernels, mlp(): pl.pallas_call(mlp_kernel, grid=(1,), in_specs=[pl.BlockSpec(memory_space...  12.2 us
    ppermute x4, starting transfers between devices, per_device(): lax.ppermute(w, both, near(which))  10.6 us
  transfers between devices with their start and end apart: 14, of which 7 were waited for; matrix products, arithmetic and copies ran while one was open for 5% of the time, Pallas kernels for 15%

profile of v1, /device:TPU:8, one launch (start us, length us, event | category | flops | bytes accessed | tf_op | source)
XLA Modules:
  0.0 206.1 jit_solution(17676670099693931)
XLA Ops:
  0.0 7.7 %pack.1 = bf16[128,96,128]{2,1,0:T(8,128)(2,1)} custom-call(bf16[1024,768]{1,0:T(8,128)(2,1)} %mine_hbm.1, bf16[2,4,256,384]{3,2,1,0:T(8,128)(2,1)} %spectrum_ref.1, bf16[256,256]{1,0:T(8,128)(2,1)} %constant.48.clone.split_ref), custom_call_target="tpu_custom_call" | custom-call | flops 2000000000 | bytes 6291456 | tf_op jit(solution)/shard_map/pack/pallas_call | solution.py:83
  7.7 14.4 %all-to-all-start = ((bf16[128,96,128]{2,1,0:T(8,128)(2,1)}), bf16[128,96,128]{2,1,0:T(8,128)(2,1)}, u32[]{:S(2)}, u32[]{:S(2)}) async-start(bf16[128,96,128]{2,1,0:T(8,128)(2,1)} %pack.1), calls=%async_computation | async-start | bytes 6291456 | tf_op jit(solution)/shard_map/all_to_all | solution.py:368
  22.1 5.1 %collective-permute-start.2 = (bf16[2,384,1536]{2,1,0:T(8,128)(2,1)S(1)}, bf16[2,384,1536]{2,1,0:T(8,128)(2,1)}, u32[]{:S(2)}, u32[]{:S(2)}) collective-permute-start(bf16[2,384,1536]{2,1,0:T(8,128)(2,1)S(1)} %copy-done.1), channel_id=1, source_target_pairs={{0,129},{4,133},{8,137},{12,141},{16,145},{20,149},{24,153},{28,15... | collective-permute-start | bytes 7077896 | tf_op jit(solution)/shard_map/ppermute | solution.py:371
  27.1 2.1 %collective-permute-start.3 = (bf16[2,1536,384]{2,1,0:T(8,128)(2,1)}, bf16[2,1536,384]{2,1,0:T(8,128)(2,1)}, u32[]{:S(2)}, u32[]{:S(2)}) collective-permute-start(bf16[2,1536,384]{2,1,0:T(8,128)(2,1)} %down_mine.3), channel_id=1, source_target_pairs={{2,131},{6,135},{10,139},{14,143},{18,147},{22,151},{26,155},{30,1... | collective-permute-start | bytes 7077896 | tf_op jit(solution)/shard_map/ppermute | solution.py:371
  29.2 2.1 %constant_dynamic-slice_fusion = bf16[512,768]{1,0:T(8,128)(2,1)} fusion(bf16[1024,768]{1,0:T(8,128)(2,1)} %mine_hbm.1, s32[]{:T(128)S(6)} %select_n.37), kind=kLoop, calls=%fused_computation.8 | loop fusion | bytes 1572868 | tf_op jit(solution)/shard_map/dynamic_slice | solution.py:372
  32.1 2.8 %collective-permute-start.1 = (f32[2,768]{1,0:T(2,128)S(1)}, f32[2,768]{1,0:T(2,128)S(1)}, u32[]{:S(2)}, u32[]{:S(2)}) collective-permute-start(f32[2,768]{1,0:T(2,128)S(1)} %get-tuple-element.46), channel_id=1, source_target_pairs={{0,1},{1,0},{2,3},{3,2},{4,5},{5,4},{6,7},{7,6},{8,9},{9,8},{10,11... | collective-permute-start | bytes 18440 | tf_op jit(solution)/shard_map/ppermute | solution.py:374
  34.9 2.0 collective-permute-start.4
  37.6 4.8 %prepare.2 = (bf16[768,1024]{1,0:T(8,128)(2,1)}, bf16[1024,768]{1,0:T(8,128)(2,1)}) custom-call(s32[2]{0:T(128)} %pad_add_fusion.place_ref.side_ref, bf16[2,384,384]{2,1,0:T(8,128)(2,1)} %in_passed.1, bf16[2,384,384]{2,1,0:T(8,128)(2,1)} %in_passed.1, bf16[2,384,384]{2,1,0:T(8,128)(2,1)} %out_passed.1, bf16[2,384,384]{2,1,0:T(8,128)(2,1)} %out_passed.1), custom_call_target="tpu_custom_call" | custom-call | flops 2000000000 | bytes 6291456 | tf_op jit(solution)/shard_map/prepare/pallas_call | solution.py:334
  42.4 23.8 %collective-permute-done.1 = f32[2,768]{1,0:T(2,128)S(1)} collective-permute-done((f32[2,768]{1,0:T(2,128)S(1)}, f32[2,768]{1,0:T(2,128)S(1)}, u32[]{:S(2)}, u32[]{:S(2)}) %collective-permute-start.1) | collective-permute-done | bytes 6176 | tf_op jit(solution)/shard_map/ppermute | solution.py:374
  66.2 1.5 collective-permute-start.5
  67.7 25.1 %all-to-all-done.data_ref = bf16[128,96,128]{2,1,0:T(8,128)(2,1)} async-done(((bf16[128,96,128]{2,1,0:T(8,128)(2,1)}), bf16[128,96,128]{2,1,0:T(8,128)(2,1)}, u32[]{:S(2)}, u32[]{:S(2)}) %all-to-all-start) | async-done | bytes 3145760 | tf_op jit(solution)/shard_map/all_to_all | solution.py:368
  92.7 16.2 %convolve.1 = bf16[6144,128]{1,0:T(8,128)(2,1)} custom-call(bf16[128,96,128]{2,1,0:T(8,128)(2,1)} %all-to-all-done.data_ref, bf16[1024,512]{1,0:T(8,128)(2,1)} %constant.49.clone.forward_ref, bf16[512,512]{1,0:T(8,128)(2,1)} %constant.50.clone.second_ref, bf16[512,512]{1,0:T(8,128)(2,1)} %constant.51.clone.third_ref, ...), custom_call_target="tpu_custom_call" | custom-call | flops 6400000000 | bytes 8388608 | tf_op jit(solution)/shard_map/convolve/pallas_call | solution.py:164
  109.0 1.3 collective-permute-start.9
  110.3 14.9 %all-to-all-start.1 = ((bf16[256,24,128]{2,1,0:T(8,128)(2,1)}), bf16[256,24,128]{2,1,0:T(8,128)(2,1)}, u32[]{:S(2)}, u32[]{:S(2)}) async-start(bf16[256,24,128]{2,1,0:T(8,128)(2,1)} %bitcast.8), calls=%async_computation.1 | async-start | bytes 3145728 | tf_op jit(solution)/shard_map/all_to_all | solution.py:382
  125.3 3.5 %collective-permute-start.8 = (bf16[2,384,1536]{2,1,0:T(8,128)(2,1)}, bf16[2,384,1536]{2,1,0:T(8,128)(2,1)}, u32[]{:S(2)}, u32[]{:S(2)}) collective-permute-start(bf16[2,384,1536]{2,1,0:T(8,128)(2,1)} %collective-permute-done.2), channel_id=1, source_target_pairs={{0,2},{4,6},{8,10},{12,14},{16,18},{20,22},{24,26},{28,30},{32,34}... | collective-permute-start | bytes 7077896 | tf_op jit(solution)/shard_map/ppermute | solution.py:383
  128.7 1.3 collective-permute-start.6
  130.1 1.5 collective-permute-start.7
  132.5 1.6 collective-permute-done.7.out_passed
  135.0 4.6 %prepare.3 = (bf16[768,1024]{1,0:T(8,128)(2,1)}, bf16[1024,768]{1,0:T(8,128)(2,1)}) custom-call(s32[2]{0:T(128)} %pad_add_fusion.1.place_ref, bf16[2,384,384]{2,1,0:T(8,128)(2,1)} %collective-permute-done.4.in_got, bf16[2,384,384]{2,1,0:T(8,128)(2,1)} %copy-done.16, bf16[2,384,384]{2,1,0:T(8,128)(2,1)} %collective-permute-done.5.out_got, ...), custom_call_target="tpu_custom_call" | custom-call | flops 2000000000 | bytes 6291456 | tf_op jit(solution)/shard_map/prepare/pallas_call | solution.py:334
  139.6 1.9 broadcast_select_fusion.down_theirs
  141.6 3.4 %broadcast_select_fusion.1.up_theirs = bf16[2,384,1536]{2,1,0:T(8,128)(2,1)} fusion(bf16[2,384,1536]{2,1,0:T(8,128)(2,1)} %collective-permute-done.2, bf16[2,384,1536]{2,1,0:T(8,128)(2,1)} %collective-permute-done.8, pred[]{:T(512)S(6)} %eq.8), kind=kLoop, calls=%fused_computation.1 | loop fusion | flops 1179648 | bytes 7077889 | tf_op jit(solution)/shard_map/jit(_where)/select_n | solution.py:384
  145.0 21.1 %all-to-all-done.1 = bf16[256,24,128]{2,1,0:T(8,128)(2,1)} async-done(((bf16[256,24,128]{2,1,0:T(8,128)(2,1)}), bf16[256,24,128]{2,1,0:T(8,128)(2,1)}, u32[]{:S(2)}, u32[]{:S(2)}) %all-to-all-start.1) | async-done | bytes 1572896 | tf_op jit(solution)/shard_map/all_to_all | solution.py:382
  166.0 1.4 copy-done.6
  167.4 1.1 copy-done.9
  168.6 1.4 copy-done.11
  170.0 1.4 copy-done.12
  171.4 7.0 %hidden.1 = (f32[2,512,768]{2,1,0:T(8,128)S(1)}, bf16[2,512,1024]{2,1,0:T(8,128)(2,1)S(1)}) custom-call(s32[2]{0:T(128)S(1)} %copy-done.7, f32[2,2,768]{2,1,0:T(2,128)S(1)} %pad_maximum_fusion.scales_ref, bf16[256,256]{1,0:T(8,128)(2,1)S(1)} %copy-done.10, bf16[6144,128]{1,0:T(8,128)(2,1)} %bitcast.5.conv_hbm, bf16[1024,768]{1,0:T(8,128)(2,1)S(1)} %copy-done.6, ...), custom_call_target="tpu_custom_call" | custom-call | flops 3000000000 | bytes 12582912 | tf_op jit(solution)/shard_map/hidden/pallas_call | solution.py:240
  178.5 6.5 %mlp.2 = (bf16[256,768]{1,0:T(8,128)(2,1)S(1)}, bf16[256,768]{1,0:T(8,128)(2,1)}) custom-call(s32[2]{0:T(128)S(1)} %copy-done.7, f32[2,512,768]{2,1,0:T(8,128)S(1)} %get-tuple-element.35.hidden_ref, bf16[2,512,1024]{2,1,0:T(8,128)(2,1)S(1)} %get-tuple-element.36.shuffled_ref, bf16[2,384,1536]{2,1,0:T(8,128)(2,1)S(1)} %copy-done.2, ...), custom_call_target="tpu_custom_call" | custom-call | flops 3584000000 | bytes 14680064 | tf_op jit(solution)/shard_map/mlp/pallas_call | solution.py:290
  185.8 5.7 %mlp.3 = (bf16[256,768]{1,0:T(8,128)(2,1)S(1)}, bf16[256,768]{1,0:T(8,128)(2,1)S(1)}) custom-call(s32[2]{0:T(128)S(1)} %copy-done.7, f32[2,512,768]{2,1,0:T(8,128)S(1)} %get-tuple-element.35.hidden_ref, bf16[2,512,1024]{2,1,0:T(8,128)(2,1)S(1)} %get-tuple-element.36.shuffled_ref, bf16[2,384,1536]{2,1,0:T(8,128)(2,1)S(1)} %copy-done.2, ...), custom_call_target="tpu_custom_call" | custom-call | flops 3584000000 | bytes 14680064 | tf_op jit(solution)/shard_map/mlp/pallas_call | solution.py:290
  191.5 2.8 %collective-permute-start.11 = (bf16[256,768]{1,0:T(8,128)(2,1)S(1)}, bf16[256,768]{1,0:T(8,128)(2,1)S(1)}, u32[]{:S(2)}, u32[]{:S(2)}) collective-permute-start(bf16[256,768]{1,0:T(8,128)(2,1)S(1)} %get-tuple-element.44), channel_id=1, source_target_pairs={{0,1},{1,0},{2,3},{3,2},{4,5},{5,4},{6,7},{7,6},{8,9},{9,8},{10,11... | collective-permute-start | bytes 1179656 | tf_op jit(solution)/shard_map/ppermute | solution.py:393
  194.5 4.1 %collective-permute-done.10 = bf16[256,768]{1,0:T(8,128)(2,1)} collective-permute-done((bf16[256,768]{1,0:T(8,128)(2,1)}, bf16[256,768]{1,0:T(8,128)(2,1)}, u32[]{:S(2)}, u32[]{:S(2)}) %collective-permute-start.10) | collective-permute-done | bytes 393248 | tf_op jit(solution)/shard_map/ppermute | solution.py:393
  199.6 5.7 %collective-permute-done.11 = bf16[256,768]{1,0:T(8,128)(2,1)S(1)} collective-permute-done((bf16[256,768]{1,0:T(8,128)(2,1)S(1)}, bf16[256,768]{1,0:T(8,128)(2,1)S(1)}, u32[]{:S(2)}, u32[]{:S(2)}) %collective-permute-start.11) | collective-permute-done | bytes 393248 | tf_op jit(solution)/shard_map/ppermute | solution.py:393
  (53 shorter events, 6.1 us)
Async XLA Ops:
  7.7 14.4 %copy-start.1 = (bf16[2,384,1536]{2,1,0:T(8,128)(2,1)S(1)}, bf16[2,384,1536]{2,1,0:T(8,128)(2,1)}, u32[]{:S(2)}) copy-start(bf16[2,384,1536]{2,1,0:T(8,128)(2,1)} %up_mine.3) | copy-start | bytes 7077892
  7.7 85.1 %all-to-all-start = ((bf16[128,96,128]{2,1,0:T(8,128)(2,1)}), bf16[128,96,128]{2,1,0:T(8,128)(2,1)}, u32[]{:S(2)}, u32[]{:S(2)}) async-start(bf16[128,96,128]{2,1,0:T(8,128)(2,1)} %pack.1), calls=%async_computation | async-start | bytes 6291456 | tf_op jit(solution)/shard_map/all_to_all | solution.py:368
  22.0 10.0 %copy-start.14 = (f32[768]{0:T(1024)S(1)}, f32[768]{0:T(1024)}, u32[]{:S(2)}) copy-start(f32[768]{0:T(1024)} %param.18) | copy-start | bytes 9220
  22.0 10.0 %copy-start.15 = (f32[768]{0:T(1024)S(1)}, f32[768]{0:T(1024)}, u32[]{:S(2)}) copy-start(f32[768]{0:T(1024)} %param.19) | copy-start | bytes 9220
  22.1 86.9 %collective-permute-start.2 = (bf16[2,384,1536]{2,1,0:T(8,128)(2,1)S(1)}, bf16[2,384,1536]{2,1,0:T(8,128)(2,1)}, u32[]{:S(2)}, u32[]{:S(2)}) collective-permute-start(bf16[2,384,1536]{2,1,0:T(8,128)(2,1)S(1)} %copy-done.1), channel_id=1, source_target_pairs={{0,129},{4,133},{8,137},{12,141},{16,145},{20,149},{24,153},{28,15... | collective-permute-start | bytes 7077896 | tf_op jit(solution)/shard_map/ppermute | solution.py:371
  27.1 81.9 %collective-permute-start.3 = (bf16[2,1536,384]{2,1,0:T(8,128)(2,1)}, bf16[2,1536,384]{2,1,0:T(8,128)(2,1)}, u32[]{:S(2)}, u32[]{:S(2)}) collective-permute-start(bf16[2,1536,384]{2,1,0:T(8,128)(2,1)} %down_mine.3), channel_id=1, source_target_pairs={{2,131},{6,135},{10,139},{14,143},{18,147},{22,151},{26,155},{30,1... | collective-permute-start | bytes 7077896 | tf_op jit(solution)/shard_map/ppermute | solution.py:371
  31.3 36.4 %collective-permute-start = (bf16[512,768]{1,0:T(8,128)(2,1)}, bf16[512,768]{1,0:T(8,128)(2,1)S(1)}, u32[]{:S(2)}, u32[]{:S(2)}) collective-permute-start(bf16[512,768]{1,0:T(8,128)(2,1)} %constant_dynamic-slice_fusion), channel_id=1, source_target_pairs={{0,1},{1,0},{2,3},{3,2},{4,5},{5,4},{6,7},{7,6},{8,9},{9,8},{10,11... | collective-permute-start | bytes 2359304 | tf_op jit(solution)/shard_map/ppermute | solution.py:372
  32.1 34.1 %collective-permute-start.1 = (f32[2,768]{1,0:T(2,128)S(1)}, f32[2,768]{1,0:T(2,128)S(1)}, u32[]{:S(2)}, u32[]{:S(2)}) collective-permute-start(f32[2,768]{1,0:T(2,128)S(1)} %get-tuple-element.46), channel_id=1, source_target_pairs={{0,1},{1,0},{2,3},{3,2},{4,5},{5,4},{6,7},{7,6},{8,9},{9,8},{10,11... | collective-permute-start | bytes 18440 | tf_op jit(solution)/shard_map/ppermute | solution.py:374
  34.9 74.0 %collective-permute-start.4 = (bf16[2,384,384]{2,1,0:T(8,128)(2,1)}, bf16[2,384,384]{2,1,0:T(8,128)(2,1)}, u32[]{:S(2)}, u32[]{:S(2)}) collective-permute-start(bf16[2,384,384]{2,1,0:T(8,128)(2,1)} %in_passed.1), channel_id=1, source_target_pairs={{0,129},{4,133},{8,137},{12,141},{16,145},{20,149},{24,153},{28,15... | collective-permute-start | bytes 1769480 | tf_op jit(solution)/shard_map/ppermute | solution.py:371
  66.2 42.8 %collective-permute-start.5 = (bf16[2,384,384]{2,1,0:T(8,128)(2,1)}, bf16[2,384,384]{2,1,0:T(8,128)(2,1)}, u32[]{:S(2)}, u32[]{:S(2)}) collective-permute-start(bf16[2,384,384]{2,1,0:T(8,128)(2,1)} %out_passed.1), channel_id=1, source_target_pairs={{2,131},{6,135},{10,139},{14,143},{18,147},{22,151},{26,155},{30,1... | collective-permute-start | bytes 1769480 | tf_op jit(solution)/shard_map/ppermute | solution.py:371
  67.7 41.3 %copy-start.8 = (bf16[512,768]{1,0:T(8,128)(2,1)}, bf16[512,768]{1,0:T(8,128)(2,1)S(1)}, u32[]{:S(2)}) copy-start(bf16[512,768]{1,0:T(8,128)(2,1)S(1)} %collective-permute-done.theirs_hbm) | copy-start | bytes 2359300
  109.0 30.6 %collective-permute-start.9 = (bf16[2,1536,384]{2,1,0:T(8,128)(2,1)}, bf16[2,1536,384]{2,1,0:T(8,128)(2,1)}, u32[]{:S(2)}, u32[]{:S(2)}) collective-permute-start(bf16[2,1536,384]{2,1,0:T(8,128)(2,1)} %collective-permute-done.3), channel_id=1, source_target_pairs={{2,0},{6,4},{10,8},{14,12},{18,16},{22,20},{26,24},{30,28},{34,32}... | collective-permute-start | bytes 7077896 | tf_op jit(solution)/shard_map/ppermute | solution.py:383
  110.3 55.7 %all-to-all-start.1 = ((bf16[256,24,128]{2,1,0:T(8,128)(2,1)}), bf16[256,24,128]{2,1,0:T(8,128)(2,1)}, u32[]{:S(2)}, u32[]{:S(2)}) async-start(bf16[256,24,128]{2,1,0:T(8,128)(2,1)} %bitcast.8), calls=%async_computation.1 | async-start | bytes 3145728 | tf_op jit(solution)/shard_map/all_to_all | solution.py:382
  125.3 16.3 %collective-permute-start.8 = (bf16[2,384,1536]{2,1,0:T(8,128)(2,1)}, bf16[2,384,1536]{2,1,0:T(8,128)(2,1)}, u32[]{:S(2)}, u32[]{:S(2)}) collective-permute-start(bf16[2,384,1536]{2,1,0:T(8,128)(2,1)} %collective-permute-done.2), channel_id=1, source_target_pairs={{0,2},{4,6},{8,10},{12,14},{16,18},{20,22},{24,26},{28,30},{32,34}... | collective-permute-start | bytes 7077896 | tf_op jit(solution)/shard_map/ppermute | solution.py:383
  128.7 3.8 %collective-permute-start.6 = (bf16[2,384,384]{2,1,0:T(8,128)(2,1)}, bf16[2,384,384]{2,1,0:T(8,128)(2,1)S(1)}, u32[]{:S(2)}, u32[]{:S(2)}) collective-permute-start(bf16[2,384,384]{2,1,0:T(8,128)(2,1)} %collective-permute-done.4.in_got), channel_id=1, source_target_pairs={{0,2},{4,6},{8,10},{12,14},{16,18},{20,22},{24,26},{28,30},{32,34}... | collective-permute-start | bytes 1769480 | tf_op jit(solution)/shard_map/ppermute | solution.py:383
  130.1 4.1 %collective-permute-start.7 = (bf16[2,384,384]{2,1,0:T(8,128)(2,1)}, bf16[2,384,384]{2,1,0:T(8,128)(2,1)S(1)}, u32[]{:S(2)}, u32[]{:S(2)}) collective-permute-start(bf16[2,384,384]{2,1,0:T(8,128)(2,1)} %collective-permute-done.5.out_got), channel_id=1, source_target_pairs={{2,0},{6,4},{10,8},{14,12},{18,16},{22,20},{26,24},{30,28},{34,32}... | collective-permute-start | bytes 1769480 | tf_op jit(solution)/shard_map/ppermute | solution.py:383
  132.5 1.7 copy-start.16
  134.2 0.8 copy-start.17
  141.6 24.5 %copy-start.7 = (s32[2]{0:T(128)S(1)}, s32[2]{0:T(128)}, u32[]{:S(2)}) copy-start(s32[2]{0:T(128)} %pad_add_fusion.place_ref.side_ref) | copy-start | bytes 28
  141.6 24.5 %copy-start.10 = (bf16[256,256]{1,0:T(8,128)(2,1)S(1)}, bf16[256,256]{1,0:T(8,128)(2,1)}, u32[]{:S(2)}) copy-start(bf16[256,256]{1,0:T(8,128)(2,1)} %constant.48.clone.split_ref) | copy-start | bytes 393220
  166.0 1.4 copy-start.6
  167.4 1.1 copy-start.9
  168.6 1.4 copy-start.11
  170.0 1.4 copy-start.12
  171.4 7.1 %copy-start = (bf16[2,384,1536]{2,1,0:T(8,128)(2,1)S(1)}, bf16[2,384,1536]{2,1,0:T(8,128)(2,1)}, u32[]{:S(2)}) copy-start(bf16[2,384,1536]{2,1,0:T(8,128)(2,1)} %broadcast_select_fusion.1.up_theirs) | copy-start | bytes 7077892
  171.4 7.1 %copy-start.2 = (bf16[2,384,1536]{2,1,0:T(8,128)(2,1)S(1)}, bf16[2,384,1536]{2,1,0:T(8,128)(2,1)}, u32[]{:S(2)}) copy-start(bf16[2,384,1536]{2,1,0:T(8,128)(2,1)} %up_mine.3) | copy-start | bytes 7077892
  171.4 7.1 %copy-start.3 = (bf16[2,1536,384]{2,1,0:T(8,128)(2,1)S(1)}, bf16[2,1536,384]{2,1,0:T(8,128)(2,1)}, u32[]{:S(2)}) copy-start(bf16[2,1536,384]{2,1,0:T(8,128)(2,1)} %down_mine.3) | copy-start | bytes 7077892
  171.4 7.1 %copy-start.4 = (bf16[1024,768]{1,0:T(8,128)(2,1)S(1)}, bf16[1024,768]{1,0:T(8,128)(2,1)}, u32[]{:S(2)}) copy-start(bf16[1024,768]{1,0:T(8,128)(2,1)} %get-tuple-element.39.mix_mine) | copy-start | bytes 4718596
  171.4 7.1 %copy-start.5 = (bf16[1024,768]{1,0:T(8,128)(2,1)S(1)}, bf16[1024,768]{1,0:T(8,128)(2,1)}, u32[]{:S(2)}) copy-start(bf16[1024,768]{1,0:T(8,128)(2,1)} %get-tuple-element.40.mix_theirs) | copy-start | bytes 4718596
  185.0 13.6 %collective-permute-start.10 = (bf16[256,768]{1,0:T(8,128)(2,1)}, bf16[256,768]{1,0:T(8,128)(2,1)}, u32[]{:S(2)}, u32[]{:S(2)}) collective-permute-start(bf16[256,768]{1,0:T(8,128)(2,1)} %get-tuple-element.42), channel_id=1, source_target_pairs={{0,1},{1,0},{2,3},{3,2},{4,5},{5,4},{6,7},{7,6},{8,9},{9,8},{10,11... | collective-permute-start | bytes 1179656 | tf_op jit(solution)/shard_map/ppermute | solution.py:393
  191.5 13.9 %collective-permute-start.11 = (bf16[256,768]{1,0:T(8,128)(2,1)S(1)}, bf16[256,768]{1,0:T(8,128)(2,1)S(1)}, u32[]{:S(2)}, u32[]{:S(2)}) collective-permute-start(bf16[256,768]{1,0:T(8,128)(2,1)S(1)} %get-tuple-element.44), channel_id=1, source_target_pairs={{0,1},{1,0},{2,3},{3,2},{4,5},{5,4},{6,7},{7,6},{8,9},{9,8},{10,11... | collective-permute-start | bytes 1179656 | tf_op jit(solution)/shard_map/ppermute | solution.py:393
  199.6 5.8 %copy-start.13 = (bf16[1024,768]{1,0:T(8,128)(2,1)}, bf16[1024,768]{1,0:T(8,128)(2,1)S(1)}, u32[]{:S(2)}) copy-start(bf16[1024,768]{1,0:T(8,128)(2,1)S(1)} %constant_dynamic-update-slice_fusion.1) | copy-start | bytes 4718596

commit v2 on v1

v2 whole, which is shorter than its diff:
```python
import functools
import math

import jax
import jax.numpy as jnp
import ml_dtypes
import numpy as np
from jax import lax
from jax.experimental import pallas as pl
from jax.experimental.pallas import tpu as pltpu
from jax.sharding import PartitionSpec as P

D = 1536
NB = 4
PBLK = 256
QBLK = 512
LANES = 128
F32 = jnp.float32
BF16 = jnp.bfloat16
VMEM_LIMIT = 56 * 1024 * 1024
SMALL_LIMIT = 32 * 1024 * 1024
CONV_LIMIT = 40 * 1024 * 1024


def dft_numpy(length):
    index = np.arange(length, dtype=np.int64)
    angle = (index[:, None] * index[None, :] % length).astype(np.float32)
    angle = angle * np.float32(2.0 * math.pi / length)
    return (
        np.cos(angle).astype(ml_dtypes.bfloat16).astype(np.float32),
        np.sin(angle).astype(ml_dtypes.bfloat16).astype(np.float32),
    )


def make_tables(groups):
    low = QBLK // groups
    order = (np.arange(groups)[None, :] * low + np.arange(low)[:, None]).reshape(-1)
    cos_long, sin_long = dft_numpy(QBLK)
    cos_long, sin_long = cos_long[order][:, order], sin_long[order][:, order]
    cos_short, sin_short = dft_numpy(PBLK)
    second = np.block([[cos_short, -sin_short], [sin_short, cos_short]])
    third = np.block([[cos_short, sin_short], [-sin_short, cos_short]])
    seq_len = PBLK * QBLK
    angle = (order[:, None].astype(np.int64) * np.arange(PBLK)[None, :] % seq_len).astype(np.float32)
    angle = angle * np.float32(2.0 * math.pi / seq_len)
    half = [t.astype(ml_dtypes.bfloat16) for t in (cos_long, -sin_long, second, third)]
    return half + [np.cos(angle).astype(np.float32), np.sin(angle).astype(np.float32)]


def pair_split(pairs):
    table = np.zeros((2 * pairs, 2 * pairs), np.float32)
    for e in range(2):
        for d in range(pairs):
            table[e * pairs + d, 2 * d + e] = 1.0
    return table.astype(ml_dtypes.bfloat16)


def nt_dot(left, right):
    return lax.dot_general(left, right, (((1,), (1,)), ((), ())), preferred_element_type=F32)


def pack_kernel(tokens_ref, spectrum_ref, split_ref, out_ref, wide):
    split = split_ref[...]
    count = split.shape[0] // 2
    for low in range(4):
        turned = nt_dot(split, tokens_ref[low * 256 : (low + 1) * 256, :])
        for e in range(2):
            for half in range(2):
                wide[e * 8 + half * 4 + low] = turned[
                    e * count : (e + 1) * count, half * LANES : (half + 1) * LANES
                ]
    row = lax.broadcasted_iota(jnp.int32, (count, LANES), 0)
    pick = (row == lax.broadcasted_iota(jnp.int32, (count, LANES), 1)).astype(F32).astype(BF16)
    for part in range(2):
        for low in range(4):
            turned = nt_dot(pick, spectrum_ref[part, low])
            for half in range(2):
                wide[16 + part * 8 + half * 4 + low] = turned[:, half * LANES : (half + 1) * LANES]
    out_ref[...] = jnp.swapaxes(wide[...], 0, 1).astype(BF16)


def pack(tokens, spectrum):
    count = LANES
    return pl.pallas_call(
        pack_kernel,
        grid=(3,),
        in_specs=[
            pl.BlockSpec((1024, 2 * LANES), lambda i: (0, i)),
            pl.BlockSpec((2, 4, 256, LANES), lambda i: (0, 0, 0, i)),
            pl.BlockSpec((2 * LANES, 2 * LANES), lambda i: (0, 0)),
        ],
        out_specs=pl.BlockSpec((count, 32, LANES), lambda i: (0, i, 0)),
        out_shape=jax.ShapeDtypeStruct((LANES, 96, LANES), BF16),
        scratch_shapes=[pltpu.VMEM((32, count, LANES), F32)],
        compiler_params=pltpu.CompilerParams(vmem_limit_bytes=VMEM_LIMIT),
        cost_estimate=pl.CostEstimate(flops=2 * 10**9, bytes_accessed=6 * 2**20, transcendentals=0),
        name="pack",
    )(tokens, spectrum, pair_split(count))


def conv_kernel(data_hbm, *rest):
    sources, (out_hbm, data, wide, back, outs, sems, table_sems, out_sems), tables = rest[:6], rest[6:14], rest[14:]
    cos_long_ref, sin_long_ref, second_ref, third_ref, cos_ref, sin_ref, staged = tables

    def fetch(slot):
        rows = pl.ds(pl.multiple_of(slot * 32, 32), 32)
        return pltpu.make_async_copy(data_hbm.at[:, rows, :], data.at[slot], sems.at[slot])

    loads = [pltpu.make_async_copy(sources[i], tables[i], table_sems.at[i]) for i in range(6)]
    fetch(0).start()
    for i in (0, 1, 4, 5, 2, 3):
        loads[i].start()
    fetch(1).start()
    fetch(2).start()

    def filters(part):
        return jnp.concatenate(
            [
                jnp.concatenate([wide[16 + part * 8 + half * 4 + low] for half in range(2)], axis=1)
                for low in range(4)
            ],
            axis=0,
        )

    @pl.loop(0, 3)
    def _(slot):
        fetch(slot).wait()
        for part in range(4):
            at = slice(part * 32, (part + 1) * 32)
            wide[:, at, :] = jnp.swapaxes(data[slot, at].astype(F32), 0, 1)

        @pl.when(slot == 0)
        def _():
            for load in loads:
                load.wait()

        channels = range(2)
        blocks = [
            jnp.concatenate(
                [
                    jnp.concatenate([wide[e * 8 + half * 4 + low] for half in range(2)], axis=1).astype(BF16)
                    for low in range(4)
                ],
                axis=0,
            )
            for e in channels
        ]
        turn_cos, turn_sin = cos_ref[...], sin_ref[...]
        first_real = [jnp.dot(cos_long_ref[...], block, preferred_element_type=F32) for block in blocks]
        first_imag = [jnp.dot(sin_long_ref[...], block, preferred_element_type=F32) for block in blocks]
        turned = [
            jnp.concatenate(
                [
                    (first_real[e] * turn_cos + first_imag[e] * turn_sin).astype(BF16),
                    (first_imag[e] * turn_cos - first_real[e] * turn_sin).astype(BF16),
                ],
                axis=1,
            )
            for e in channels
        ]
        spectral = [jnp.dot(turned[e], second_ref[...], preferred_element_type=F32) for e in channels]
        filter_real, filter_imag = filters(0), filters(1)
        filtered = [
            jnp.concatenate(
                [
                    (spectral[e][:, :PBLK] * filter_real - spectral[e][:, PBLK:] * filter_imag).astype(BF16),
                    (spectral[e][:, :PBLK] * filter_imag + spectral[e][:, PBLK:] * filter_real).astype(BF16),
                ],
                axis=1,
            )
            for e in channels
        ]
        third = [jnp.dot(filtered[e], third_ref[...], preferred_element_type=F32) for e in channels]
        for e in channels:
            back_real, back_imag = third[e][:, :PBLK], third[e][:, PBLK:]
            back[e, 0] = (back_real * turn_cos - back_imag * turn_sin).astype(BF16)
            back[e, 1] = (back_real * turn_sin + back_imag * turn_cos).astype(BF16)
        for e in channels:
            conv = jnp.dot(cos_long_ref[...], back[e, 0], preferred_element_type=F32)
            conv = conv + jnp.dot(sin_long_ref[...], back[e, 1], preferred_element_type=F32)
            conv = conv * (1.0 / (PBLK * QBLK))
            for low in range(4):
                for half in range(2):
                    row = (low // 2) * 24 + ((slot * 2 + e) * 2 + half) * 2 + low % 2
                    outs[row] = conv[low * LANES : (low + 1) * LANES, half * LANES : (half + 1) * LANES]

    stores = []
    for part in range(4):
        at = slice(part * 32, (part + 1) * 32)
        staged[at] = jnp.swapaxes(outs[:, at, :], 0, 1).astype(BF16)
        stores.append(pltpu.make_async_copy(staged.at[at], out_hbm.at[at], out_sems.at[part]))
        stores[-1].start()
    for store in stores:
        store.wait()


def convolve(data, tables):
    in_hbm = lambda x: pltpu.with_memory_space_constraint(x, pltpu.HBM)
    return pl.pallas_call(
        conv_kernel,
        in_specs=[pl.BlockSpec(memory_space=pltpu.HBM)] * (1 + len(tables)),
        out_specs=pl.BlockSpec(memory_space=pltpu.HBM),
        out_shape=pltpu.HBM((LANES, 48, LANES), BF16),
        scratch_shapes=[
            pltpu.VMEM((3, LANES, 32, LANES), BF16),
            pltpu.VMEM((32, LANES, LANES), F32),
            pltpu.VMEM((2, 2, QBLK, PBLK), BF16),
            pltpu.VMEM((48, LANES, LANES), F32),
            pltpu.SemaphoreType.DMA((3,)),
            pltpu.SemaphoreType.DMA((6,)),
            pltpu.SemaphoreType.DMA((4,)),
        ]
        + [pltpu.VMEM(t.shape, t.dtype) for t in tables]
        + [pltpu.VMEM((LANES, 48, LANES), BF16)],
        compiler_params=pltpu.CompilerParams(vmem_limit_bytes=CONV_LIMIT),
        cost_estimate=pl.CostEstimate(flops=64 * 10**8, bytes_accessed=8 * 2**20, transcendentals=0),
        name="convolve",
    )(*(in_hbm(x) for x in (data, *tables))).reshape(LANES * 48, LANES)


def hidden_kernel(
    side_ref, scales_ref, split_ref, mix_mine, mix_theirs, conv_hbm, mine_hbm, theirs_hbm,
    hidden_ref, shuffled_ref, conv_ref, tokens_ref, mix_ref, wide, normed, sems, conv_sems,
):
    side = side_ref[0]
    width = hidden_ref.shape[2]
    count = hidden_ref.shape[1]
    start = pl.multiple_of(side * count, count)
    quarter = conv_hbm.shape[0] // 4
    arrivals = []
    for part in range(4):
        at = slice(part * quarter, (part + 1) * quarter)
        arrivals.append(pltpu.make_async_copy(conv_hbm.at[at], conv_ref.at[at], conv_sems.at[part]))
        arrivals[-1].start()
    copies = [
        pltpu.make_async_copy(mine_hbm.at[pl.ds(start, count)], tokens_ref.at[0], sems.at[0]),
        pltpu.make_async_copy(theirs_hbm, tokens_ref.at[1], sems.at[1]),
        pltpu.make_async_copy(mix_mine, mix_ref.at[0], sems.at[2]),
        pltpu.make_async_copy(mix_theirs, mix_ref.at[1], sems.at[3]),
    ]
    copies[0].start()
    copies[1].start()
    split = split_ref[...]
    for part in range(4):
        at = slice(part * quarter, (part + 1) * quarter)
        arrivals[part].wait()
        wide[:, at, :] = jnp.swapaxes(conv_ref[at].astype(F32), 0, 1)
    copies[2].start()
    copies[3].start()
    copies[0].wait()
    copies[1].wait()
    for block in range(count // LANES):
        low, half = block // 2, block % 2
        rows = slice(block * LANES, (block + 1) * LANES)
        total = 0.0
        for s in range(2):
            home = side if s == 0 else 1 - side
            pieces = []
            for slot in range(3):
                turned = jnp.concatenate(
                    [
                        wide[home * 24 + ((slot * 2 + e) * 2 + half) * 2 + low].T
                        for e in range(2)
                    ],
                    axis=1,
                ).astype(BF16)
                conv = jnp.dot(turned, split, preferred_element_type=F32)
                cols = slice(slot * 256, (slot + 1) * 256)
                values = tokens_ref[s, rows, cols].astype(F32)
                mixed = conv + scales_ref[s, 0:1, cols] * values
                hidden = values + mixed * jax.nn.sigmoid(values)
                hidden_ref[s, rows, cols] = hidden
                pieces.append(jnp.sum(hidden, axis=1, keepdims=True))
            total = total + (pieces[0] + pieces[1] + pieces[2])
        mean = total / (2 * width)
        first = hidden_ref[0, rows, :] - mean
        second = hidden_ref[1, rows, :] - mean
        square = jnp.sum(first * first, axis=1, keepdims=True) + jnp.sum(second * second, axis=1, keepdims=True)
        scale = lax.rsqrt(square / (2 * width) + 1e-05)
        normed[0, rows, :] = (first * scale * scales_ref[0, 1:2, :]).astype(BF16)
        normed[1, rows, :] = (second * scale * scales_ref[1, 1:2, :]).astype(BF16)
    for s in range(2):
        copies[2 + s].wait()
        shuffled_ref[s] = jnp.dot(normed[s], mix_ref[s], preferred_element_type=F32).astype(BF16)


def make_hidden(side, conv, mine, theirs, scales, mix):
    rows = theirs.shape[0]
    conv = conv.reshape(LANES, 48, LANES)
    return pl.pallas_call(
        hidden_kernel,
        in_specs=[pl.BlockSpec(memory_space=pltpu.SMEM)]
        + [pl.BlockSpec(memory_space=pltpu.VMEM)] * 2
        + [pl.BlockSpec(memory_space=pltpu.HBM)] * 5,
        out_shape=[
            jax.ShapeDtypeStruct((2, rows, 768), F32),
            jax.ShapeDtypeStruct((2, rows, 1024), BF16),
        ],
        scratch_shapes=[
            pltpu.VMEM(conv.shape, BF16),
            pltpu.VMEM((2, rows, 768), BF16),
            pltpu.VMEM((2, *mix[0].shape), BF16),
            pltpu.VMEM((48, LANES, LANES), F32),
            pltpu.VMEM((2, rows, 768), BF16),
            pltpu.SemaphoreType.DMA((4,)),
            pltpu.SemaphoreType.DMA((4,)),
        ],
        compiler_params=pltpu.CompilerParams(vmem_limit_bytes=SMALL_LIMIT),
        cost_estimate=pl.CostEstimate(flops=3 * 10**9, bytes_accessed=12 * 2**20, transcendentals=10**6),
        name="hidden",
    )(
        side,
        scales,
        pair_split(LANES),
        *(pltpu.with_memory_space_constraint(x, pltpu.HBM) for x in (*mix, conv, mine, theirs)),
    )


def mlp_kernel(
    first_row, side_ref, hidden_ref, shuffled_ref, up_mine, up_theirs, down_mine, down_theirs, mix_mine, mix_theirs,
    keep_ref, send_ref, down_buf, gathered,
):
    side = side_ref[0]
    rows = slice(first_row, first_row + keep_ref.shape[0])
    for group, (up_ref, down_ref) in enumerate(((up_mine, down_mine), (up_theirs, down_theirs))):
        home = side if group == 0 else 1 - side
        for c in range(2):
            lanes = pl.multiple_of((2 * home + c) * 256, 256)
            total = 0.0
            for s in range(2):
                start = pl.multiple_of((side if s == 0 else 1 - side) * 192, 192)
                mixed = shuffled_ref[s, rows, pl.ds(lanes, 256)][:, :192]
                total = total + jnp.dot(mixed, up_ref[c, pl.ds(start, 192), :], preferred_element_type=F32)
            active = jax.nn.gelu(total, approximate=True).astype(BF16)
            down_buf[...] = jnp.dot(active, down_ref[c], preferred_element_type=F32).astype(BF16)
            for s in range(2):
                start = pl.multiple_of((side if s == 0 else 1 - side) * LANES, LANES)
                gathered[s, :, pl.ds(lanes, 256)] = down_buf[:, pl.ds(start, 256)]
    for s, (ref, mix_ref) in enumerate(((keep_ref, mix_mine), (send_ref, mix_theirs))):
        outcome = jnp.dot(gathered[s], mix_ref[...], preferred_element_type=F32)
        ref[...] = (hidden_ref[s, rows, :] + outcome).astype(BF16)


def mlp(side, hidden, shuffled, ups, downs, mix, first_row, rows):
    return pl.pallas_call(
        functools.partial(mlp_kernel, first_row),
        in_specs=[pl.BlockSpec(memory_space=pltpu.SMEM)] + [pl.BlockSpec(memory_space=pltpu.VMEM)] * 8,
        out_shape=[jax.ShapeDtypeStruct((rows, 768), BF16)] * 2,
        scratch_shapes=[pltpu.VMEM((rows, 384), BF16), pltpu.VMEM((2, rows, 1024), BF16)],
        compiler_params=pltpu.CompilerParams(vmem_limit_bytes=SMALL_LIMIT),
        cost_estimate=pl.CostEstimate(
            flops=rows * 14 * 10**6, bytes_accessed=14 * 2**20, transcendentals=rows * 6144
        ),
        name="mlp",
    )(side, hidden, shuffled, *ups, *downs, *mix)


def choose(place_ref, want, got, passed, target, sem, begin):
    for core, source in ((want, got), (1 - want, passed)):
        @pl.when(place_ref[1] == core)
        def _():
            copy = pltpu.make_async_copy(source, target, sem)
            copy.start() if begin else copy.wait()


def places(shape, axis, offset, piece):
    row = lax.broadcasted_iota(jnp.int32, shape, axis)
    group = sum((row >= c * piece).astype(jnp.int32) for c in range(1, NB))
    target = lax.broadcasted_iota(jnp.int32, shape, 1 - axis)
    return (target == row + group * (256 - piece) + offset).astype(F32).astype(BF16)


def rearrange(home, b, weight_in, weight_out, first_ref, last_ref):
    inner = weight_in.shape[0]
    piece = inner // NB
    picked = jnp.dot(weight_in, places((inner, NB * 256), 0, b * piece, piece), preferred_element_type=F32)
    first_ref[b * inner : (b + 1) * inner, :] = picked.astype(BF16)
    offset = b * piece + jnp.where(home == 0, 0, 256 - 2 * piece)
    picked = jnp.dot(places((NB * 256, inner), 1, offset, piece), weight_out, preferred_element_type=F32)
    last_ref[:, b * inner : (b + 1) * inner] = picked.astype(BF16)


def prepare_mine_kernel(place_ref, in_ref, out_ref, first_ref, last_ref):
    for b in range(in_ref.shape[0]):
        rearrange(place_ref[0], b, in_ref[b], out_ref[b], first_ref, last_ref)


def prepare_theirs_kernel(
    place_ref, in_got, in_passed, out_got, out_passed, up_got, up_passed, down_got, down_passed,
    first_ref, last_ref, up_theirs, down_theirs, in_ref, out_ref, up_ref, down_ref, sems,
):
    picks = [
        (0, in_got, in_passed, in_ref, sems.at[0]),
        (1, out_got, out_passed, out_ref, sems.at[1]),
        (0, up_got, up_passed, up_ref, sems.at[2]),
        (1, down_got, down_passed, down_ref, sems.at[3]),
    ]
    for pick in picks:
        choose(place_ref, *pick, True)
    choose(place_ref, *picks[0], False)
    choose(place_ref, *picks[1], False)
    for b in range(in_ref.shape[0]):
        rearrange(1 - place_ref[0], b, in_ref[b], out_ref[b], first_ref, last_ref)
    choose(place_ref, *picks[2], False)
    choose(place_ref, *picks[3], False)
    stores = [
        pltpu.make_async_copy(up_ref, up_theirs, sems.at[4]),
        pltpu.make_async_copy(down_ref, down_theirs, sems.at[5]),
    ]
    for store in stores:
        store.start()
    for store in stores:
        store.wait()


def prepare_shapes(blocks, inner):
    return [
        jax.ShapeDtypeStruct((blocks * inner, NB * 256), BF16),
        jax.ShapeDtypeStruct((NB * 256, blocks * inner), BF16),
    ]


def prepare_mine(place, mix_in, mix_out):
    return pl.pallas_call(
        prepare_mine_kernel,
        in_specs=[pl.BlockSpec(memory_space=pltpu.SMEM)] + [pl.BlockSpec(memory_space=pltpu.VMEM)] * 2,
        out_specs=[pl.BlockSpec(memory_space=pltpu.VMEM)] * 2,
        out_shape=prepare_shapes(mix_in.shape[0], mix_in.shape[1]),
        compiler_params=pltpu.CompilerParams(vmem_limit_bytes=SMALL_LIMIT),
        cost_estimate=pl.CostEstimate(flops=10**9, bytes_accessed=2**20, transcendentals=0),
        name="prepare_mine",
    )(place, mix_in, mix_out)


def prepare_theirs(place, pairs):
    mix_in, mix_out = pairs[0][0], pairs[1][0]
    arrays = [x for pair in pairs for x in pair]
    return pl.pallas_call(
        prepare_theirs_kernel,
        in_specs=[pl.BlockSpec(memory_space=pltpu.SMEM)] + [pl.BlockSpec(memory_space=pltpu.HBM)] * len(arrays),
        out_specs=[pl.BlockSpec(memory_space=pltpu.VMEM)] * 2 + [pl.BlockSpec(memory_space=pltpu.HBM)] * 2,
        out_shape=prepare_shapes(mix_in.shape[0], mix_in.shape[1])
        + [pltpu.HBM(pair[0].shape, BF16) for pair in pairs[2:]],
        scratch_shapes=[
            pltpu.VMEM(mix_in.shape, BF16),
            pltpu.VMEM(mix_out.shape, BF16),
            pltpu.VMEM(pairs[2][0].shape, BF16),
            pltpu.VMEM(pairs[3][0].shape, BF16),
            pltpu.SemaphoreType.DMA((6,)),
        ],
        compiler_params=pltpu.CompilerParams(vmem_limit_bytes=VMEM_LIMIT),
        cost_estimate=pl.CostEstimate(flops=10**6, bytes_accessed=2**16, transcendentals=0),
        name="prepare_theirs",
    )(place, *(pltpu.with_memory_space_constraint(x, pltpu.HBM) for x in arrays))


def make_per_device(chunks):
    def per_device(tokens, spectrum, skip, gain, mix_in, w_up, w_down, mix_out):
        groups = lax.axis_size("seq")
        both = ("seq", "ch")
        side = lax.axis_index("ch")
        core = lax.axis_index("seq") % 2
        swap = [(0, 1), (1, 0)]
        step = groups // 2

        def near(which):
            return [
                (s * 2 + h, (s ^ step) * 2 + 1 - h) for h in range(2) for s in range(groups) if s % 2 == which
            ]

        def across(which):
            return [(s, s ^ 1) for s in range(groups) if s % 2 == which]

        count = tokens.shape[0] // 2
        place = jnp.stack([side, core]).astype(jnp.int32)
        packed = pack(tokens, spectrum)
        data = lax.all_to_all(packed, "seq", split_axis=0, concat_axis=0, tiled=True)

        weights, cores = (w_up, w_down, mix_in, mix_out), (0, 1, 0, 1)
        got = [lax.ppermute(w, both, near(which)) for w, which in zip(weights, cores)]
        theirs = lax.ppermute(lax.dynamic_slice_in_dim(tokens, (1 - side) * count, count, axis=0), "ch", swap)
        scales_mine = jnp.stack([skip, gain])
        scales = jnp.stack([scales_mine, lax.ppermute(scales_mine, "ch", swap)])
        first_mine, last_mine = prepare_mine(place, mix_in, mix_out)
        tables = [jnp.asarray(t) for t in make_tables(groups)]
        data, first_mine, last_mine, theirs, scales, tables = lax.optimization_barrier(
            (data, first_mine, last_mine, theirs, scales, tables)
        )
        conv = convolve(data, tables)

        conv, got = lax.optimization_barrier((conv, got))
        conv = lax.all_to_all(conv, both, split_axis=0, concat_axis=0, tiled=True)
        passed = [lax.ppermute(g, "seq", across(which)) for g, which in zip(got, cores)]
        pairs = [(got[i], passed[i]) for i in (2, 3, 0, 1)]
        first_theirs, last_theirs, up_theirs, down_theirs = prepare_theirs(place, pairs)
        mix_first = (first_mine, first_theirs)
        mix_last = (last_mine, last_theirs)
        hidden, shuffled = make_hidden(place, conv, tokens, theirs, scales, mix_first)
        out = jnp.zeros(tokens.shape, tokens.dtype)
        rows = count // chunks
        for q in range(chunks):
            keep, send = mlp(
                place, hidden, shuffled, (w_up, up_theirs), (w_down, down_theirs), mix_last, q * rows, rows
            )
            sent = lax.ppermute(send, "ch", swap)
            out = lax.dynamic_update_slice_in_dim(out, keep, side * count + q * rows, axis=0)
            out = lax.dynamic_update_slice_in_dim(out, sent, (1 - side) * count + q * rows, axis=0)
        return out

    return per_device


def solution(mesh):
    return jax.shard_map(
        make_per_device(2),
        mesh=mesh,
        in_specs=(
            P("seq", "ch"),
            P(None, "seq", None, "ch"),
            P("ch"),
            P("ch"),
            P("ch", None, None),
            P("ch", None, None),
            P("ch", None, None),
            P("ch", None, None),
        ),
        out_specs=P("seq", "ch"),
        check_vma=False,
    )
```

time: 207 us -> 196 us (0.947)
  other arithmetic: 6.66 us -> 1.38 us
  Pallas kernels: 52.5 us -> 47.3 us
    select_n x2 -> x0, other arithmetic: 5.33 us -> none  [per_device(): jnp.where(core == cores[i], got[i], passed[i])]
    pallas_call x6, Pallas kernels: 45.5 us -> 40.5 us  [the longest x1 12.5 us: convolve(): pl.pallas_call(conv_kernel, in_specs=[pl.BlockSpec(memory_space=pltpu.HBM...]
    all_to_all x1, waiting for transfers between devices: 21.1 us -> 18.4 us  [per_device(): conv = lax.all_to_all(conv, both, split_axis=0, concat_axis=0, tiled=True)]
    ppermute x4, waiting for transfers between devices: 0.01 us -> 2.08 us  [per_device(): lax.ppermute(w, both, near(which))]
    unnamed x36 -> x44, local copies, waits for them, and re-layouts: 6.22 us -> 6.91 us
  transfers between devices with their start and end apart: 14 -> 14, of which waited for: 7 -> 8; matrix products, arithmetic and copies ran while one was open for 5% -> 2% of each run, Pallas kernels for 15% -> 15%
where the time goes in v2:
time: 196 us
  waiting for transfers between devices  80.7 us (41%)
  starting transfers between devices  54.9 us (28%)
  Pallas kernels  47.3 us (24%)
  local copies, waits for them, and re-layouts  11 us (6%)
    all_to_all x1, waiting for transfers between devices, per_device(): lax.all_to_all(packed, 'seq', split_axis=0, concat_axis=0, tiled=True)  24.2 us
    ppermute x1, waiting for transfers between devices, per_device(): scales = jnp.stack([scales_mine, lax.ppermute(scales_mine, 'ch', swap)])  23.6 us
    all_to_all x1, waiting for transfers between devices, per_device(): conv = lax.all_to_all(conv, both, split_axis=0, concat_axis=0, tiled=True)  18.4 us
    all_to_all x1, starting transfers between devices, per_device(): lax.all_to_all(packed, 'seq', split_axis=0, concat_axis=0, tiled=True)  14.4 us
    all_to_all x1, starting transfers between devices, per_device(): conv = lax.all_to_all(conv, both, split_axis=0, concat_axis=0, tiled=True)  14.3 us
    pallas_call x1, Pallas kernels, convolve(): pl.pallas_call(conv_kernel, in_specs=[pl.BlockSpec(memory_space=pltpu.HBM...  12.5 us
    pallas_call x2, Pallas kernels, mlp(): pl.pallas_call(functools.partial(mlp_kernel, first_row), in_specs=[pl.Blo...  12.2 us
    ppermute x4, starting transfers between devices, per_device(): lax.ppermute(w, both, near(which))  10.7 us
  transfers between devices with their start and end apart: 14, of which 8 were waited for; matrix products, arithmetic and copies ran while one was open for 2% of the time, Pallas kernels for 15%

profile of v2, /device:TPU:8, one launch (start us, length us, event | category | flops | bytes accessed | tf_op | source)
XLA Modules:
  0.0 195.6 jit_solution(5002616108967041121)
XLA Ops:
  0.0 5.5 %pack.1 = bf16[128,96,128]{2,1,0:T(8,128)(2,1)} custom-call(bf16[1024,768]{1,0:T(8,128)(2,1)} %mine_hbm.1, bf16[2,4,256,384]{3,2,1,0:T(8,128)(2,1)} %spectrum_ref.1, bf16[256,256]{1,0:T(8,128)(2,1)} %constant.48.clone.split_ref), custom_call_target="tpu_custom_call" | custom-call | flops 2000000000 | bytes 6291456 | tf_op jit(solution)/shard_map/pack/pallas_call | solution.py:84
  5.5 14.4 %all-to-all-start = ((bf16[128,96,128]{2,1,0:T(8,128)(2,1)}), bf16[128,96,128]{2,1,0:T(8,128)(2,1)}, u32[]{:S(2)}, u32[]{:S(2)}) async-start(bf16[128,96,128]{2,1,0:T(8,128)(2,1)} %pack.1), calls=%async_computation | async-start | bytes 6291456 | tf_op jit(solution)/shard_map/all_to_all | solution.py:477
  19.9 5.2 %collective-permute-start.2 = (bf16[2,384,1536]{2,1,0:T(8,128)(2,1)S(1)}, bf16[2,384,1536]{2,1,0:T(8,128)(2,1)}, u32[]{:S(2)}, u32[]{:S(2)}) collective-permute-start(bf16[2,384,1536]{2,1,0:T(8,128)(2,1)S(1)} %copy-done), channel_id=1, source_target_pairs={{0,129},{4,133},{8,137},{12,141},{16,145},{20,149},{24,153},{28,15... | collective-permute-start | bytes 7077896 | tf_op jit(solution)/shard_map/ppermute | solution.py:480
  25.1 2.0 %collective-permute-start.3 = (bf16[2,1536,384]{2,1,0:T(8,128)(2,1)}, bf16[2,1536,384]{2,1,0:T(8,128)(2,1)}, u32[]{:S(2)}, u32[]{:S(2)}) collective-permute-start(bf16[2,1536,384]{2,1,0:T(8,128)(2,1)} %down_mine.3), channel_id=1, source_target_pairs={{2,131},{6,135},{10,139},{14,143},{18,147},{22,151},{26,155},{30,1... | collective-permute-start | bytes 7077896 | tf_op jit(solution)/shard_map/ppermute | solution.py:480
  27.1 2.1 %constant_dynamic-slice_fusion = bf16[512,768]{1,0:T(8,128)(2,1)} fusion(bf16[1024,768]{1,0:T(8,128)(2,1)} %mine_hbm.1, s32[]{:T(128)S(6)} %select_n.21), kind=kLoop, calls=%fused_computation.6 | loop fusion | bytes 1572868 | tf_op jit(solution)/shard_map/dynamic_slice | solution.py:481
  30.6 2.7 %collective-permute-start.1 = (f32[2,768]{1,0:T(2,128)}, f32[2,768]{1,0:T(2,128)S(1)}, u32[]{:S(2)}, u32[]{:S(2)}) collective-permute-start(f32[2,768]{1,0:T(2,128)} %get-tuple-element.62), channel_id=1, source_target_pairs={{0,1},{1,0},{2,3},{3,2},{4,5},{5,4},{6,7},{7,6},{8,9},{9,8},{10,11... | collective-permute-start | bytes 18440 | tf_op jit(solution)/shard_map/ppermute | solution.py:483
  33.3 2.0 %collective-permute-start.4 = (bf16[2,384,384]{2,1,0:T(8,128)(2,1)S(1)}, bf16[2,384,384]{2,1,0:T(8,128)(2,1)S(1)}, u32[]{:S(2)}, u32[]{:S(2)}) collective-permute-start(bf16[2,384,384]{2,1,0:T(8,128)(2,1)S(1)} %copy-done.9), channel_id=1, source_target_pairs={{0,129},{4,133},{8,137},{12,141},{16,145},{20,149},{24,153},{28,15... | collective-permute-start | bytes 1769480 | tf_op jit(solution)/shard_map/ppermute | solution.py:480
  35.4 2.8 %prepare_mine.1 = (bf16[768,1024]{1,0:T(8,128)(2,1)S(1)}, bf16[1024,768]{1,0:T(8,128)(2,1)S(1)}) custom-call(s32[2]{0:T(128)S(1)} %pad_add_fusion.place_ref.side_ref, bf16[2,384,384]{2,1,0:T(8,128)(2,1)S(1)} %copy-done.9, bf16[2,384,384]{2,1,0:T(8,128)(2,1)} %out_ref.1), custom_call_target="tpu_custom_call" | custom-call | flops 1000000000 | bytes 1048576 | tf_op jit(solution)/shard_map/prepare_mine/pallas_call | solution.py:424
  38.3 1.1 copy-done.4
  39.4 1.1 copy-done.11
  40.6 23.6 %collective-permute-done.1 = f32[2,768]{1,0:T(2,128)S(1)} collective-permute-done((f32[2,768]{1,0:T(2,128)}, f32[2,768]{1,0:T(2,128)S(1)}, u32[]{:S(2)}, u32[]{:S(2)}) %collective-permute-start.1) | collective-permute-done | bytes 6176 | tf_op jit(solution)/shard_map/ppermute | solution.py:483
  64.1 1.5 collective-permute-start.5
  66.3 24.2 %all-to-all-done.data_hbm = bf16[128,96,128]{2,1,0:T(8,128)(2,1)} async-done(((bf16[128,96,128]{2,1,0:T(8,128)(2,1)}), bf16[128,96,128]{2,1,0:T(8,128)(2,1)}, u32[]{:S(2)}, u32[]{:S(2)}) %all-to-all-start) | async-done | bytes 3145760 | tf_op jit(solution)/shard_map/all_to_all | solution.py:477
  90.5 12.5 %convolve.1 = bf16[128,48,128]{2,1,0:T(8,128)(2,1)} custom-call(bf16[128,96,128]{2,1,0:T(8,128)(2,1)} %all-to-all-done.data_hbm, bf16[512,512]{1,0:T(8,128)(2,1)} %constant.49.clone.rest_0_, bf16[512,512]{1,0:T(8,128)(2,1)} %constant.50.clone.rest_1_, bf16[512,512]{1,0:T(8,128)(2,1)} %constant.51.clone.rest_2_, bf16[512,512]{1,0:T(8,128)(2,1)} %constant.52.clone.rest_3_, ...), custom_call_target="tpu_custom_call" | custom-call | flops 6400000000 | bytes 8388608 | tf_op jit(solution)/shard_map/convolve/pallas_call | solution.py:199
  103.0 2.1 %collective-permute-done.4.in_got = bf16[2,384,384]{2,1,0:T(8,128)(2,1)S(1)} collective-permute-done((bf16[2,384,384]{2,1,0:T(8,128)(2,1)S(1)}, bf16[2,384,384]{2,1,0:T(8,128)(2,1)S(1)}, u32[]{:S(2)}, u32[]{:S(2)}) %collective-permute-start.4) | collective-permute-done | bytes 589856 | tf_op jit(solution)/shard_map/ppermute | solution.py:480
  105.9 14.3 %all-to-all-start.1 = ((bf16[256,24,128]{2,1,0:T(8,128)(2,1)}), bf16[256,24,128]{2,1,0:T(8,128)(2,1)}, u32[]{:S(2)}, u32[]{:S(2)}) async-start(bf16[256,24,128]{2,1,0:T(8,128)(2,1)} %bitcast.8), calls=%async_computation.1 | async-start | bytes 3145728 | tf_op jit(solution)/shard_map/all_to_all | solution.py:492
  120.3 2.3 %collective-permute-start.8 = (bf16[2,384,1536]{2,1,0:T(8,128)(2,1)}, bf16[2,384,1536]{2,1,0:T(8,128)(2,1)S(1)}, u32[]{:S(2)}, u32[]{:S(2)}) collective-permute-start(bf16[2,384,1536]{2,1,0:T(8,128)(2,1)} %collective-permute-done.2.up_got), channel_id=1, source_target_pairs={{0,2},{4,6},{8,10},{12,14},{16,18},{20,22},{24,26},{28,30},{32,34}... | collective-permute-start | bytes 7077896 | tf_op jit(solution)/shard_map/ppermute | solution.py:493
  122.6 1.3 collective-permute-start.9
  123.9 3.2 %collective-permute-start.6 = (bf16[2,384,384]{2,1,0:T(8,128)(2,1)}, bf16[2,384,384]{2,1,0:T(8,128)(2,1)S(1)}, u32[]{:S(2)}, u32[]{:S(2)}) collective-permute-start(bf16[2,384,384]{2,1,0:T(8,128)(2,1)} %copy-done.15), channel_id=1, source_target_pairs={{0,2},{4,6},{8,10},{12,14},{16,18},{20,22},{24,26},{28,30},{32,34}... | collective-permute-start | bytes 1769480 | tf_op jit(solution)/shard_map/ppermute | solution.py:493
  127.1 1.5 collective-permute-start.7
  128.9 2.3 %collective-permute-done.7.out_passed = bf16[2,384,384]{2,1,0:T(8,128)(2,1)S(1)} collective-permute-done((bf16[2,384,384]{2,1,0:T(8,128)(2,1)}, bf16[2,384,384]{2,1,0:T(8,128)(2,1)S(1)}, u32[]{:S(2)}, u32[]{:S(2)}) %collective-permute-start.7) | collective-permute-done | bytes 589856 | tf_op jit(solution)/shard_map/ppermute | solution.py:493
  132.1 1.5 copy-done.12
  133.6 1.4 copy-done.13
  135.0 7.5 %prepare_theirs.1 = (bf16[768,1024]{1,0:T(8,128)(2,1)}, bf16[1024,768]{1,0:T(8,128)(2,1)}, bf16[2,384,1536]{2,1,0:T(8,128)(2,1)}, bf16[2,1536,384]{2,1,0:T(8,128)(2,1)}) custom-call(s32[2]{0:T(128)} %copy-done.7, bf16[2,384,384]{2,1,0:T(8,128)(2,1)} %copy-done.15, bf16[2,384,384]{2,1,0:T(8,128)(2,1)} %copy-done.16, ...), custom_call_target="tpu_custom_call" | custom-call | flops 1000000 | bytes 65536 | tf_op jit(solution)/shard_map/prepare_theirs/pallas_call | solution.py:438
  142.6 18.4 %all-to-all-done.1 = bf16[256,24,128]{2,1,0:T(8,128)(2,1)} async-done(((bf16[256,24,128]{2,1,0:T(8,128)(2,1)}), bf16[256,24,128]{2,1,0:T(8,128)(2,1)}, u32[]{:S(2)}, u32[]{:S(2)}) %all-to-all-start.1) | async-done | bytes 1572896 | tf_op jit(solution)/shard_map/all_to_all | solution.py:492
  161.0 6.8 %hidden.1 = (f32[2,512,768]{2,1,0:T(8,128)S(1)}, bf16[2,512,1024]{2,1,0:T(8,128)(2,1)S(1)}) custom-call(s32[2]{0:T(128)S(1)} %copy-done.8, f32[2,2,768]{2,1,0:T(2,128)S(1)} %pad_maximum_fusion.scales_ref, bf16[256,256]{1,0:T(8,128)(2,1)S(1)} %copy-done.10, bf16[768,1024]{1,0:T(8,128)(2,1)} %copy-done.11, bf16[768,1024]{1,0:T(8,128)(2,1)} %get-tuple-element.48.mix_theirs, ...), custom_call_target="tpu_custom_call" | custom-call | flops 3000000000 | bytes 12582912 | tf_op jit(solution)/shard_map/hidden/pallas_call | solution.py:290
  167.9 6.5 %mlp.2 = (bf16[256,768]{1,0:T(8,128)(2,1)S(1)}, bf16[256,768]{1,0:T(8,128)(2,1)}) custom-call(s32[2]{0:T(128)S(1)} %copy-done.8, f32[2,512,768]{2,1,0:T(8,128)S(1)} %get-tuple-element.51.hidden_ref, bf16[2,512,1024]{2,1,0:T(8,128)(2,1)S(1)} %get-tuple-element.52.shuffled_ref, bf16[2,384,1536]{2,1,0:T(8,128)(2,1)S(1)} %copy-done, ...), custom_call_target="tpu_custom_call" | custom-call | flops 3584000000 | bytes 14680064 | tf_op jit(solution)/shard_map/mlp/pallas_call | solution.py:345
  175.2 5.7 %mlp.3 = (bf16[256,768]{1,0:T(8,128)(2,1)S(1)}, bf16[256,768]{1,0:T(8,128)(2,1)S(1)}) custom-call(s32[2]{0:T(128)S(1)} %copy-done.8, f32[2,512,768]{2,1,0:T(8,128)S(1)} %get-tuple-element.51.hidden_ref, bf16[2,512,1024]{2,1,0:T(8,128)(2,1)S(1)} %get-tuple-element.52.shuffled_ref, bf16[2,384,1536]{2,1,0:T(8,128)(2,1)S(1)} %copy-done, ...), custom_call_target="tpu_custom_call" | custom-call | flops 3584000000 | bytes 14680064 | tf_op jit(solution)/shard_map/mlp/pallas_call | solution.py:345
  180.9 2.8 %collective-permute-start.11 = (bf16[256,768]{1,0:T(8,128)(2,1)S(1)}, bf16[256,768]{1,0:T(8,128)(2,1)S(1)}, u32[]{:S(2)}, u32[]{:S(2)}) collective-permute-start(bf16[256,768]{1,0:T(8,128)(2,1)S(1)} %get-tuple-element.60), channel_id=1, source_target_pairs={{0,1},{1,0},{2,3},{3,2},{4,5},{5,4},{6,7},{7,6},{8,9},{9,8},{10,11... | collective-permute-start | bytes 1179656 | tf_op jit(solution)/shard_map/ppermute | solution.py:505
  183.9 4.1 %collective-permute-done.10 = bf16[256,768]{1,0:T(8,128)(2,1)} collective-permute-done((bf16[256,768]{1,0:T(8,128)(2,1)}, bf16[256,768]{1,0:T(8,128)(2,1)}, u32[]{:S(2)}, u32[]{:S(2)}) %collective-permute-start.10) | collective-permute-done | bytes 393248 | tf_op jit(solution)/shard_map/ppermute | solution.py:505
  188.0 1.0 constant_dynamic-update-slice_fusion.2
  189.0 5.8 %collective-permute-done.11 = bf16[256,768]{1,0:T(8,128)(2,1)S(1)} collective-permute-done((bf16[256,768]{1,0:T(8,128)(2,1)S(1)}, bf16[256,768]{1,0:T(8,128)(2,1)S(1)}, u32[]{:S(2)}, u32[]{:S(2)}) %collective-permute-start.11) | collective-permute-done | bytes 393248 | tf_op jit(solution)/shard_map/ppermute | solution.py:505
  (58 shorter events, 6.0 us)
Async XLA Ops:
  5.5 14.4 %copy-start = (bf16[2,384,1536]{2,1,0:T(8,128)(2,1)S(1)}, bf16[2,384,1536]{2,1,0:T(8,128)(2,1)}, u32[]{:S(2)}) copy-start(bf16[2,384,1536]{2,1,0:T(8,128)(2,1)} %up_mine.3) | copy-start | bytes 7077892
  5.5 85.1 %all-to-all-start = ((bf16[128,96,128]{2,1,0:T(8,128)(2,1)}), bf16[128,96,128]{2,1,0:T(8,128)(2,1)}, u32[]{:S(2)}, u32[]{:S(2)}) async-start(bf16[128,96,128]{2,1,0:T(8,128)(2,1)} %pack.1), calls=%async_computation | async-start | bytes 6291456 | tf_op jit(solution)/shard_map/all_to_all | solution.py:477
  19.8 10.2 %copy-start.20 = (f32[768]{0:T(1024)S(1)}, f32[768]{0:T(1024)}, u32[]{:S(2)}) copy-start(f32[768]{0:T(1024)} %param.18) | copy-start | bytes 9220
  19.8 10.2 %copy-start.21 = (f32[768]{0:T(1024)S(1)}, f32[768]{0:T(1024)}, u32[]{:S(2)}) copy-start(f32[768]{0:T(1024)} %param.19) | copy-start | bytes 9220
  19.9 13.5 %copy-start.9 = (bf16[2,384,384]{2,1,0:T(8,128)(2,1)S(1)}, bf16[2,384,384]{2,1,0:T(8,128)(2,1)}, u32[]{:S(2)}) copy-start(bf16[2,384,384]{2,1,0:T(8,128)(2,1)} %in_ref.1) | copy-start | bytes 1769476
  19.9 85.2 %collective-permute-start.2 = (bf16[2,384,1536]{2,1,0:T(8,128)(2,1)S(1)}, bf16[2,384,1536]{2,1,0:T(8,128)(2,1)}, u32[]{:S(2)}, u32[]{:S(2)}) collective-permute-start(bf16[2,384,1536]{2,1,0:T(8,128)(2,1)S(1)} %copy-done), channel_id=1, source_target_pairs={{0,129},{4,133},{8,137},{12,141},{16,145},{20,149},{24,153},{28,15... | collective-permute-start | bytes 7077896 | tf_op jit(solution)/shard_map/ppermute | solution.py:480
  25.1 80.0 %collective-permute-start.3 = (bf16[2,1536,384]{2,1,0:T(8,128)(2,1)}, bf16[2,1536,384]{2,1,0:T(8,128)(2,1)}, u32[]{:S(2)}, u32[]{:S(2)}) collective-permute-start(bf16[2,1536,384]{2,1,0:T(8,128)(2,1)} %down_mine.3), channel_id=1, source_target_pairs={{2,131},{6,135},{10,139},{14,143},{18,147},{22,151},{26,155},{30,1... | collective-permute-start | bytes 7077896 | tf_op jit(solution)/shard_map/ppermute | solution.py:480
  29.2 37.2 %collective-permute-start = (bf16[512,768]{1,0:T(8,128)(2,1)}, bf16[512,768]{1,0:T(8,128)(2,1)}, u32[]{:S(2)}, u32[]{:S(2)}) collective-permute-start(bf16[512,768]{1,0:T(8,128)(2,1)} %constant_dynamic-slice_fusion), channel_id=1, source_target_pairs={{0,1},{1,0},{2,3},{3,2},{4,5},{5,4},{6,7},{7,6},{8,9},{9,8},{10,11... | collective-permute-start | bytes 2359304 | tf_op jit(solution)/shard_map/ppermute | solution.py:481
  30.6 33.5 %collective-permute-start.1 = (f32[2,768]{1,0:T(2,128)}, f32[2,768]{1,0:T(2,128)S(1)}, u32[]{:S(2)}, u32[]{:S(2)}) collective-permute-start(f32[2,768]{1,0:T(2,128)} %get-tuple-element.62), channel_id=1, source_target_pairs={{0,1},{1,0},{2,3},{3,2},{4,5},{5,4},{6,7},{7,6},{8,9},{9,8},{10,11... | collective-permute-start | bytes 18440 | tf_op jit(solution)/shard_map/ppermute | solution.py:483
  33.3 71.7 %collective-permute-start.4 = (bf16[2,384,384]{2,1,0:T(8,128)(2,1)S(1)}, bf16[2,384,384]{2,1,0:T(8,128)(2,1)S(1)}, u32[]{:S(2)}, u32[]{:S(2)}) collective-permute-start(bf16[2,384,384]{2,1,0:T(8,128)(2,1)S(1)} %copy-done.9), channel_id=1, source_target_pairs={{0,129},{4,133},{8,137},{12,141},{16,145},{20,149},{24,153},{28,15... | collective-permute-start | bytes 1769480 | tf_op jit(solution)/shard_map/ppermute | solution.py:480
  35.4 2.9 %copy-start.7 = (s32[2]{0:T(128)}, s32[2]{0:T(128)S(1)}, u32[]{:S(2)}) copy-start(s32[2]{0:T(128)S(1)} %pad_add_fusion.place_ref.side_ref) | copy-start | bytes 28
  35.4 30.2 %copy-start.18 = (f32[1,2,768]{2,1,0:T(2,128)S(1)}, f32[1,2,768]{2,1,0:T(2,128)}, u32[]{:S(2)}) copy-start(f32[1,2,768]{2,1,0:T(2,128)} %get-tuple-element.61) | copy-start | bytes 18436
  64.1 1.5 copy-start.19
  64.1 40.9 %collective-permute-start.5 = (bf16[2,384,384]{2,1,0:T(8,128)(2,1)}, bf16[2,384,384]{2,1,0:T(8,128)(2,1)}, u32[]{:S(2)}, u32[]{:S(2)}) collective-permute-start(bf16[2,384,384]{2,1,0:T(8,128)(2,1)} %out_ref.1), channel_id=1, source_target_pairs={{2,131},{6,135},{10,139},{14,143},{18,147},{22,151},{26,155},{30,1... | collective-permute-start | bytes 1769480 | tf_op jit(solution)/shard_map/ppermute | solution.py:480
  105.9 55.1 %all-to-all-start.1 = ((bf16[256,24,128]{2,1,0:T(8,128)(2,1)}), bf16[256,24,128]{2,1,0:T(8,128)(2,1)}, u32[]{:S(2)}, u32[]{:S(2)}) async-start(bf16[256,24,128]{2,1,0:T(8,128)(2,1)} %bitcast.8), calls=%async_computation.1 | async-start | bytes 3145728 | tf_op jit(solution)/shard_map/all_to_all | solution.py:492
  120.2 40.8 %copy-start.8 = (s32[2]{0:T(128)S(1)}, s32[2]{0:T(128)}, u32[]{:S(2)}) copy-start(s32[2]{0:T(128)} %copy-done.7) | copy-start | bytes 28
  120.2 40.8 %copy-start.10 = (bf16[256,256]{1,0:T(8,128)(2,1)S(1)}, bf16[256,256]{1,0:T(8,128)(2,1)}, u32[]{:S(2)}) copy-start(bf16[256,256]{1,0:T(8,128)(2,1)} %constant.48.clone.split_ref) | copy-start | bytes 393220
  120.3 11.0 %collective-permute-start.8 = (bf16[2,384,1536]{2,1,0:T(8,128)(2,1)}, bf16[2,384,1536]{2,1,0:T(8,128)(2,1)S(1)}, u32[]{:S(2)}, u32[]{:S(2)}) collective-permute-start(bf16[2,384,1536]{2,1,0:T(8,128)(2,1)} %collective-permute-done.2.up_got), channel_id=1, source_target_pairs={{0,2},{4,6},{8,10},{12,14},{16,18},{20,22},{24,26},{28,30},{32,34}... | collective-permute-start | bytes 7077896 | tf_op jit(solution)/shard_map/ppermute | solution.py:493
  122.6 9.5 %collective-permute-start.9 = (bf16[2,1536,384]{2,1,0:T(8,128)(2,1)}, bf16[2,1536,384]{2,1,0:T(8,128)(2,1)S(1)}, u32[]{:S(2)}, u32[]{:S(2)}) collective-permute-start(bf16[2,1536,384]{2,1,0:T(8,128)(2,1)} %collective-permute-done.3.down_got), channel_id=1, source_target_pairs={{2,0},{6,4},{10,8},{14,12},{18,16},{22,20},{26,24},{30,28},{34,32}... | collective-permute-start | bytes 7077896 | tf_op jit(solution)/shard_map/ppermute | solution.py:493
  123.9 5.0 %collective-permute-start.6 = (bf16[2,384,384]{2,1,0:T(8,128)(2,1)}, bf16[2,384,384]{2,1,0:T(8,128)(2,1)S(1)}, u32[]{:S(2)}, u32[]{:S(2)}) collective-permute-start(bf16[2,384,384]{2,1,0:T(8,128)(2,1)} %copy-done.15), channel_id=1, source_target_pairs={{0,2},{4,6},{8,10},{12,14},{16,18},{20,22},{24,26},{28,30},{32,34}... | collective-permute-start | bytes 1769480 | tf_op jit(solution)/shard_map/ppermute | solution.py:493
  127.1 4.1 %collective-permute-start.7 = (bf16[2,384,384]{2,1,0:T(8,128)(2,1)}, bf16[2,384,384]{2,1,0:T(8,128)(2,1)S(1)}, u32[]{:S(2)}, u32[]{:S(2)}) collective-permute-start(bf16[2,384,384]{2,1,0:T(8,128)(2,1)} %collective-permute-done.5.out_got), channel_id=1, source_target_pairs={{2,0},{6,4},{10,8},{14,12},{18,16},{22,20},{26,24},{30,28},{34,32}... | collective-permute-start | bytes 1769480 | tf_op jit(solution)/shard_map/ppermute | solution.py:493
  128.9 3.2 %copy-start.16 = (bf16[2,384,384]{2,1,0:T(8,128)(2,1)}, bf16[2,384,384]{2,1,0:T(8,128)(2,1)S(1)}, u32[]{:S(2)}) copy-start(bf16[2,384,384]{2,1,0:T(8,128)(2,1)S(1)} %collective-permute-done.6.in_passed) | copy-start | bytes 1769476
  132.1 1.5 copy-start.12
  133.6 1.4 copy-start.13
  161.0 6.9 %copy-start.1 = (bf16[2,1536,384]{2,1,0:T(8,128)(2,1)S(1)}, bf16[2,1536,384]{2,1,0:T(8,128)(2,1)}, u32[]{:S(2)}) copy-start(bf16[2,1536,384]{2,1,0:T(8,128)(2,1)} %down_mine.3) | copy-start | bytes 7077892
  161.0 6.9 %copy-start.2 = (bf16[2,384,1536]{2,1,0:T(8,128)(2,1)S(1)}, bf16[2,384,1536]{2,1,0:T(8,128)(2,1)}, u32[]{:S(2)}) copy-start(bf16[2,384,1536]{2,1,0:T(8,128)(2,1)} %get-tuple-element.53.up_theirs) | copy-start | bytes 7077892
  161.0 6.9 %copy-start.3 = (bf16[2,1536,384]{2,1,0:T(8,128)(2,1)S(1)}, bf16[2,1536,384]{2,1,0:T(8,128)(2,1)}, u32[]{:S(2)}) copy-start(bf16[2,1536,384]{2,1,0:T(8,128)(2,1)} %get-tuple-element.54.down_theirs) | copy-start | bytes 7077892
  161.0 6.9 %copy-start.5 = (bf16[1024,768]{1,0:T(8,128)(2,1)S(1)}, bf16[1024,768]{1,0:T(8,128)(2,1)}, u32[]{:S(2)}) copy-start(bf16[1024,768]{1,0:T(8,128)(2,1)} %copy-done.4) | copy-start | bytes 4718596
  161.0 6.9 %copy-start.6 = (bf16[1024,768]{1,0:T(8,128)(2,1)S(1)}, bf16[1024,768]{1,0:T(8,128)(2,1)}, u32[]{:S(2)}) copy-start(bf16[1024,768]{1,0:T(8,128)(2,1)} %get-tuple-element.56.mix_theirs) | copy-start | bytes 4718596
  174.4 13.6 %collective-permute-start.10 = (bf16[256,768]{1,0:T(8,128)(2,1)}, bf16[256,768]{1,0:T(8,128)(2,1)}, u32[]{:S(2)}, u32[]{:S(2)}) collective-permute-start(bf16[256,768]{1,0:T(8,128)(2,1)} %get-tuple-element.58), channel_id=1, source_target_pairs={{0,1},{1,0},{2,3},{3,2},{4,5},{5,4},{6,7},{7,6},{8,9},{9,8},{10,11... | collective-permute-start | bytes 1179656 | tf_op jit(solution)/shard_map/ppermute | solution.py:505
  180.9 13.9 %collective-permute-start.11 = (bf16[256,768]{1,0:T(8,128)(2,1)S(1)}, bf16[256,768]{1,0:T(8,128)(2,1)S(1)}, u32[]{:S(2)}, u32[]{:S(2)}) collective-permute-start(bf16[256,768]{1,0:T(8,128)(2,1)S(1)} %get-tuple-element.60), channel_id=1, source_target_pairs={{0,1},{1,0},{2,3},{3,2},{4,5},{5,4},{6,7},{7,6},{8,9},{9,8},{10,11... | collective-permute-start | bytes 1179656 | tf_op jit(solution)/shard_map/ppermute | solution.py:505
  189.0 5.8 %copy-start.14 = (bf16[1024,768]{1,0:T(8,128)(2,1)}, bf16[1024,768]{1,0:T(8,128)(2,1)S(1)}, u32[]{:S(2)}) copy-start(bf16[1024,768]{1,0:T(8,128)(2,1)S(1)} %constant_dynamic-update-slice_fusion.1) | copy-start | bytes 4718596
  (4 other events, 3.9 us)

commit v3 on v2

--- a/solution.py
+++ b/solution.py
@@ -103,7 +103,7 @@
     cos_long_ref, sin_long_ref, second_ref, third_ref, cos_ref, sin_ref, staged = tables
 
     def fetch(slot):
-        rows = pl.ds(pl.multiple_of(slot * 32, 32), 32)
+        rows = pl.ds(slot * 32, 32)
         return pltpu.make_async_copy(data_hbm.at[:, rows, :], data.at[slot], sems.at[slot])
 
     loads = [pltpu.make_async_copy(sources[i], tables[i], table_sems.at[i]) for i in range(6)]
@@ -113,32 +113,29 @@
     fetch(1).start()
     fetch(2).start()
 
-    def filters(part):
+    def filters(now, part):
         return jnp.concatenate(
             [
-                jnp.concatenate([wide[16 + part * 8 + half * 4 + low] for half in range(2)], axis=1)
+                jnp.concatenate([wide[now, 16 + part * 8 + half * 4 + low] for half in range(2)], axis=1)
                 for low in range(4)
             ],
             axis=0,
         )
 
-    @pl.loop(0, 3)
-    def _(slot):
+    for slot in range(3):
+        now = slot % 2
         fetch(slot).wait()
         for part in range(4):
             at = slice(part * 32, (part + 1) * 32)
-            wide[:, at, :] = jnp.swapaxes(data[slot, at].astype(F32), 0, 1)
-
-        @pl.when(slot == 0)
-        def _():
+            wide[now, :, at, :] = jnp.swapaxes(data[slot, at].astype(F32), 0, 1)
+        if slot == 0:
             for load in loads:
                 load.wait()
-
         channels = range(2)
         blocks = [
             jnp.concatenate(
                 [
-                    jnp.concatenate([wide[e * 8 + half * 4 + low] for half in range(2)], axis=1).astype(BF16)
+                    jnp.concatenate([wide[now, e * 8 + half * 4 + low] for half in range(2)], axis=1).astype(BF16)
                     for low in range(4)
                 ],
                 axis=0,
@@ -159,7 +156,7 @@
             for e in channels
         ]
         spectral = [jnp.dot(turned[e], second_ref[...], preferred_element_type=F32) for e in channels]
-        filter_real, filter_imag = filters(0), filters(1)
+        filter_real, filter_imag = filters(now, 0), filters(now, 1)
         filtered = [
             jnp.concatenate(
                 [
@@ -203,7 +200,7 @@
         out_shape=pltpu.HBM((LANES, 48, LANES), BF16),
         scratch_shapes=[
             pltpu.VMEM((3, LANES, 32, LANES), BF16),
-            pltpu.VMEM((32, LANES, LANES), F32),
+            pltpu.VMEM((2, 32, LANES, LANES), F32),
             pltpu.VMEM((2, 2, QBLK, PBLK), BF16),
             pltpu.VMEM((48, LANES, LANES), F32),
             pltpu.SemaphoreType.DMA((3,)),
@@ -316,6 +313,12 @@
     )
 
 
+def gelu(x):
+    slope = math.sqrt(2.0 / math.pi)
+    half = 0.5 * x
+    return half + half * jnp.tanh(x * (slope + (slope * 0.044715) * (x * x)))
+
+
 def mlp_kernel(
     first_row, side_ref, hidden_ref, shuffled_ref, up_mine, up_theirs, down_mine, down_theirs, mix_mine, mix_theirs,
     keep_ref, send_ref, down_buf, gathered,
@@ -324,18 +327,23 @@
     rows = slice(first_row, first_row + keep_ref.shape[0])
     for group, (up_ref, down_ref) in enumerate(((up_mine, down_mine), (up_theirs, down_theirs))):
         home = side if group == 0 else 1 - side
+        ups, places_at = [], []
         for c in range(2):
             lanes = pl.multiple_of((2 * home + c) * 256, 256)
+            places_at.append(lanes)
             total = 0.0
             for s in range(2):
                 start = pl.multiple_of((side if s == 0 else 1 - side) * 192, 192)
                 mixed = shuffled_ref[s, rows, pl.ds(lanes, 256)][:, :192]
                 total = total + jnp.dot(mixed, up_ref[c, pl.ds(start, 192), :], preferred_element_type=F32)
-            active = jax.nn.gelu(total, approximate=True).astype(BF16)
-            down_buf[...] = jnp.dot(active, down_ref[c], preferred_element_type=F32).astype(BF16)
+            ups.append(total)
+        for c in range(2):
+            active = gelu(ups[c]).astype(BF16)
+            down_buf[group, c] = jnp.dot(active, down_ref[c], preferred_element_type=F32).astype(BF16)
+        for c in range(2):
             for s in range(2):
                 start = pl.multiple_of((side if s == 0 else 1 - side) * LANES, LANES)
-                gathered[s, :, pl.ds(lanes, 256)] = down_buf[:, pl.ds(start, 256)]
+                gathered[s, :, pl.ds(places_at[c], 256)] = down_buf[group, c, :, pl.ds(start, 256)]
     for s, (ref, mix_ref) in enumerate(((keep_ref, mix_mine), (send_ref, mix_theirs))):
         outcome = jnp.dot(gathered[s], mix_ref[...], preferred_element_type=F32)
         ref[...] = (hidden_ref[s, rows, :] + outcome).astype(BF16)
@@ -346,7 +354,7 @@
         functools.partial(mlp_kernel, first_row),
         in_specs=[pl.BlockSpec(memory_space=pltpu.SMEM)] + [pl.BlockSpec(memory_space=pltpu.VMEM)] * 8,
         out_shape=[jax.ShapeDtypeStruct((rows, 768), BF16)] * 2,
-        scratch_shapes=[pltpu.VMEM((rows, 384), BF16), pltpu.VMEM((2, rows, 1024), BF16)],
+        scratch_shapes=[pltpu.VMEM((2, 2, rows, 384), BF16), pltpu.VMEM((2, rows, 1024), BF16)],
         compiler_params=pltpu.CompilerParams(vmem_limit_bytes=SMALL_LIMIT),
         cost_estimate=pl.CostEstimate(
             flops=rows * 14 * 10**6, bytes_accessed=14 * 2**20, transcendentals=rows * 6144
@@ -386,29 +394,23 @@
 
 
 def prepare_theirs_kernel(
-    place_ref, in_got, in_passed, out_got, out_passed, up_got, up_passed, down_got, down_passed,
-    first_ref, last_ref, up_theirs, down_theirs, in_ref, out_ref, up_ref, down_ref, sems,
+    place_ref, up_got, up_passed, down_got, down_passed,
+    first_ref, last_ref, up_theirs, down_theirs, up_ref, down_ref, sems,
 ):
-    picks = [
-        (0, in_got, in_passed, in_ref, sems.at[0]),
-        (1, out_got, out_passed, out_ref, sems.at[1]),
-        (0, up_got, up_passed, up_ref, sems.at[2]),
-        (1, down_got, down_passed, down_ref, sems.at[3]),
-    ]
+    inner = up_ref.shape[1]
+    picks = [(0, up_got, up_passed, up_ref, sems.at[0]), (1, down_got, down_passed, down_ref, sems.at[1])]
     for pick in picks:
         choose(place_ref, *pick, True)
-    choose(place_ref, *picks[0], False)
-    choose(place_ref, *picks[1], False)
-    for b in range(in_ref.shape[0]):
-        rearrange(1 - place_ref[0], b, in_ref[b], out_ref[b], first_ref, last_ref)
-    choose(place_ref, *picks[2], False)
-    choose(place_ref, *picks[3], False)
+    for pick in picks:
+        choose(place_ref, *pick, False)
     stores = [
-        pltpu.make_async_copy(up_ref, up_theirs, sems.at[4]),
-        pltpu.make_async_copy(down_ref, down_theirs, sems.at[5]),
+        pltpu.make_async_copy(up_ref.at[:, :, pl.ds(inner, up_ref.shape[2] - inner)], up_theirs, sems.at[2]),
+        pltpu.make_async_copy(down_ref.at[:, pl.ds(inner, down_ref.shape[1] - inner)], down_theirs, sems.at[3]),
     ]
     for store in stores:
         store.start()
+    for b in range(up_ref.shape[0]):
+        rearrange(1 - place_ref[0], b, up_ref[b, :, :inner], down_ref[b, :inner, :], first_ref, last_ref)
     for store in stores:
         store.wait()
 
@@ -432,21 +434,19 @@
     )(place, mix_in, mix_out)
 
 
-def prepare_theirs(place, pairs):
-    mix_in, mix_out = pairs[0][0], pairs[1][0]
-    arrays = [x for pair in pairs for x in pair]
+def prepare_theirs(place, ups, downs):
+    blocks, inner, wide = ups[0].shape
+    arrays = [*ups, *downs]
     return pl.pallas_call(
         prepare_theirs_kernel,
-        in_specs=[pl.BlockSpec(memory_space=pltpu.SMEM)] + [pl.BlockSpec(memory_space=pltpu.HBM)] * len(arrays),
+        in_specs=[pl.BlockSpec(memory_space=pltpu.SMEM)] + [pl.BlockSpec(memory_space=pltpu.HBM)] * 4,
         out_specs=[pl.BlockSpec(memory_space=pltpu.VMEM)] * 2 + [pl.BlockSpec(memory_space=pltpu.HBM)] * 2,
-        out_shape=prepare_shapes(mix_in.shape[0], mix_in.shape[1])
-        + [pltpu.HBM(pair[0].shape, BF16) for pair in pairs[2:]],
+        out_shape=prepare_shapes(blocks, inner)
+        + [pltpu.HBM((blocks, inner, wide - inner), BF16), pltpu.HBM((blocks, wide - inner, inner), BF16)],
         scratch_shapes=[
-            pltpu.VMEM(mix_in.shape, BF16),
-            pltpu.VMEM(mix_out.shape, BF16),
-            pltpu.VMEM(pairs[2][0].shape, BF16),
-            pltpu.VMEM(pairs[3][0].shape, BF16),
-            pltpu.SemaphoreType.DMA((6,)),
+            pltpu.VMEM(ups[0].shape, BF16),
+            pltpu.VMEM(downs[0].shape, BF16),
+            pltpu.SemaphoreType.DMA((4,)),
         ],
         compiler_params=pltpu.CompilerParams(vmem_limit_bytes=VMEM_LIMIT),
         cost_estimate=pl.CostEstimate(flops=10**6, bytes_accessed=2**16, transcendentals=0),
@@ -476,8 +476,8 @@
         packed = pack(tokens, spectrum)
         data = lax.all_to_all(packed, "seq", split_axis=0, concat_axis=0, tiled=True)
 
-        weights, cores = (w_up, w_down, mix_in, mix_out), (0, 1, 0, 1)
-        got = [lax.ppermute(w, both, near(which)) for w, which in zip(weights, cores)]
+        weights = (jnp.concatenate([mix_in, w_up], axis=2), jnp.concatenate([mix_out, w_down], axis=1))
+        got = [lax.ppermute(w, both, near(which)) for which, w in enumerate(weights)]
         theirs = lax.ppermute(lax.dynamic_slice_in_dim(tokens, (1 - side) * count, count, axis=0), "ch", swap)
         scales_mine = jnp.stack([skip, gain])
         scales = jnp.stack([scales_mine, lax.ppermute(scales_mine, "ch", swap)])
@@ -488,23 +488,24 @@
         )
         conv = convolve(data, tables)
 
-        conv, got = lax.optimization_barrier((conv, got))
+        _, got = lax.optimization_barrier((conv, got))
         conv = lax.all_to_all(conv, both, split_axis=0, concat_axis=0, tiled=True)
-        passed = [lax.ppermute(g, "seq", across(which)) for g, which in zip(got, cores)]
-        pairs = [(got[i], passed[i]) for i in (2, 3, 0, 1)]
-        first_theirs, last_theirs, up_theirs, down_theirs = prepare_theirs(place, pairs)
+        passed = [lax.ppermute(g, "seq", across(which)) for which, g in enumerate(got)]
+        first_theirs, last_theirs, up_theirs, down_theirs = prepare_theirs(
+            place, (got[0], passed[0]), (got[1], passed[1])
+        )
         mix_first = (first_mine, first_theirs)
         mix_last = (last_mine, last_theirs)
         hidden, shuffled = make_hidden(place, conv, tokens, theirs, scales, mix_first)
         out = jnp.zeros(tokens.shape, tokens.dtype)
-        rows = count // chunks
-        for q in range(chunks):
-            keep, send = mlp(
-                place, hidden, shuffled, (w_up, up_theirs), (w_down, down_theirs), mix_last, q * rows, rows
-            )
+        at = 0
+        for rows in chunks:
+            keep, send = mlp(place, hidden, shuffled, (w_up, up_theirs), (w_down, down_theirs), mix_last, at, rows)
+            place, send = lax.optimization_barrier((place, send))
             sent = lax.ppermute(send, "ch", swap)
-            out = lax.dynamic_update_slice_in_dim(out, keep, side * count + q * rows, axis=0)
-            out = lax.dynamic_update_slice_in_dim(out, sent, (1 - side) * count + q * rows, axis=0)
+            out = lax.dynamic_update_slice_in_dim(out, keep, side * count + at, axis=0)
+            out = lax.dynamic_update_slice_in_dim(out, sent, (1 - side) * count + at, axis=0)
+            at += rows
         return out
 
     return per_device
@@ -512,7 +513,7 @@
 
 def solution(mesh):
     return jax.shard_map(
-        make_per_device(2),
+        make_per_device((208, 240, 64)),
         mesh=mesh,
         in_specs=(
             P("seq", "ch"),

time: 196 us -> 190 us (0.969)
  starting transfers between devices: 54.9 us -> 48.2 us
  other arithmetic: 1.38 us -> 6.92 us
  local copies, waits for them, and re-layouts: 11 us -> 5.46 us
    concatenate x0 -> x2, other arithmetic: none -> 5.54 us  [the longest x1 3.71 us: per_device(): jnp.concatenate([mix_out, w_down], axis=1)]
    unnamed x44 -> x32, local copies, waits for them, and re-layouts: 6.91 us -> 2.48 us
    all_to_all x1, waiting for transfers between devices: 24.2 us -> 20.1 us  [per_device(): lax.all_to_all(packed, 'seq', split_axis=0, concat_axis=0, tiled=True)]
    all_to_all x1, waiting for transfers between devices: 18.4 us -> 22.3 us  [per_device(): conv = lax.all_to_all(conv, both, split_axis=0, concat_axis=0, tiled=True)]
    ppermute x4 -> x2, waiting for transfers between devices: 2.63 us -> 6.07 us  [per_device(): lax.ppermute(g, 'seq', across(which))]
    ppermute x4 -> x2, starting transfers between devices: 10.7 us -> 7.48 us  [per_device(): lax.ppermute(w, both, near(which))]
    ppermute x4 -> x2, starting transfers between devices: 8.31 us -> 5.14 us  [per_device(): lax.ppermute(g, 'seq', across(which))]
    ppermute x2 -> x3, waiting for transfers between devices: 9.83 us -> 6.98 us  [per_device(): sent = lax.ppermute(send, 'ch', swap)]
  transfers between devices with their start and end apart: 14 -> 11, of which waited for: 8 -> 7; matrix products, arithmetic and copies ran while one was open for 2% -> 5% of each run, Pallas kernels for 15% -> 16%
where the time goes in v3:
time: 190 us
  waiting for transfers between devices  81.4 us (43%)
  starting transfers between devices  48.2 us (25%)
  Pallas kernels  47.3 us (25%)
  other arithmetic  6.92 us (4%)
  local copies, waits for them, and re-layouts  5.46 us (3%)
    ppermute x1, waiting for transfers between devices, per_device(): scales = jnp.stack([scales_mine, lax.ppermute(scales_mine, 'ch', swap)])  25.9 us
    all_to_all x1, waiting for transfers between devices, per_device(): conv = lax.all_to_all(conv, both, split_axis=0, concat_axis=0, tiled=True)  22.3 us
    all_to_all x1, waiting for transfers between devices, per_device(): lax.all_to_all(packed, 'seq', split_axis=0, concat_axis=0, tiled=True)  20.1 us
    all_to_all x1, starting transfers between devices, per_device(): lax.all_to_all(packed, 'seq', split_axis=0, concat_axis=0, tiled=True)  14.4 us
    pallas_call x3, Pallas kernels, mlp(): pl.pallas_call(functools.partial(mlp_kernel, first_row), in_specs=[pl.Blo...  13.2 us
    all_to_all x1, starting transfers between devices, per_device(): conv = lax.all_to_all(conv, both, split_axis=0, concat_axis=0, tiled=True)  12.8 us
    pallas_call x1, Pallas kernels, convolve(): pl.pallas_call(conv_kernel, in_specs=[pl.BlockSpec(memory_space=pltpu.HBM...  12.3 us
    ppermute x2, starting transfers between devices, per_device(): lax.ppermute(w, both, near(which))  7.48 us
  transfers between devices with their start and end apart: 11, of which 7 were waited for; matrix products, arithmetic and copies ran while one was open for 5% of the time, Pallas kernels for 16%

profile of v3, /device:TPU:8, one launch (start us, length us, event | category | flops | bytes accessed | tf_op | source)
XLA Modules:
  0.0 189.6 jit_solution(17702350449086790221)
XLA Ops:
  0.0 5.5 %pack.1 = bf16[128,96,128]{2,1,0:T(8,128)(2,1)} custom-call(bf16[1024,768]{1,0:T(8,128)(2,1)} %mine_hbm.1, bf16[2,4,256,384]{3,2,1,0:T(8,128)(2,1)} %spectrum_ref.1, bf16[256,256]{1,0:T(8,128)(2,1)} %constant.53.clone.split_ref), custom_call_target="tpu_custom_call" | custom-call | flops 2000000000 | bytes 6291456 | tf_op jit(solution)/shard_map/pack/pallas_call | solution.py:84
  5.5 14.4 %all-to-all-start = ((bf16[128,96,128]{2,1,0:T(8,128)(2,1)}), bf16[128,96,128]{2,1,0:T(8,128)(2,1)}, u32[]{:S(2)}, u32[]{:S(2)}) async-start(bf16[128,96,128]{2,1,0:T(8,128)(2,1)} %pack.1), calls=%async_computation | async-start | bytes 6291456 | tf_op jit(solution)/shard_map/all_to_all | solution.py:477
  19.9 3.7 %pad_maximum_fusion.1 = bf16[2,1920,384]{2,1,0:T(8,128)(2,1)} fusion(bf16[2,1536,384]{2,1,0:T(8,128)(2,1)} %down_mine.5, bf16[2,384,384]{2,1,0:T(8,128)(2,1)S(1)} %copy-done.8), kind=kLoop, calls=%fused_computation.1 | loop fusion | flops 5898240 | bytes 5898240 | tf_op jit(solution)/shard_map/concatenate | solution.py:479
  23.6 2.4 %collective-permute-start.3 = (bf16[2,1920,384]{2,1,0:T(8,128)(2,1)}, bf16[2,1920,384]{2,1,0:T(8,128)(2,1)}, u32[]{:S(2)}, u32[]{:S(2)}) collective-permute-start(bf16[2,1920,384]{2,1,0:T(8,128)(2,1)} %pad_maximum_fusion.1), channel_id=1, source_target_pairs={{2,131},{6,135},{10,139},{14,143},{18,147},{22,151},{26,155},{30,1... | collective-permute-start | bytes 8847368 | tf_op jit(solution)/shard_map/ppermute | solution.py:480
  26.1 1.8 pad_maximum_fusion
  27.9 5.0 %collective-permute-start.2 = (bf16[2,384,1920]{2,1,0:T(8,128)(2,1)}, bf16[2,384,1920]{2,1,0:T(8,128)(2,1)}, u32[]{:S(2)}, u32[]{:S(2)}) collective-permute-start(bf16[2,384,1920]{2,1,0:T(8,128)(2,1)} %pad_maximum_fusion), channel_id=1, source_target_pairs={{0,129},{4,133},{8,137},{12,141},{16,145},{20,149},{24,153},{28,15... | collective-permute-start | bytes 8847368 | tf_op jit(solution)/shard_map/ppermute | solution.py:480
  32.9 2.1 %constant_dynamic-slice_fusion = bf16[512,768]{1,0:T(8,128)(2,1)} fusion(bf16[1024,768]{1,0:T(8,128)(2,1)} %mine_hbm.1, s32[]{:T(128)S(6)} %select_n.27), kind=kLoop, calls=%fused_computation.10 | loop fusion | bytes 1572868 | tf_op jit(solution)/shard_map/dynamic_slice | solution.py:481
  35.0 0.8 collective-permute-start
  36.5 2.7 %collective-permute-start.1 = (f32[2,768]{1,0:T(2,128)}, f32[2,768]{1,0:T(2,128)}, u32[]{:S(2)}, u32[]{:S(2)}) collective-permute-start(f32[2,768]{1,0:T(2,128)} %get-tuple-element.70), channel_id=1, source_target_pairs={{0,1},{1,0},{2,3},{3,2},{4,5},{5,4},{6,7},{7,6},{8,9},{9,8},{10,11... | collective-permute-start | bytes 18440 | tf_op jit(solution)/shard_map/ppermute | solution.py:483
  39.3 2.3 %prepare_mine.1 = (bf16[768,1024]{1,0:T(8,128)(2,1)S(1)}, bf16[1024,768]{1,0:T(8,128)(2,1)S(1)}) custom-call(s32[2]{0:T(128)S(1)} %pad_add_fusion.place_ref.side_ref, bf16[2,384,384]{2,1,0:T(8,128)(2,1)S(1)} %copy-done.7, bf16[2,384,384]{2,1,0:T(8,128)(2,1)S(1)} %copy-done.8), custom_call_target="tpu_custom_call" | custom-call | flops 1000000000 | bytes 1048576 | tf_op jit(solution)/shard_map/prepare_mine/pallas_call | solution.py:426
  41.6 1.1 copy-done.4
  42.7 1.1 copy-done.12
  43.9 25.9 %collective-permute-done.1 = f32[2,768]{1,0:T(2,128)} collective-permute-done((f32[2,768]{1,0:T(2,128)}, f32[2,768]{1,0:T(2,128)}, u32[]{:S(2)}, u32[]{:S(2)}) %collective-permute-start.1) | collective-permute-done | bytes 6176 | tf_op jit(solution)/shard_map/ppermute | solution.py:483
  69.8 0.7 pad_maximum_fusion.2.scales_ref
  70.5 20.1 %all-to-all-done.data_hbm = bf16[128,96,128]{2,1,0:T(8,128)(2,1)} async-done(((bf16[128,96,128]{2,1,0:T(8,128)(2,1)}), bf16[128,96,128]{2,1,0:T(8,128)(2,1)}, u32[]{:S(2)}, u32[]{:S(2)}) %all-to-all-start) | async-done | bytes 3145760 | tf_op jit(solution)/shard_map/all_to_all | solution.py:477
  90.6 12.3 %convolve.1 = bf16[128,48,128]{2,1,0:T(8,128)(2,1)} custom-call(bf16[128,96,128]{2,1,0:T(8,128)(2,1)} %all-to-all-done.data_hbm, bf16[512,512]{1,0:T(8,128)(2,1)} %constant.54.clone.rest_0_, bf16[512,512]{1,0:T(8,128)(2,1)} %constant.55.clone.rest_1_, bf16[512,512]{1,0:T(8,128)(2,1)} %constant.56.clone.rest_2_, bf16[512,512]{1,0:T(8,128)(2,1)} %constant.57.clone.rest_3_, ...), custom_call_target="tpu_custom_call" | custom-call | flops 6400000000 | bytes 8388608 | tf_op jit(solution)/shard_map/convolve/pallas_call | solution.py:196
  102.9 12.8 %all-to-all-start.1 = ((bf16[256,24,128]{2,1,0:T(8,128)(2,1)}), bf16[256,24,128]{2,1,0:T(8,128)(2,1)}, u32[]{:S(2)}, u32[]{:S(2)}) async-start(bf16[256,24,128]{2,1,0:T(8,128)(2,1)} %bitcast.7), calls=%async_computation.1 | async-start | bytes 3145728 | tf_op jit(solution)/shard_map/all_to_all | solution.py:492
  115.7 3.6 %collective-permute-start.4 = (bf16[2,384,1920]{2,1,0:T(8,128)(2,1)}, bf16[2,384,1920]{2,1,0:T(8,128)(2,1)}, u32[]{:S(2)}, u32[]{:S(2)}) collective-permute-start(bf16[2,384,1920]{2,1,0:T(8,128)(2,1)} %collective-permute-done.2.up_got), channel_id=1, source_target_pairs={{0,2},{4,6},{8,10},{12,14},{16,18},{20,22},{24,26},{28,30},{32,34}... | collective-permute-start | bytes 8847368 | tf_op jit(solution)/shard_map/ppermute | solution.py:493
  119.4 1.5 collective-permute-start.5
  120.9 2.2 %collective-permute-done.4.up_passed = bf16[2,384,1920]{2,1,0:T(8,128)(2,1)} collective-permute-done((bf16[2,384,1920]{2,1,0:T(8,128)(2,1)}, bf16[2,384,1920]{2,1,0:T(8,128)(2,1)}, u32[]{:S(2)}, u32[]{:S(2)}) %collective-permute-start.4) | collective-permute-done | bytes 2949152 | tf_op jit(solution)/shard_map/ppermute | solution.py:493
  123.1 3.9 %collective-permute-done.5.down_passed = bf16[2,1920,384]{2,1,0:T(8,128)(2,1)} collective-permute-done((bf16[2,1920,384]{2,1,0:T(8,128)(2,1)}, bf16[2,1920,384]{2,1,0:T(8,128)(2,1)}, u32[]{:S(2)}, u32[]{:S(2)}) %collective-permute-start.5) | collective-permute-done | bytes 2949152 | tf_op jit(solution)/shard_map/ppermute | solution.py:493
  127.0 7.2 %prepare_theirs.1 = (bf16[768,1024]{1,0:T(8,128)(2,1)}, bf16[1024,768]{1,0:T(8,128)(2,1)}, bf16[2,384,1536]{2,1,0:T(8,128)(2,1)}, bf16[2,1536,384]{2,1,0:T(8,128)(2,1)}) custom-call(s32[2]{0:T(128)} %copy-done.9, bf16[2,384,1920]{2,1,0:T(8,128)(2,1)} %collective-permute-done.2.up_got, bf16[2,384,1920]{2,1,0:T(8,128)(2,1)} %collective-permute-done.4.up_passed, ...), custom_call_target="tpu_custom_call" | custom-call | flops 1000000 | bytes 65536 | tf_op jit(solution)/shard_map/prepare_theirs/pallas_call | solution.py:440
  134.2 22.3 %all-to-all-done.1 = bf16[256,24,128]{2,1,0:T(8,128)(2,1)} async-done(((bf16[256,24,128]{2,1,0:T(8,128)(2,1)}), bf16[256,24,128]{2,1,0:T(8,128)(2,1)}, u32[]{:S(2)}, u32[]{:S(2)}) %all-to-all-start.1) | async-done | bytes 1572896 | tf_op jit(solution)/shard_map/all_to_all | solution.py:492
  156.5 6.9 %hidden.1 = (f32[2,512,768]{2,1,0:T(8,128)S(1)}, bf16[2,512,1024]{2,1,0:T(8,128)(2,1)S(1)}) custom-call(s32[2]{0:T(128)S(1)} %copy-done.10, f32[2,2,768]{2,1,0:T(2,128)S(1)} %pad_maximum_fusion.2.scales_ref, bf16[256,256]{1,0:T(8,128)(2,1)S(1)} %copy-done.11, bf16[768,1024]{1,0:T(8,128)(2,1)} %copy-done.12, bf16[768,1024]{1,0:T(8,128)(2,1)} %get-tuple-element.43.mix_theirs, ...), custom_call_target="tpu_custom_call" | custom-call | flops 3000000000 | bytes 12582912 | tf_op jit(solution)/shard_map/hidden/pallas_call | solution.py:287
  163.4 4.8 %mlp.3 = (bf16[208,768]{1,0:T(8,128)(2,1)S(1)}, bf16[208,768]{1,0:T(8,128)(2,1)S(1)}) custom-call(s32[2]{0:T(128)S(1)} %copy-done.10, f32[2,512,768]{2,1,0:T(8,128)S(1)} %get-tuple-element.52.hidden_ref, bf16[2,512,1024]{2,1,0:T(8,128)(2,1)S(1)} %get-tuple-element.53.shuffled_ref, bf16[2,384,1536]{2,1,0:T(8,128)(2,1)S(1)} %copy-done, ...), custom_call_target="tpu_custom_call" | custom-call | flops 2912000000 | bytes 14680064 | tf_op jit(solution)/shard_map/mlp/pallas_call | solution.py:353
  168.2 1.2 collective-permute-start.6
  169.4 5.3 %mlp.4 = (bf16[240,768]{1,0:T(8,128)(2,1)S(1)}, bf16[240,768]{1,0:T(8,128)(2,1)S(1)}) custom-call(s32[2]{0:T(128)S(1)} %copy-done.10, f32[2,512,768]{2,1,0:T(8,128)S(1)} %get-tuple-element.52.hidden_ref, bf16[2,512,1024]{2,1,0:T(8,128)(2,1)S(1)} %get-tuple-element.53.shuffled_ref, bf16[2,384,1536]{2,1,0:T(8,128)(2,1)S(1)} %copy-done, ...), custom_call_target="tpu_custom_call" | custom-call | flops 3360000000 | bytes 14680064 | tf_op jit(solution)/shard_map/mlp/pallas_call | solution.py:353
  174.7 2.8 %collective-permute-start.7 = (bf16[240,768]{1,0:T(8,128)(2,1)S(1)}, bf16[240,768]{1,0:T(8,128)(2,1)S(1)}, u32[]{:S(2)}, u32[]{:S(2)}) collective-permute-start(bf16[240,768]{1,0:T(8,128)(2,1)S(1)} %get-tuple-element.64), channel_id=1, source_target_pairs={{0,1},{1,0},{2,3},{3,2},{4,5},{5,4},{6,7},{7,6},{8,9},{9,8},{10,11... | collective-permute-start | bytes 1105928 | tf_op jit(solution)/shard_map/ppermute | solution.py:505
  177.5 3.0 %mlp.5 = (bf16[64,768]{1,0:T(8,128)(2,1)S(1)}, bf16[64,768]{1,0:T(8,128)(2,1)S(1)}) custom-call(s32[2]{0:T(128)S(1)} %copy-done.10, f32[2,512,768]{2,1,0:T(8,128)S(1)} %get-tuple-element.52.hidden_ref, bf16[2,512,1024]{2,1,0:T(8,128)(2,1)S(1)} %get-tuple-element.53.shuffled_ref, bf16[2,384,1536]{2,1,0:T(8,128)(2,1)S(1)} %copy-done, ...), custom_call_target="tpu_custom_call" | custom-call | flops 896000000 | bytes 14680064 | tf_op jit(solution)/shard_map/mlp/pallas_call | solution.py:353
  180.6 0.9 collective-permute-start.8
  181.7 6.0 %collective-permute-done.7 = bf16[240,768]{1,0:T(8,128)(2,1)S(1)} collective-permute-done((bf16[240,768]{1,0:T(8,128)(2,1)S(1)}, bf16[240,768]{1,0:T(8,128)(2,1)S(1)}, u32[]{:S(2)}, u32[]{:S(2)}) %collective-permute-start.7) | collective-permute-done | bytes 368672 | tf_op jit(solution)/shard_map/ppermute | solution.py:505
  187.8 1.0 collective-permute-done.8
  (45 shorter events, 1.8 us)
Async XLA Ops:
  5.5 14.4 %copy-start.8 = (bf16[2,384,384]{2,1,0:T(8,128)(2,1)S(1)}, bf16[2,384,384]{2,1,0:T(8,128)(2,1)}, u32[]{:S(2)}) copy-start(bf16[2,384,384]{2,1,0:T(8,128)(2,1)} %out_ref.1) | copy-start | bytes 1769476
  5.5 85.1 %all-to-all-start = ((bf16[128,96,128]{2,1,0:T(8,128)(2,1)}), bf16[128,96,128]{2,1,0:T(8,128)(2,1)}, u32[]{:S(2)}, u32[]{:S(2)}) async-start(bf16[128,96,128]{2,1,0:T(8,128)(2,1)} %pack.1), calls=%async_computation | async-start | bytes 6291456 | tf_op jit(solution)/shard_map/all_to_all | solution.py:477
  19.9 6.2 %copy-start = (bf16[2,384,1536]{2,1,0:T(8,128)(2,1)S(1)}, bf16[2,384,1536]{2,1,0:T(8,128)(2,1)}, u32[]{:S(2)}) copy-start(bf16[2,384,1536]{2,1,0:T(8,128)(2,1)} %up_mine.5) | copy-start | bytes 7077892
  19.9 6.2 %copy-start.7 = (bf16[2,384,384]{2,1,0:T(8,128)(2,1)S(1)}, bf16[2,384,384]{2,1,0:T(8,128)(2,1)}, u32[]{:S(2)}) copy-start(bf16[2,384,384]{2,1,0:T(8,128)(2,1)} %in_ref.1) | copy-start | bytes 1769476
  23.6 12.2 %copy-start.14 = (f32[768]{0:T(1024)S(1)}, f32[768]{0:T(1024)}, u32[]{:S(2)}) copy-start(f32[768]{0:T(1024)} %param.18) | copy-start | bytes 9220
  23.6 12.2 %copy-start.15 = (f32[768]{0:T(1024)S(1)}, f32[768]{0:T(1024)}, u32[]{:S(2)}) copy-start(f32[768]{0:T(1024)} %param.19) | copy-start | bytes 9220
  23.6 92.1 %collective-permute-start.3 = (bf16[2,1920,384]{2,1,0:T(8,128)(2,1)}, bf16[2,1920,384]{2,1,0:T(8,128)(2,1)}, u32[]{:S(2)}, u32[]{:S(2)}) collective-permute-start(bf16[2,1920,384]{2,1,0:T(8,128)(2,1)} %pad_maximum_fusion.1), channel_id=1, source_target_pairs={{2,131},{6,135},{10,139},{14,143},{18,147},{22,151},{26,155},{30,1... | collective-permute-start | bytes 8847368 | tf_op jit(solution)/shard_map/ppermute | solution.py:480
  27.9 87.8 %collective-permute-start.2 = (bf16[2,384,1920]{2,1,0:T(8,128)(2,1)}, bf16[2,384,1920]{2,1,0:T(8,128)(2,1)}, u32[]{:S(2)}, u32[]{:S(2)}) collective-permute-start(bf16[2,384,1920]{2,1,0:T(8,128)(2,1)} %pad_maximum_fusion), channel_id=1, source_target_pairs={{0,129},{4,133},{8,137},{12,141},{16,145},{20,149},{24,153},{28,15... | collective-permute-start | bytes 8847368 | tf_op jit(solution)/shard_map/ppermute | solution.py:480
  35.0 35.4 %collective-permute-start = (bf16[512,768]{1,0:T(8,128)(2,1)}, bf16[512,768]{1,0:T(8,128)(2,1)}, u32[]{:S(2)}, u32[]{:S(2)}) collective-permute-start(bf16[512,768]{1,0:T(8,128)(2,1)} %constant_dynamic-slice_fusion), channel_id=1, source_target_pairs={{0,1},{1,0},{2,3},{3,2},{4,5},{5,4},{6,7},{7,6},{8,9},{9,8},{10,11... | collective-permute-start | bytes 2359304 | tf_op jit(solution)/shard_map/ppermute | solution.py:481
  36.5 33.3 %collective-permute-start.1 = (f32[2,768]{1,0:T(2,128)}, f32[2,768]{1,0:T(2,128)}, u32[]{:S(2)}, u32[]{:S(2)}) collective-permute-start(f32[2,768]{1,0:T(2,128)} %get-tuple-element.70), channel_id=1, source_target_pairs={{0,1},{1,0},{2,3},{3,2},{4,5},{5,4},{6,7},{7,6},{8,9},{9,8},{10,11... | collective-permute-start | bytes 18440 | tf_op jit(solution)/shard_map/ppermute | solution.py:483
  39.3 63.6 %copy-start.9 = (s32[2]{0:T(128)}, s32[2]{0:T(128)S(1)}, u32[]{:S(2)}) copy-start(s32[2]{0:T(128)S(1)} %pad_add_fusion.place_ref.side_ref) | copy-start | bytes 28
  41.6 1.1 copy-start.4
  42.7 1.1 copy-start.12
  102.9 53.6 %all-to-all-start.1 = ((bf16[256,24,128]{2,1,0:T(8,128)(2,1)}), bf16[256,24,128]{2,1,0:T(8,128)(2,1)}, u32[]{:S(2)}, u32[]{:S(2)}) async-start(bf16[256,24,128]{2,1,0:T(8,128)(2,1)} %bitcast.7), calls=%async_computation.1 | async-start | bytes 3145728 | tf_op jit(solution)/shard_map/all_to_all | solution.py:492
  115.7 7.4 %collective-permute-start.4 = (bf16[2,384,1920]{2,1,0:T(8,128)(2,1)}, bf16[2,384,1920]{2,1,0:T(8,128)(2,1)}, u32[]{:S(2)}, u32[]{:S(2)}) collective-permute-start(bf16[2,384,1920]{2,1,0:T(8,128)(2,1)} %collective-permute-done.2.up_got), channel_id=1, source_target_pairs={{0,2},{4,6},{8,10},{12,14},{16,18},{20,22},{24,26},{28,30},{32,34}... | collective-permute-start | bytes 8847368 | tf_op jit(solution)/shard_map/ppermute | solution.py:493
  119.4 7.6 %collective-permute-start.5 = (bf16[2,1920,384]{2,1,0:T(8,128)(2,1)}, bf16[2,1920,384]{2,1,0:T(8,128)(2,1)}, u32[]{:S(2)}, u32[]{:S(2)}) collective-permute-start(bf16[2,1920,384]{2,1,0:T(8,128)(2,1)} %collective-permute-done.3.down_got), channel_id=1, source_target_pairs={{2,0},{6,4},{10,8},{14,12},{18,16},{22,20},{26,24},{30,28},{34,32}... | collective-permute-start | bytes 8847368 | tf_op jit(solution)/shard_map/ppermute | solution.py:493
  120.9 35.6 %copy-start.10 = (s32[2]{0:T(128)S(1)}, s32[2]{0:T(128)}, u32[]{:S(2)}) copy-start(s32[2]{0:T(128)} %copy-done.9) | copy-start | bytes 28
  120.9 35.6 %copy-start.11 = (bf16[256,256]{1,0:T(8,128)(2,1)S(1)}, bf16[256,256]{1,0:T(8,128)(2,1)}, u32[]{:S(2)}) copy-start(bf16[256,256]{1,0:T(8,128)(2,1)} %constant.53.clone.split_ref) | copy-start | bytes 393220
  156.5 6.9 %copy-start.1 = (bf16[2,1536,384]{2,1,0:T(8,128)(2,1)S(1)}, bf16[2,1536,384]{2,1,0:T(8,128)(2,1)}, u32[]{:S(2)}) copy-start(bf16[2,1536,384]{2,1,0:T(8,128)(2,1)} %down_mine.5) | copy-start | bytes 7077892
  156.5 6.9 %copy-start.2 = (bf16[2,384,1536]{2,1,0:T(8,128)(2,1)S(1)}, bf16[2,384,1536]{2,1,0:T(8,128)(2,1)}, u32[]{:S(2)}) copy-start(bf16[2,384,1536]{2,1,0:T(8,128)(2,1)} %get-tuple-element.54.up_theirs) | copy-start | bytes 7077892
  156.5 6.9 %copy-start.3 = (bf16[2,1536,384]{2,1,0:T(8,128)(2,1)S(1)}, bf16[2,1536,384]{2,1,0:T(8,128)(2,1)}, u32[]{:S(2)}) copy-start(bf16[2,1536,384]{2,1,0:T(8,128)(2,1)} %get-tuple-element.55.down_theirs) | copy-start | bytes 7077892
  156.5 6.9 %copy-start.5 = (bf16[1024,768]{1,0:T(8,128)(2,1)S(1)}, bf16[1024,768]{1,0:T(8,128)(2,1)}, u32[]{:S(2)}) copy-start(bf16[1024,768]{1,0:T(8,128)(2,1)} %copy-done.4) | copy-start | bytes 4718596
  156.5 6.9 %copy-start.6 = (bf16[1024,768]{1,0:T(8,128)(2,1)S(1)}, bf16[1024,768]{1,0:T(8,128)(2,1)}, u32[]{:S(2)}) copy-start(bf16[1024,768]{1,0:T(8,128)(2,1)} %get-tuple-element.57.mix_theirs) | copy-start | bytes 4718596
  168.2 13.4 %collective-permute-start.6 = (bf16[208,768]{1,0:T(8,128)(2,1)S(1)}, bf16[208,768]{1,0:T(8,128)(2,1)S(1)}, u32[]{:S(2)}, u32[]{:S(2)}) collective-permute-start(bf16[208,768]{1,0:T(8,128)(2,1)S(1)} %get-tuple-element.60), channel_id=1, source_target_pairs={{0,1},{1,0},{2,3},{3,2},{4,5},{5,4},{6,7},{7,6},{8,9},{9,8},{10,11... | collective-permute-start | bytes 958472 | tf_op jit(solution)/shard_map/ppermute | solution.py:505
  174.7 13.0 %collective-permute-start.7 = (bf16[240,768]{1,0:T(8,128)(2,1)S(1)}, bf16[240,768]{1,0:T(8,128)(2,1)S(1)}, u32[]{:S(2)}, u32[]{:S(2)}) collective-permute-start(bf16[240,768]{1,0:T(8,128)(2,1)S(1)} %get-tuple-element.64), channel_id=1, source_target_pairs={{0,1},{1,0},{2,3},{3,2},{4,5},{5,4},{6,7},{7,6},{8,9},{9,8},{10,11... | collective-permute-start | bytes 1105928 | tf_op jit(solution)/shard_map/ppermute | solution.py:505
  180.6 8.2 %collective-permute-start.8 = (bf16[64,768]{1,0:T(8,128)(2,1)S(1)}, bf16[64,768]{1,0:T(8,128)(2,1)S(1)}, u32[]{:S(2)}, u32[]{:S(2)}) collective-permute-start(bf16[64,768]{1,0:T(8,128)(2,1)S(1)} %get-tuple-element.68), channel_id=1, source_target_pairs={{0,1},{1,0},{2,3},{3,2},{4,5},{5,4},{6,7},{7,6},{8,9},{9,8},{10,11... | collective-permute-start | bytes 294920 | tf_op jit(solution)/shard_map/ppermute | solution.py:505
  187.8 1.1 copy-start.13

commit v4 on v3

--- a/solution.py
+++ b/solution.py
@@ -73,7 +73,7 @@
     pick = (row == lax.broadcasted_iota(jnp.int32, (count, LANES), 1)).astype(F32).astype(BF16)
     for part in range(2):
         for low in range(4):
-            turned = nt_dot(pick, spectrum_ref[part, low])
+            turned = spectrum_ref[part, low].astype(F32).T
             for half in range(2):
                 wide[16 + part * 8 + half * 4 + low] = turned[:, half * LANES : (half + 1) * LANES]
     out_ref[...] = jnp.swapaxes(wide[...], 0, 1).astype(BF16)
@@ -102,16 +102,20 @@
     sources, (out_hbm, data, wide, back, outs, sems, table_sems, out_sems), tables = rest[:6], rest[6:14], rest[14:]
     cos_long_ref, sin_long_ref, second_ref, third_ref, cos_ref, sin_ref, staged = tables
 
-    def fetch(slot):
-        rows = pl.ds(slot * 32, 32)
-        return pltpu.make_async_copy(data_hbm.at[:, rows, :], data.at[slot], sems.at[slot])
+    def fetch(slot, part):
+        at = pl.ds(part * 32, 32)
+        return pltpu.make_async_copy(
+            data_hbm.at[at, pl.ds(slot * 32, 32), :], data.at[slot, at], sems.at[slot * 4 + part]
+        )
 
     loads = [pltpu.make_async_copy(sources[i], tables[i], table_sems.at[i]) for i in range(6)]
-    fetch(0).start()
+    for part in range(4):
+        fetch(0, part).start()
     for i in (0, 1, 4, 5, 2, 3):
         loads[i].start()
-    fetch(1).start()
-    fetch(2).start()
+    for slot in (1, 2):
+        for part in range(4):
+            fetch(slot, part).start()
 
     def filters(now, part):
         return jnp.concatenate(
@@ -124,13 +128,13 @@
 
     for slot in range(3):
         now = slot % 2
-        fetch(slot).wait()
         for part in range(4):
             at = slice(part * 32, (part + 1) * 32)
+            fetch(slot, part).wait()
             wide[now, :, at, :] = jnp.swapaxes(data[slot, at].astype(F32), 0, 1)
         if slot == 0:
-            for load in loads:
-                load.wait()
+            loads[0].wait()
+            loads[1].wait()
         channels = range(2)
         blocks = [
             jnp.concatenate(
@@ -142,9 +146,12 @@
             )
             for e in channels
         ]
-        turn_cos, turn_sin = cos_ref[...], sin_ref[...]
         first_real = [jnp.dot(cos_long_ref[...], block, preferred_element_type=F32) for block in blocks]
         first_imag = [jnp.dot(sin_long_ref[...], block, preferred_element_type=F32) for block in blocks]
+        if slot == 0:
+            for i in (4, 5, 2, 3):
+                loads[i].wait()
+        turn_cos, turn_sin = cos_ref[...], sin_ref[...]
         turned = [
             jnp.concatenate(
                 [
@@ -203,7 +210,7 @@
             pltpu.VMEM((2, 32, LANES, LANES), F32),
             pltpu.VMEM((2, 2, QBLK, PBLK), BF16),
             pltpu.VMEM((48, LANES, LANES), F32),
-            pltpu.SemaphoreType.DMA((3,)),
+            pltpu.SemaphoreType.DMA((12,)),
             pltpu.SemaphoreType.DMA((6,)),
             pltpu.SemaphoreType.DMA((4,)),
         ]
@@ -513,7 +520,7 @@
 
 def solution(mesh):
     return jax.shard_map(
-        make_per_device((208, 240, 64)),
+        make_per_device((160, 192, 112, 48)),
         mesh=mesh,
         in_specs=(
             P("seq", "ch"),

time: 190 us -> 192 us (1.011)
  starting transfers between devices: 48.2 us -> 51.1 us
  waiting for transfers between devices: 81.4 us -> 79.2 us
    ppermute x3 -> x4, starting transfers between devices: 4.86 us -> 7.55 us  [per_device(): sent = lax.ppermute(send, 'ch', swap)]
    ppermute x3 -> x4, waiting for transfers between devices: 6.98 us -> 4.74 us  [per_device(): sent = lax.ppermute(send, 'ch', swap)]
    pallas_call x3 -> x4, Pallas kernels: 13.2 us -> 14 us  [mlp(): pl.pallas_call(functools.partial(mlp_kernel, first_row), in_specs=[pl.Blo...]
  transfers between devices with their start and end apart: 11 -> 12, of which waited for: 7 -> 6; matrix products, arithmetic and copies ran while one was open for 5% -> 5% of each run, Pallas kernels for 16% -> 17%
where the time goes in v4:
time: 192 us
  waiting for transfers between devices  79.2 us (41%)
  starting transfers between devices  51.1 us (27%)
  Pallas kernels  47.9 us (25%)
  local copies, waits for them, and re-layouts  6.57 us (3%)
  other arithmetic  6.37 us (3%)
    ppermute x1, waiting for transfers between devices, per_device(): scales = jnp.stack([scales_mine, lax.ppermute(scales_mine, 'ch', swap)])  26.1 us
    all_to_all x1, waiting for transfers between devices, per_device(): conv = lax.all_to_all(conv, both, split_axis=0, concat_axis=0, tiled=True)  22.3 us
    all_to_all x1, waiting for transfers between devices, per_device(): lax.all_to_all(packed, 'seq', split_axis=0, concat_axis=0, tiled=True)  20.1 us
    all_to_all x1, starting transfers between devices, per_device(): lax.all_to_all(packed, 'seq', split_axis=0, concat_axis=0, tiled=True)  14.4 us
    pallas_call x4, Pallas kernels, mlp(): pl.pallas_call(functools.partial(mlp_kernel, first_row), in_specs=[pl.Blo...  14 us
    all_to_all x1, starting transfers between devices, per_device(): conv = lax.all_to_all(conv, both, split_axis=0, concat_axis=0, tiled=True)  12.8 us
    pallas_call x1, Pallas kernels, convolve(): pl.pallas_call(conv_kernel, in_specs=[pl.BlockSpec(memory_space=pltpu.HBM...  12.2 us
    ppermute x4, starting transfers between devices, per_device(): sent = lax.ppermute(send, 'ch', swap)  7.55 us
  transfers between devices with their start and end apart: 12, of which 6 were waited for; matrix products, arithmetic and copies ran while one was open for 5% of the time, Pallas kernels for 17%

profile of v4, /device:TPU:8, one launch (start us, length us, event | category | flops | bytes accessed | tf_op | source)
XLA Modules:
  0.0 191.6 jit_solution(16249683827402573995)
XLA Ops:
  0.0 5.4 %pack.1 = bf16[128,96,128]{2,1,0:T(8,128)(2,1)} custom-call(bf16[1024,768]{1,0:T(8,128)(2,1)} %mine_hbm.1, bf16[2,4,256,384]{3,2,1,0:T(8,128)(2,1)} %spectrum_ref.1, bf16[256,256]{1,0:T(8,128)(2,1)} %constant.58.clone.split_ref), custom_call_target="tpu_custom_call" | custom-call | flops 2000000000 | bytes 6291456 | tf_op jit(solution)/shard_map/pack/pallas_call | solution.py:84
  5.4 14.4 %all-to-all-start = ((bf16[128,96,128]{2,1,0:T(8,128)(2,1)}), bf16[128,96,128]{2,1,0:T(8,128)(2,1)}, u32[]{:S(2)}, u32[]{:S(2)}) async-start(bf16[128,96,128]{2,1,0:T(8,128)(2,1)} %pack.1), calls=%async_computation | async-start | bytes 6291456 | tf_op jit(solution)/shard_map/all_to_all | solution.py:484
  19.8 3.8 %pad_maximum_fusion.1 = bf16[2,1920,384]{2,1,0:T(8,128)(2,1)} fusion(bf16[2,1536,384]{2,1,0:T(8,128)(2,1)} %down_mine.7, bf16[2,384,384]{2,1,0:T(8,128)(2,1)S(1)} %copy-done.8), kind=kLoop, calls=%fused_computation.1 | loop fusion | flops 5898240 | bytes 5898240 | tf_op jit(solution)/shard_map/concatenate | solution.py:486
  23.6 2.3 %collective-permute-start.3 = (bf16[2,1920,384]{2,1,0:T(8,128)(2,1)}, bf16[2,1920,384]{2,1,0:T(8,128)(2,1)}, u32[]{:S(2)}, u32[]{:S(2)}) collective-permute-start(bf16[2,1920,384]{2,1,0:T(8,128)(2,1)} %pad_maximum_fusion.1), channel_id=1, source_target_pairs={{2,131},{6,135},{10,139},{14,143},{18,147},{22,151},{26,155},{30,1... | collective-permute-start | bytes 8847368 | tf_op jit(solution)/shard_map/ppermute | solution.py:487
  25.9 1.8 pad_maximum_fusion
  27.7 5.2 %collective-permute-start.2 = (bf16[2,384,1920]{2,1,0:T(8,128)(2,1)}, bf16[2,384,1920]{2,1,0:T(8,128)(2,1)}, u32[]{:S(2)}, u32[]{:S(2)}) collective-permute-start(bf16[2,384,1920]{2,1,0:T(8,128)(2,1)} %pad_maximum_fusion), channel_id=1, source_target_pairs={{0,129},{4,133},{8,137},{12,141},{16,145},{20,149},{24,153},{28,15... | collective-permute-start | bytes 8847368 | tf_op jit(solution)/shard_map/ppermute | solution.py:487
  32.9 2.2 %constant_dynamic-slice_fusion = bf16[512,768]{1,0:T(8,128)(2,1)} fusion(bf16[1024,768]{1,0:T(8,128)(2,1)} %mine_hbm.1, s32[]{:T(128)S(6)} %select_n.33), kind=kLoop, calls=%fused_computation.12 | loop fusion | bytes 1572868 | tf_op jit(solution)/shard_map/dynamic_slice | solution.py:488
  35.9 3.0 %collective-permute-start.1 = (f32[2,768]{1,0:T(2,128)S(1)}, f32[2,768]{1,0:T(2,128)}, u32[]{:S(2)}, u32[]{:S(2)}) collective-permute-start(f32[2,768]{1,0:T(2,128)S(1)} %get-tuple-element.78), channel_id=1, source_target_pairs={{0,1},{1,0},{2,3},{3,2},{4,5},{5,4},{6,7},{7,6},{8,9},{9,8},{10,11... | collective-permute-start | bytes 18440 | tf_op jit(solution)/shard_map/ppermute | solution.py:490
  39.0 2.3 %prepare_mine.1 = (bf16[768,1024]{1,0:T(8,128)(2,1)S(1)}, bf16[1024,768]{1,0:T(8,128)(2,1)S(1)}) custom-call(s32[2]{0:T(128)S(1)} %pad_add_fusion.place_ref.side_ref, bf16[2,384,384]{2,1,0:T(8,128)(2,1)S(1)} %copy-done.7, bf16[2,384,384]{2,1,0:T(8,128)(2,1)S(1)} %copy-done.8), custom_call_target="tpu_custom_call" | custom-call | flops 1000000000 | bytes 1048576 | tf_op jit(solution)/shard_map/prepare_mine/pallas_call | solution.py:433
  41.3 1.2 copy-done.4
  42.5 1.1 copy-done.12
  43.6 26.1 %collective-permute-done.1 = f32[2,768]{1,0:T(2,128)} collective-permute-done((f32[2,768]{1,0:T(2,128)S(1)}, f32[2,768]{1,0:T(2,128)}, u32[]{:S(2)}, u32[]{:S(2)}) %collective-permute-start.1) | collective-permute-done | bytes 6176 | tf_op jit(solution)/shard_map/ppermute | solution.py:490
  70.4 20.1 %all-to-all-done.data_hbm = bf16[128,96,128]{2,1,0:T(8,128)(2,1)} async-done(((bf16[128,96,128]{2,1,0:T(8,128)(2,1)}), bf16[128,96,128]{2,1,0:T(8,128)(2,1)}, u32[]{:S(2)}, u32[]{:S(2)}) %all-to-all-start) | async-done | bytes 3145760 | tf_op jit(solution)/shard_map/all_to_all | solution.py:484
  90.5 12.2 %convolve.1 = bf16[128,48,128]{2,1,0:T(8,128)(2,1)} custom-call(bf16[128,96,128]{2,1,0:T(8,128)(2,1)} %all-to-all-done.data_hbm, bf16[512,512]{1,0:T(8,128)(2,1)} %constant.59.clone.rest_0_, bf16[512,512]{1,0:T(8,128)(2,1)} %constant.60.clone.rest_1_, bf16[512,512]{1,0:T(8,128)(2,1)} %constant.61.clone.rest_2_, bf16[512,512]{1,0:T(8,128)(2,1)} %constant.62.clone.rest_3_, ...), custom_call_target="tpu_custom_call" | custom-call | flops 6400000000 | bytes 8388608 | tf_op jit(solution)/shard_map/convolve/pallas_call | solution.py:203
  102.6 12.8 %all-to-all-start.1 = ((bf16[256,24,128]{2,1,0:T(8,128)(2,1)}), bf16[256,24,128]{2,1,0:T(8,128)(2,1)}, u32[]{:S(2)}, u32[]{:S(2)}) async-start(bf16[256,24,128]{2,1,0:T(8,128)(2,1)} %bitcast.7), calls=%async_computation.1 | async-start | bytes 3145728 | tf_op jit(solution)/shard_map/all_to_all | solution.py:499
  115.5 3.7 %collective-permute-start.4 = (bf16[2,384,1920]{2,1,0:T(8,128)(2,1)}, bf16[2,384,1920]{2,1,0:T(8,128)(2,1)}, u32[]{:S(2)}, u32[]{:S(2)}) collective-permute-start(bf16[2,384,1920]{2,1,0:T(8,128)(2,1)} %collective-permute-done.2.up_got), channel_id=1, source_target_pairs={{0,2},{4,6},{8,10},{12,14},{16,18},{20,22},{24,26},{28,30},{32,34}... | collective-permute-start | bytes 8847368 | tf_op jit(solution)/shard_map/ppermute | solution.py:500
  119.2 1.5 collective-permute-start.5
  120.7 2.2 %collective-permute-done.4.up_passed = bf16[2,384,1920]{2,1,0:T(8,128)(2,1)} collective-permute-done((bf16[2,384,1920]{2,1,0:T(8,128)(2,1)}, bf16[2,384,1920]{2,1,0:T(8,128)(2,1)}, u32[]{:S(2)}, u32[]{:S(2)}) %collective-permute-start.4) | collective-permute-done | bytes 2949152 | tf_op jit(solution)/shard_map/ppermute | solution.py:500
  122.9 3.9 %collective-permute-done.5.down_passed = bf16[2,1920,384]{2,1,0:T(8,128)(2,1)} collective-permute-done((bf16[2,1920,384]{2,1,0:T(8,128)(2,1)}, bf16[2,1920,384]{2,1,0:T(8,128)(2,1)}, u32[]{:S(2)}, u32[]{:S(2)}) %collective-permute-start.5) | collective-permute-done | bytes 2949152 | tf_op jit(solution)/shard_map/ppermute | solution.py:500
  126.8 7.2 %prepare_theirs.1 = (bf16[768,1024]{1,0:T(8,128)(2,1)}, bf16[1024,768]{1,0:T(8,128)(2,1)}, bf16[2,384,1536]{2,1,0:T(8,128)(2,1)}, bf16[2,1536,384]{2,1,0:T(8,128)(2,1)}) custom-call(s32[2]{0:T(128)} %copy-done.9, bf16[2,384,1920]{2,1,0:T(8,128)(2,1)} %collective-permute-done.2.up_got, bf16[2,384,1920]{2,1,0:T(8,128)(2,1)} %collective-permute-done.4.up_passed, ...), custom_call_target="tpu_custom_call" | custom-call | flops 1000000 | bytes 65536 | tf_op jit(solution)/shard_map/prepare_theirs/pallas_call | solution.py:447
  134.0 22.3 %all-to-all-done.1 = bf16[256,24,128]{2,1,0:T(8,128)(2,1)} async-done(((bf16[256,24,128]{2,1,0:T(8,128)(2,1)}), bf16[256,24,128]{2,1,0:T(8,128)(2,1)}, u32[]{:S(2)}, u32[]{:S(2)}) %all-to-all-start.1) | async-done | bytes 1572896 | tf_op jit(solution)/shard_map/all_to_all | solution.py:499
  156.3 6.8 %hidden.1 = (f32[2,512,768]{2,1,0:T(8,128)S(1)}, bf16[2,512,1024]{2,1,0:T(8,128)(2,1)S(1)}) custom-call(s32[2]{0:T(128)S(1)} %copy-done.10, f32[2,2,768]{2,1,0:T(2,128)S(1)} %pad_maximum_fusion.2.scales_ref, bf16[256,256]{1,0:T(8,128)(2,1)S(1)} %copy-done.11, bf16[768,1024]{1,0:T(8,128)(2,1)} %copy-done.12, bf16[768,1024]{1,0:T(8,128)(2,1)} %get-tuple-element.47.mix_theirs, ...), custom_call_target="tpu_custom_call" | custom-call | flops 3000000000 | bytes 12582912 | tf_op jit(solution)/shard_map/hidden/pallas_call | solution.py:294
  163.2 3.7 %mlp.4 = (bf16[160,768]{1,0:T(8,128)(2,1)S(1)}, bf16[160,768]{1,0:T(8,128)(2,1)S(1)}) custom-call(s32[2]{0:T(128)S(1)} %copy-done.10, f32[2,512,768]{2,1,0:T(8,128)S(1)} %get-tuple-element.56.hidden_ref, bf16[2,512,1024]{2,1,0:T(8,128)(2,1)S(1)} %get-tuple-element.57.shuffled_ref, bf16[2,384,1536]{2,1,0:T(8,128)(2,1)S(1)} %copy-done, ...), custom_call_target="tpu_custom_call" | custom-call | flops 2240000000 | bytes 14680064 | tf_op jit(solution)/shard_map/mlp/pallas_call | solution.py:360
  166.9 1.2 collective-permute-start.6
  168.1 4.4 %mlp.5 = (bf16[192,768]{1,0:T(8,128)(2,1)S(1)}, bf16[192,768]{1,0:T(8,128)(2,1)S(1)}) custom-call(s32[2]{0:T(128)S(1)} %copy-done.10, f32[2,512,768]{2,1,0:T(8,128)S(1)} %get-tuple-element.56.hidden_ref, bf16[2,512,1024]{2,1,0:T(8,128)(2,1)S(1)} %get-tuple-element.57.shuffled_ref, bf16[2,384,1536]{2,1,0:T(8,128)(2,1)S(1)} %copy-done, ...), custom_call_target="tpu_custom_call" | custom-call | flops 2688000000 | bytes 14680064 | tf_op jit(solution)/shard_map/mlp/pallas_call | solution.py:360
  172.4 2.8 %collective-permute-start.7 = (bf16[192,768]{1,0:T(8,128)(2,1)S(1)}, bf16[192,768]{1,0:T(8,128)(2,1)S(1)}, u32[]{:S(2)}, u32[]{:S(2)}) collective-permute-start(bf16[192,768]{1,0:T(8,128)(2,1)S(1)} %get-tuple-element.68), channel_id=1, source_target_pairs={{0,1},{1,0},{2,3},{3,2},{4,5},{5,4},{6,7},{7,6},{8,9},{9,8},{10,11... | collective-permute-start | bytes 884744 | tf_op jit(solution)/shard_map/ppermute | solution.py:512
  175.2 3.0 %mlp.6 = (bf16[112,768]{1,0:T(8,128)(2,1)S(1)}, bf16[112,768]{1,0:T(8,128)(2,1)S(1)}) custom-call(s32[2]{0:T(128)S(1)} %copy-done.10, f32[2,512,768]{2,1,0:T(8,128)S(1)} %get-tuple-element.56.hidden_ref, bf16[2,512,1024]{2,1,0:T(8,128)(2,1)S(1)} %get-tuple-element.57.shuffled_ref, bf16[2,384,1536]{2,1,0:T(8,128)(2,1)S(1)} %copy-done, ...), custom_call_target="tpu_custom_call" | custom-call | flops 1568000000 | bytes 14680064 | tf_op jit(solution)/shard_map/mlp/pallas_call | solution.py:360
  178.3 2.8 %mlp.7 = (bf16[48,768]{1,0:T(8,128)(2,1)S(1)}, bf16[48,768]{1,0:T(8,128)(2,1)S(1)}) custom-call(s32[2]{0:T(128)S(1)} %copy-done.10, f32[2,512,768]{2,1,0:T(8,128)S(1)} %get-tuple-element.56.hidden_ref, bf16[2,512,1024]{2,1,0:T(8,128)(2,1)S(1)} %get-tuple-element.57.shuffled_ref, bf16[2,384,1536]{2,1,0:T(8,128)(2,1)S(1)} %copy-done, ...), custom_call_target="tpu_custom_call" | custom-call | flops 672000000 | bytes 14680064 | tf_op jit(solution)/shard_map/mlp/pallas_call | solution.py:360
  181.1 0.9 collective-permute-start.9
  182.0 2.7 %collective-permute-start.8 = (bf16[112,768]{1,0:T(8,128)(2,1)S(1)}, bf16[112,768]{1,0:T(8,128)(2,1)S(1)}, u32[]{:S(2)}, u32[]{:S(2)}) collective-permute-start(bf16[112,768]{1,0:T(8,128)(2,1)S(1)} %get-tuple-element.72), channel_id=1, source_target_pairs={{0,1},{1,0},{2,3},{3,2},{4,5},{5,4},{6,7},{7,6},{8,9},{9,8},{10,11... | collective-permute-start | bytes 516104 | tf_op jit(solution)/shard_map/ppermute | solution.py:512
  185.0 4.7 %collective-permute-done.8 = bf16[112,768]{1,0:T(8,128)(2,1)S(1)} collective-permute-done((bf16[112,768]{1,0:T(8,128)(2,1)S(1)}, bf16[112,768]{1,0:T(8,128)(2,1)S(1)}, u32[]{:S(2)}, u32[]{:S(2)}) %collective-permute-start.8) | collective-permute-done | bytes 172064 | tf_op jit(solution)/shard_map/ppermute | solution.py:512
  189.8 1.1 copy-done.13
  (50 shorter events, 2.6 us)
Async XLA Ops:
  5.4 14.4 %copy-start.8 = (bf16[2,384,384]{2,1,0:T(8,128)(2,1)S(1)}, bf16[2,384,384]{2,1,0:T(8,128)(2,1)}, u32[]{:S(2)}) copy-start(bf16[2,384,384]{2,1,0:T(8,128)(2,1)} %out_ref.1) | copy-start | bytes 1769476
  5.4 85.1 %all-to-all-start = ((bf16[128,96,128]{2,1,0:T(8,128)(2,1)}), bf16[128,96,128]{2,1,0:T(8,128)(2,1)}, u32[]{:S(2)}, u32[]{:S(2)}) async-start(bf16[128,96,128]{2,1,0:T(8,128)(2,1)} %pack.1), calls=%async_computation | async-start | bytes 6291456 | tf_op jit(solution)/shard_map/all_to_all | solution.py:484
  19.8 6.1 %copy-start = (bf16[2,384,1536]{2,1,0:T(8,128)(2,1)S(1)}, bf16[2,384,1536]{2,1,0:T(8,128)(2,1)}, u32[]{:S(2)}) copy-start(bf16[2,384,1536]{2,1,0:T(8,128)(2,1)} %up_mine.7) | copy-start | bytes 7077892
  19.8 6.1 %copy-start.7 = (bf16[2,384,384]{2,1,0:T(8,128)(2,1)S(1)}, bf16[2,384,384]{2,1,0:T(8,128)(2,1)}, u32[]{:S(2)}) copy-start(bf16[2,384,384]{2,1,0:T(8,128)(2,1)} %in_ref.1) | copy-start | bytes 1769476
  23.6 91.9 %collective-permute-start.3 = (bf16[2,1920,384]{2,1,0:T(8,128)(2,1)}, bf16[2,1920,384]{2,1,0:T(8,128)(2,1)}, u32[]{:S(2)}, u32[]{:S(2)}) collective-permute-start(bf16[2,1920,384]{2,1,0:T(8,128)(2,1)} %pad_maximum_fusion.1), channel_id=1, source_target_pairs={{2,131},{6,135},{10,139},{14,143},{18,147},{22,151},{26,155},{30,1... | collective-permute-start | bytes 8847368 | tf_op jit(solution)/shard_map/ppermute | solution.py:487
  27.7 8.2 %copy-start.14 = (f32[768]{0:T(1024)S(1)}, f32[768]{0:T(1024)}, u32[]{:S(2)}) copy-start(f32[768]{0:T(1024)} %param.18) | copy-start | bytes 9220
  27.7 8.2 %copy-start.15 = (f32[768]{0:T(1024)S(1)}, f32[768]{0:T(1024)}, u32[]{:S(2)}) copy-start(f32[768]{0:T(1024)} %param.19) | copy-start | bytes 9220
  27.7 87.8 %collective-permute-start.2 = (bf16[2,384,1920]{2,1,0:T(8,128)(2,1)}, bf16[2,384,1920]{2,1,0:T(8,128)(2,1)}, u32[]{:S(2)}, u32[]{:S(2)}) collective-permute-start(bf16[2,384,1920]{2,1,0:T(8,128)(2,1)} %pad_maximum_fusion), channel_id=1, source_target_pairs={{0,129},{4,133},{8,137},{12,141},{16,145},{20,149},{24,153},{28,15... | collective-permute-start | bytes 8847368 | tf_op jit(solution)/shard_map/ppermute | solution.py:487
  35.0 35.4 %collective-permute-start = (bf16[512,768]{1,0:T(8,128)(2,1)}, bf16[512,768]{1,0:T(8,128)(2,1)}, u32[]{:S(2)}, u32[]{:S(2)}) collective-permute-start(bf16[512,768]{1,0:T(8,128)(2,1)} %constant_dynamic-slice_fusion), channel_id=1, source_target_pairs={{0,1},{1,0},{2,3},{3,2},{4,5},{5,4},{6,7},{7,6},{8,9},{9,8},{10,11... | collective-permute-start | bytes 2359304 | tf_op jit(solution)/shard_map/ppermute | solution.py:488
  35.9 33.8 %collective-permute-start.1 = (f32[2,768]{1,0:T(2,128)S(1)}, f32[2,768]{1,0:T(2,128)}, u32[]{:S(2)}, u32[]{:S(2)}) collective-permute-start(f32[2,768]{1,0:T(2,128)S(1)} %get-tuple-element.78), channel_id=1, source_target_pairs={{0,1},{1,0},{2,3},{3,2},{4,5},{5,4},{6,7},{7,6},{8,9},{9,8},{10,11... | collective-permute-start | bytes 18440 | tf_op jit(solution)/shard_map/ppermute | solution.py:490
  39.0 2.3 %copy-start.9 = (s32[2]{0:T(128)}, s32[2]{0:T(128)S(1)}, u32[]{:S(2)}) copy-start(s32[2]{0:T(128)S(1)} %pad_add_fusion.place_ref.side_ref) | copy-start | bytes 28
  41.3 1.2 copy-start.4
  42.5 1.1 copy-start.12
  102.6 53.6 %all-to-all-start.1 = ((bf16[256,24,128]{2,1,0:T(8,128)(2,1)}), bf16[256,24,128]{2,1,0:T(8,128)(2,1)}, u32[]{:S(2)}, u32[]{:S(2)}) async-start(bf16[256,24,128]{2,1,0:T(8,128)(2,1)} %bitcast.7), calls=%async_computation.1 | async-start | bytes 3145728 | tf_op jit(solution)/shard_map/all_to_all | solution.py:499
  115.5 7.4 %collective-permute-start.4 = (bf16[2,384,1920]{2,1,0:T(8,128)(2,1)}, bf16[2,384,1920]{2,1,0:T(8,128)(2,1)}, u32[]{:S(2)}, u32[]{:S(2)}) collective-permute-start(bf16[2,384,1920]{2,1,0:T(8,128)(2,1)} %collective-permute-done.2.up_got), channel_id=1, source_target_pairs={{0,2},{4,6},{8,10},{12,14},{16,18},{20,22},{24,26},{28,30},{32,34}... | collective-permute-start | bytes 8847368 | tf_op jit(solution)/shard_map/ppermute | solution.py:500
  119.2 7.6 %collective-permute-start.5 = (bf16[2,1920,384]{2,1,0:T(8,128)(2,1)}, bf16[2,1920,384]{2,1,0:T(8,128)(2,1)}, u32[]{:S(2)}, u32[]{:S(2)}) collective-permute-start(bf16[2,1920,384]{2,1,0:T(8,128)(2,1)} %collective-permute-done.3.down_got), channel_id=1, source_target_pairs={{2,0},{6,4},{10,8},{14,12},{18,16},{22,20},{26,24},{30,28},{34,32}... | collective-permute-start | bytes 8847368 | tf_op jit(solution)/shard_map/ppermute | solution.py:500
  120.7 35.6 %copy-start.10 = (s32[2]{0:T(128)S(1)}, s32[2]{0:T(128)}, u32[]{:S(2)}) copy-start(s32[2]{0:T(128)} %copy-done.9) | copy-start | bytes 28
  120.7 35.5 %copy-start.11 = (bf16[256,256]{1,0:T(8,128)(2,1)S(1)}, bf16[256,256]{1,0:T(8,128)(2,1)}, u32[]{:S(2)}) copy-start(bf16[256,256]{1,0:T(8,128)(2,1)} %constant.58.clone.split_ref) | copy-start | bytes 393220
  156.2 6.9 %copy-start.1 = (bf16[2,1536,384]{2,1,0:T(8,128)(2,1)S(1)}, bf16[2,1536,384]{2,1,0:T(8,128)(2,1)}, u32[]{:S(2)}) copy-start(bf16[2,1536,384]{2,1,0:T(8,128)(2,1)} %down_mine.7) | copy-start | bytes 7077892
  156.2 6.9 %copy-start.2 = (bf16[2,384,1536]{2,1,0:T(8,128)(2,1)S(1)}, bf16[2,384,1536]{2,1,0:T(8,128)(2,1)}, u32[]{:S(2)}) copy-start(bf16[2,384,1536]{2,1,0:T(8,128)(2,1)} %get-tuple-element.58.up_theirs) | copy-start | bytes 7077892
  156.2 6.9 %copy-start.3 = (bf16[2,1536,384]{2,1,0:T(8,128)(2,1)S(1)}, bf16[2,1536,384]{2,1,0:T(8,128)(2,1)}, u32[]{:S(2)}) copy-start(bf16[2,1536,384]{2,1,0:T(8,128)(2,1)} %get-tuple-element.59.down_theirs) | copy-start | bytes 7077892
  156.2 6.9 %copy-start.5 = (bf16[1024,768]{1,0:T(8,128)(2,1)S(1)}, bf16[1024,768]{1,0:T(8,128)(2,1)}, u32[]{:S(2)}) copy-start(bf16[1024,768]{1,0:T(8,128)(2,1)} %copy-done.4) | copy-start | bytes 4718596
  156.3 6.9 %copy-start.6 = (bf16[1024,768]{1,0:T(8,128)(2,1)S(1)}, bf16[1024,768]{1,0:T(8,128)(2,1)}, u32[]{:S(2)}) copy-start(bf16[1024,768]{1,0:T(8,128)(2,1)} %get-tuple-element.61.mix_theirs) | copy-start | bytes 4718596
  166.9 17.9 %collective-permute-start.6 = (bf16[160,768]{1,0:T(8,128)(2,1)S(1)}, bf16[160,768]{1,0:T(8,128)(2,1)S(1)}, u32[]{:S(2)}, u32[]{:S(2)}) collective-permute-start(bf16[160,768]{1,0:T(8,128)(2,1)S(1)} %get-tuple-element.64), channel_id=1, source_target_pairs={{0,1},{1,0},{2,3},{3,2},{4,5},{5,4},{6,7},{7,6},{8,9},{9,8},{10,11... | collective-permute-start | bytes 737288 | tf_op jit(solution)/shard_map/ppermute | solution.py:512
  172.4 12.5 %collective-permute-start.7 = (bf16[192,768]{1,0:T(8,128)(2,1)S(1)}, bf16[192,768]{1,0:T(8,128)(2,1)S(1)}, u32[]{:S(2)}, u32[]{:S(2)}) collective-permute-start(bf16[192,768]{1,0:T(8,128)(2,1)S(1)} %get-tuple-element.68), channel_id=1, source_target_pairs={{0,1},{1,0},{2,3},{3,2},{4,5},{5,4},{6,7},{7,6},{8,9},{9,8},{10,11... | collective-permute-start | bytes 884744 | tf_op jit(solution)/shard_map/ppermute | solution.py:512
  181.1 8.7 %collective-permute-start.9 = (bf16[48,768]{1,0:T(8,128)(2,1)S(1)}, bf16[48,768]{1,0:T(8,128)(2,1)S(1)}, u32[]{:S(2)}, u32[]{:S(2)}) collective-permute-start(bf16[48,768]{1,0:T(8,128)(2,1)S(1)} %get-tuple-element.76), channel_id=1, source_target_pairs={{0,1},{1,0},{2,3},{3,2},{4,5},{5,4},{6,7},{7,6},{8,9},{9,8},{10,11... | collective-permute-start | bytes 221192 | tf_op jit(solution)/shard_map/ppermute | solution.py:512
  182.0 7.7 %collective-permute-start.8 = (bf16[112,768]{1,0:T(8,128)(2,1)S(1)}, bf16[112,768]{1,0:T(8,128)(2,1)S(1)}, u32[]{:S(2)}, u32[]{:S(2)}) collective-permute-start(bf16[112,768]{1,0:T(8,128)(2,1)S(1)} %get-tuple-element.72), channel_id=1, source_target_pairs={{0,1},{1,0},{2,3},{3,2},{4,5},{5,4},{6,7},{7,6},{8,9},{9,8},{10,11... | collective-permute-start | bytes 516104 | tf_op jit(solution)/shard_map/ppermute | solution.py:512
  189.8 1.1 copy-start.13
